TPU v7x, 256 devices: a whole 4x4x8 slice. The times are simulated.
256 devices in a mesh: dp: 32 (over x_hi, z, core), node: 8 (over x_lo, y).
Axes of the slice: x: 4 (x_hi: 2, x_lo: 2; x = x_hi * 2 + x_lo), y: 4, z: 8, core: 2. Of those that a mesh axis runs over, the one named last changes fastest.
Arguments:
- hidden: bfloat16 [131072, 1024], P(('dp', 'node')), may hold values from -6 to 6
- norm_gain: float32 [1024], replicated, may hold values from 0.1 to 1.9
- w_query: bfloat16 [1024, 1024], P('node', 'dp'), may hold values from -0.1875 to 0.1875
- w_key: bfloat16 [1024, 256], P('node', 'dp'), may hold values from -0.1875 to 0.1875
- w_value: bfloat16 [1024, 256], P('node', 'dp'), may hold values from -0.1875 to 0.1875
- w_out: bfloat16 [1024, 1024], P('node', 'dp'), may hold values from -0.1875 to 0.1875
- doc_lengths: int32 [512, 4], P(('dp', 'node')), may hold values from 1 to 128, 256 in all within a row
- cotangent: bfloat16 [131072, 1024], P(('dp', 'node')), may hold values from -24 to 24
Outputs:
- output: bfloat16 [131072, 1024], P(('dp', 'node'))
- grad_hidden: bfloat16 [131072, 1024], P(('dp', 'node'))
- grad_query: float32 [1024, 1024], P('node', 'dp')
- grad_key: float32 [1024, 256], P('node', 'dp')
- grad_value: float32 [1024, 256], P('node', 'dp')
- grad_out: float32 [1024, 1024], P('node', 'dp')
Inputs may be any that keep to these rules, and one draw needn't show every extreme that they name: `doc_lengths`: each row holds the lengths of 4 documents that fill one sequence of 256 tokens; the longest is exactly half of 256.
All inputs are finite; a program needn't handle non-finite values.
Results may differ from a plain program's by a relative error of at most 0.0098.
Values may be sent and summed in bfloat16 or wider, within the bound.
No kernel may reach another device: no remote copies, remote signals or barrier semaphores. Data moves between devices by JAX's collectives and lax.ppermute only.
A program may use at most 128 MiB of HBM per device.

v0:
```python
import jax
import jax.numpy as jnp
from jax import lax
from jax.sharding import PartitionSpec as P

HD = 64
SEQ_LEN = 256


def rotary(length, head_dim):
    halfway = head_dim // 2
    frequency = 500000.0 ** (-2.0 * jnp.arange(halfway, dtype=jnp.float32) / head_dim)
    angles = jnp.arange(length, dtype=jnp.float32)[:, None] * frequency[None, :]
    return (jnp.cos(angles), jnp.sin(angles))


def rotate(tensor, cosine, sine_part, direction):
    halfway = tensor.shape[-1] // 2
    first = tensor[..., :halfway]
    second = tensor[..., halfway:]
    across = cosine[:, None, :]
    upward = direction * sine_part[:, None, :]
    return jnp.concatenate(
        [first * across - second * upward, first * upward + second * across], axis=-1
    )


def doc_allowed(doc_lengths, length):
    bounds = jnp.cumsum(doc_lengths, axis=-1)
    places = jnp.arange(length, dtype=jnp.int32)
    segment = jnp.sum((places[:, None] >= bounds[..., None, :]).astype(jnp.int32), axis=-1)
    same_doc = segment[..., :, None] == segment[..., None, :]
    causal = places[:, None] >= places[None, :]
    return jnp.logical_and(same_doc, causal)


def token_sum(left, right):
    return jnp.einsum("td,tf->df", left, right, preferred_element_type=jnp.float32)


def local(hidden, norm_gain, w_query, w_key, w_value, w_out, doc_lengths, cotangent):
    secondary = (
        lax.all_gather(w_query, "dp", axis=1, tiled=True),
        lax.all_gather(w_key, "dp", axis=1, tiled=True),
        lax.all_gather(w_value, "dp", axis=1, tiled=True),
        lax.all_gather(w_out, "dp", axis=1, tiled=True),
    )
    query_full, key_full, value_full, out_full = (
        lax.all_gather(secondary[0], "node", axis=0, tiled=True),
        lax.all_gather(secondary[1], "node", axis=0, tiled=True),
        lax.all_gather(secondary[2], "node", axis=0, tiled=True),
        lax.all_gather(secondary[3], "node", axis=0, tiled=True),
    )
    batch = doc_lengths.shape[0]
    length = SEQ_LEN
    q_heads = query_full.shape[1] // HD
    kv_heads = key_full.shape[1] // HD
    group_size = q_heads // kv_heads
    scale = HD ** (-0.5)
    cosine, sine_part = rotary(length, HD)
    allowed = doc_allowed(doc_lengths, length)[:, None, None]
    rows = hidden.astype(jnp.float32)
    inverse = lax.rsqrt(jnp.mean(rows * rows, axis=-1, keepdims=True) + 1e-05)
    unit_rows = rows * inverse
    normed = (unit_rows * norm_gain).astype(jnp.bfloat16)
    query_proj = jnp.dot(normed, query_full, preferred_element_type=jnp.float32).reshape(
        batch, length, q_heads, HD
    )
    key_proj = jnp.dot(normed, key_full, preferred_element_type=jnp.float32).reshape(
        batch, length, kv_heads, HD
    )
    query_rot = rotate(query_proj, cosine, sine_part, 1.0).astype(jnp.bfloat16)
    key_rot = rotate(key_proj, cosine, sine_part, 1.0).astype(jnp.bfloat16)
    value_rows = jnp.dot(normed, value_full, preferred_element_type=jnp.float32).astype(
        jnp.bfloat16
    )
    grouped = query_rot.reshape(batch, length, kv_heads, group_size, HD)
    value_heads = value_rows.reshape(batch, length, kv_heads, HD)
    scores = (
        jnp.einsum("bqkgd,bskd->bkgqs", grouped, key_rot, preferred_element_type=jnp.float32)
        * scale
    )
    raw_weights = jnp.where(allowed, jnp.exp(scores), 0.0)
    probability = raw_weights / jnp.sum(raw_weights, axis=-1, keepdims=True)
    prob_bf = probability.astype(jnp.bfloat16)
    mixed = jnp.einsum(
        "bkgqs,bskd->bqkgd", prob_bf, value_heads, preferred_element_type=jnp.float32
    )
    mixed = mixed.reshape(batch * length, q_heads * HD).astype(jnp.bfloat16)
    output = (rows + jnp.dot(mixed, out_full, preferred_element_type=jnp.float32)).astype(
        jnp.bfloat16
    )
    query_back, key_back, value_back, out_back = (
        lax.all_gather(secondary[0], "node", axis=0, tiled=True),
        lax.all_gather(secondary[1], "node", axis=0, tiled=True),
        lax.all_gather(secondary[2], "node", axis=0, tiled=True),
        lax.all_gather(secondary[3], "node", axis=0, tiled=True),
    )
    term_out = token_sum(mixed, cotangent)
    d_mixed = jnp.einsum(
        "tf,df->td", cotangent, out_back, preferred_element_type=jnp.float32
    ).astype(jnp.bfloat16)
    mixed_heads = d_mixed.reshape(batch, length, kv_heads, group_size, HD)
    d_prob = jnp.einsum(
        "bqkgd,bskd->bkgqs", mixed_heads, value_heads, preferred_element_type=jnp.float32
    )
    inner = jnp.sum(probability * d_prob, axis=-1, keepdims=True)
    d_score = (probability * (d_prob - inner) * scale).astype(jnp.bfloat16)
    query_grad_rot = jnp.einsum(
        "bkgqs,bskd->bqkgd", d_score, key_rot, preferred_element_type=jnp.float32
    )
    query_grad_rot = query_grad_rot.reshape(batch, length, q_heads, HD)
    d_query = (
        rotate(query_grad_rot, cosine, sine_part, -1.0)
        .reshape(batch * length, q_heads * HD)
        .astype(jnp.bfloat16)
    )
    key_grad_rot = jnp.einsum(
        "bkgqs,bqkgd->bskd", d_score, grouped, preferred_element_type=jnp.float32
    )
    d_key = (
        rotate(key_grad_rot, cosine, sine_part, -1.0)
        .reshape(batch * length, kv_heads * HD)
        .astype(jnp.bfloat16)
    )
    d_value = jnp.einsum(
        "bkgqs,bqkgd->bskd", prob_bf, mixed_heads, preferred_element_type=jnp.float32
    )
    d_value = d_value.reshape(batch * length, kv_heads * HD).astype(jnp.bfloat16)
    term_query = token_sum(normed, d_query)
    term_key = token_sum(normed, d_key)
    term_value = token_sum(normed, d_value)
    d_normed = jnp.einsum("tf,df->td", d_query, query_back, preferred_element_type=jnp.float32)
    d_normed = d_normed + jnp.einsum(
        "tf,df->td", d_key, key_back, preferred_element_type=jnp.float32
    )
    d_normed = d_normed + jnp.einsum(
        "tf,df->td", d_value, value_back, preferred_element_type=jnp.float32
    )
    d_unit = d_normed * norm_gain
    grad_hidden = (
        cotangent.astype(jnp.float32)
        + inverse * (d_unit - unit_rows * jnp.mean(d_unit * unit_rows, axis=-1, keepdims=True))
    ).astype(jnp.bfloat16)
    terms = (term_query, term_key, term_value, term_out)
    partial_terms = (
        lax.psum_scatter(terms[0], "dp", scatter_dimension=1, tiled=True),
        lax.psum_scatter(terms[1], "dp", scatter_dimension=1, tiled=True),
        lax.psum_scatter(terms[2], "dp", scatter_dimension=1, tiled=True),
        lax.psum_scatter(terms[3], "dp", scatter_dimension=1, tiled=True),
    )
    owned = (
        lax.psum_scatter(partial_terms[0], "node", scatter_dimension=0, tiled=True),
        lax.psum_scatter(partial_terms[1], "node", scatter_dimension=0, tiled=True),
        lax.psum_scatter(partial_terms[2], "node", scatter_dimension=0, tiled=True),
        lax.psum_scatter(partial_terms[3], "node", scatter_dimension=0, tiled=True),
    )
    return (output, grad_hidden, owned[0], owned[1], owned[2], owned[3])


def solution(mesh):
    placed = (
        P(("dp", "node"), None),
        P(),
        P("node", "dp"),
        P("node", "dp"),
        P("node", "dp"),
        P("node", "dp"),
        P(("dp", "node"), None),
        P(("dp", "node"), None),
    )
    return jax.shard_map(
        local,
        mesh=mesh,
        in_specs=placed,
        out_specs=(
            P(("dp", "node"), None),
            P(("dp", "node"), None),
            P("node", "dp"),
            P("node", "dp"),
            P("node", "dp"),
            P("node", "dp"),
        ),
        check_vma=False,
    )
```

profile of v0, /device:TPU:32, one launch (start us, length us, event | category | flops | bytes accessed | tf_op | source)
XLA Modules:
  0.0 889.6 jit_solution(8931731621414947099)
XLA Ops:
  7.2 43.9 %all_gather.34 = bf16[128,1024]{0,1:T(8,128)(2,1)} all-gather(bf16[128,32]{0,1:T(8,128)(2,1)} %param.13), channel_id=1, replica_groups=mesh['dp'=32,'node'=8] {'dp'}, dimensions={1}, use_global_device_ids=true | all-gather | bytes 270336 | tf_op jit(solution)/shard_map/all_gather | solution.py:46
  51.2 45.0 %all_gather.32 = bf16[128,1024]{0,1:T(8,128)(2,1)} all-gather(bf16[128,32]{0,1:T(8,128)(2,1)} %param.10), channel_id=1, replica_groups=mesh['dp'=32,'node'=8] {'dp'}, dimensions={1}, use_global_device_ids=true | all-gather | bytes 270336 | tf_op jit(solution)/shard_map/all_gather | solution.py:43
  96.3 37.2 %all_gather.30 = bf16[128,256]{0,1:T(8,128)(2,1)S(1)} all-gather(bf16[128,8]{0,1:T(8,128)(2,1)} %param.11), channel_id=1, replica_groups=mesh['dp'=32,'node'=8] {'dp'}, dimensions={1}, use_global_device_ids=true | all-gather | bytes 67584 | tf_op jit(solution)/shard_map/all_gather | solution.py:44
  135.0 27.0 %all_gather.31 = bf16[1024,256]{0,1:T(8,128)(2,1)S(1)} all-gather(bf16[128,256]{0,1:T(8,128)(2,1)S(1)} %all_gather.30), channel_id=1, replica_groups=mesh['dp'=32,'node'=8] {'node'}, dimensions={0}, use_global_device_ids=true | all-gather | bytes 589824 | tf_op jit(solution)/shard_map/all_gather | solution.py:50
  164.0 38.2 %all_gather.28 = bf16[128,256]{0,1:T(8,128)(2,1)S(1)} all-gather(bf16[128,8]{0,1:T(8,128)(2,1)S(1)} %copy-done.18), channel_id=1, replica_groups=mesh['dp'=32,'node'=8] {'dp'}, dimensions={1}, use_global_device_ids=true | all-gather | bytes 67584 | tf_op jit(solution)/shard_map/all_gather | solution.py:45
  203.7 3.8 convolution_convert_fusion
  207.5 4.1 reshape.150
  214.2 4.3 fusion.59
  229.9 25.9 %all_gather.29 = bf16[1024,256]{0,1:T(8,128)(2,1)S(1)} all-gather(bf16[128,256]{0,1:T(8,128)(2,1)S(1)} %all_gather.28), channel_id=1, replica_groups=mesh['dp'=32,'node'=8] {'node'}, dimensions={0}, use_global_device_ids=true | all-gather | bytes 589824 | tf_op jit(solution)/shard_map/all_gather | solution.py:51
  257.3 4.5 fusion.41
  261.9 15.9 %fusion.33 = f32[2,256,4,64]{1,3,2,0:T(8,128)S(1)} fusion(f32[2,4,256,256,4]{3,2,4,1,0:T(8,128)} %fusion.41, bf16[2,256,4,4,32]{1,4,3,2,0:T(8,128)(2,1)} %bitcast.149, bf16[2,256,4,4,32]{1,4,3,2,0:T(8,128)(2,1)S(1)} %bitcast.147, f32[2,4,256,256,4]{3,2,4,1,0:T(8,128)} %copy-done.20, f32[2,4,4,256]{3,2,1,0:T(4,128)S(1)} %copy-done.22, ...), kind=kOutput, calls=%fused_computation.35 | convolution fusion | flops 293609728 | bytes 18513920 | tf_op jit(solution)/shard_map/bkgqs,bqkgd->bskd/dot_general | solution.py:118
  280.5 13.4 %fusion.8 = f32[2,4,64,4,256]{4,2,3,1,0:T(8,128)S(1)} fusion(f32[2,4,256,256,4]{3,2,4,1,0:T(8,128)} %fusion.41, bf16[2,256,4,32]{1,3,2,0:T(8,128)(2,1)} %get-tuple-element.15, bf16[2,256,4,32]{1,3,2,0:T(8,128)(2,1)} %get-tuple-element.14, f32[2,4,256,256,4]{3,2,4,1,0:T(8,128)} %copy-done.20, f32[2,4,4,256]{3,2,1,0:T(4,128)S(1)} %copy-done.22, ...), kind=kOutput, calls=%fused_computation.11 | convolution fusion | flops 292036864 | bytes 19300352 | tf_op jit(solution)/shard_map/bkgqs,bskd->bqkgd/dot_general | solution.py:109
  298.7 3.3 fusion.53
  303.0 5.3 fusion.27
  317.4 21.5 %reduce-scatter.17.cloned.1.call-done = f32[1024,8]{0,1:T(8,128)} async-done(((f32[1024,256]{0,1:T(8,128)}), f32[1024,8]{0,1:T(8,128)}) %reduce-scatter.17.cloned.1.call-update) | async-done | bytes 32784 | tf_op jit(solution)/shard_map/reduce_scatter | solution.py:149
  341.9 114.8 %reduce-scatter.13.cloned.1.call-done = f32[1024,8]{0,1:T(8,128)} async-done(((f32[1024,256]{0,1:T(8,128)}), f32[1024,8]{0,1:T(8,128)}) %reduce-scatter.13.cloned.1.call-update) | async-done | bytes 32784 | tf_op jit(solution)/shard_map/reduce_scatter | solution.py:148
  456.8 3.8 fusion.13
  460.7 126.1 %reduce-scatter.9.cloned.1.call-done = f32[1024,32]{0,1:T(8,128)} async-done(((f32[1024,1024]{0,1:T(8,128)}), f32[1024,32]{0,1:T(8,128)}) %reduce-scatter.9.cloned.1.call-update) | async-done | bytes 131088 | tf_op jit(solution)/shard_map/reduce_scatter | solution.py:147
  586.8 4.3 fusion.19
  591.1 125.9 %reduce-scatter.21.cloned.1.call-done = f32[1024,32]{0,1:T(8,128)} async-done(((f32[1024,1024]{0,1:T(8,128)}), f32[1024,32]{0,1:T(8,128)}) %reduce-scatter.21.cloned.1.call-update) | async-done | bytes 131088 | tf_op jit(solution)/shard_map/reduce_scatter | solution.py:150
  719.9 38.5 %reduce-scatter.19.cloned.1.call-done = f32[128,8]{0,1:T(8,128)} async-done(((f32[1024,8]{0,1:T(8,128)}), f32[128,8]{0,1:T(8,128)}) %reduce-scatter.19.cloned.1.call-update) | async-done | bytes 4112 | tf_op jit(solution)/shard_map/reduce_scatter | solution.py:155
  758.4 41.5 %reduce-scatter.15.cloned.1.call-done = f32[128,8]{0,1:T(8,128)} async-done(((f32[1024,8]{0,1:T(8,128)}), f32[128,8]{0,1:T(8,128)}) %reduce-scatter.15.cloned.1.call-update) | async-done | bytes 4112 | tf_op jit(solution)/shard_map/reduce_scatter | solution.py:154
  799.9 41.5 %reduce-scatter.11.cloned.1.call-done = f32[128,32]{0,1:T(8,128)} async-done(((f32[1024,32]{0,1:T(8,128)}), f32[128,32]{0,1:T(8,128)}) %reduce-scatter.11.cloned.1.call-update) | async-done | bytes 16400 | tf_op jit(solution)/shard_map/reduce_scatter | solution.py:153
  841.3 41.5 %reduce-scatter.23.cloned.1.call-done = f32[128,32]{0,1:T(8,128)} async-done(((f32[1024,32]{0,1:T(8,128)}), f32[128,32]{0,1:T(8,128)}) %reduce-scatter.23.cloned.1.call-update) | async-done | bytes 16400 | tf_op jit(solution)/shard_map/reduce_scatter | solution.py:156
  (109 shorter events, 43.6 us)
Async XLA Ops:
  7.2 155.7 %copy-start = (bf16[512,1024]{1,0:T(8,128)(2,1)S(1)}, bf16[512,1024]{1,0:T(8,128)(2,1)}, u32[]{:S(2)}) copy-start(bf16[512,1024]{1,0:T(8,128)(2,1)} %param.8) | copy-start | bytes 3145732
  7.2 155.7 %copy-start.17 = (f32[1024]{0:T(1024)S(1)}, f32[1024]{0:T(1024)}, u32[]{:S(2)}) copy-start(f32[1024]{0:T(1024)} %param.9) | copy-start | bytes 12292
  7.2 196.5 %all-gather.5.cloned.1.call-start = ((), (), s32[]{:S(2)}) async-start(), calls=%async_computation.9 | async-start | bytes 2359296 | tf_op jit(solution)/shard_map/all_gather | solution.py:52
  51.1 163.1 %all-gather.3.cloned.1.call-start = ((), (), s32[]{:S(2)}) async-start(), calls=%async_computation.8 | async-start | bytes 2359296 | tf_op jit(solution)/shard_map/all_gather | solution.py:49
  96.2 242.7 %reduce-scatter.17.cloned.1.call-start = ((), (), s32[]{:S(2)}) async-start(), calls=%async_computation.14 | async-start | bytes 1081344 | tf_op jit(solution)/shard_map/reduce_scatter | solution.py:149
  163.4 40.2 %copy-start.9 = (bf16[512,1024]{1,0:T(8,128)(2,1)S(1)}, bf16[512,1024]{1,0:T(8,128)(2,1)}, u32[]{:S(2)}) copy-start(bf16[512,1024]{1,0:T(8,128)(2,1)} %param.15) | copy-start | bytes 3145732
  202.7 22.0 %copy-start.13 = (pred[2,256,256]{1,2,0:T(8,128)(4,1)}, pred[2,256,256]{1,2,0:T(8,128)(4,1)S(1)}, u32[]{:S(2)}) copy-start(pred[2,256,256]{1,2,0:T(8,128)(4,1)S(1)} %compare_and_fusion) | copy-start | bytes 393220
  221.1 1.3 copy-start.15
  221.1 1.3 copy-start.16
  222.4 2.3 copy-start.12
  222.4 2.3 copy-start.2
  224.7 3.2 copy-start.20
  224.7 3.2 copy-start.21
  229.8 226.9 %reduce-scatter.13.cloned.1.call-start = ((), (), s32[]{:S(2)}) async-start(), calls=%async_computation.12 | async-start | bytes 1081344 | tf_op jit(solution)/shard_map/reduce_scatter | solution.py:148
  257.3 4.6 copy-start.6
  257.3 4.5 copy-start.22
  280.4 306.3 %reduce-scatter.9.cloned.1.call-start = ((), (), s32[]{:S(2)}) async-start(), calls=%async_computation.10 | async-start | bytes 4325376 | tf_op jit(solution)/shard_map/reduce_scatter | solution.py:147
  302.0 415.1 %reduce-scatter.21.cloned.1.call-start = ((), (), s32[]{:S(2)}) async-start(), calls=%async_computation.16 | async-start | bytes 4325376 | tf_op jit(solution)/shard_map/reduce_scatter | solution.py:150
  308.3 2.3 copy-start.10
  313.9 444.5 %reduce-scatter.19.cloned.1.call-start = ((), (), s32[]{:S(2)}) async-start(), calls=%async_computation.15 | async-start | bytes 36864 | tf_op jit(solution)/shard_map/reduce_scatter | solution.py:155
  339.0 460.9 %reduce-scatter.15.cloned.1.call-start = ((), (), s32[]{:S(2)}) async-start(), calls=%async_computation.13 | async-start | bytes 36864 | tf_op jit(solution)/shard_map/reduce_scatter | solution.py:154
  456.8 384.6 %reduce-scatter.11.cloned.1.call-start = ((), (), s32[]{:S(2)}) async-start(), calls=%async_computation.11 | async-start | bytes 147456 | tf_op jit(solution)/shard_map/reduce_scatter | solution.py:153
  586.8 130.3 %copy-start.1 = (f32[512,1024]{1,0:T(8,128)S(1)}, f32[512,1024]{1,0:T(8,128)}, u32[]{:S(2)}) copy-start(f32[512,1024]{1,0:T(8,128)} %get-tuple-element.24) | copy-start | bytes 6291460
  586.8 296.0 %reduce-scatter.23.cloned.1.call-start = ((), (), s32[]{:S(2)}) async-start(), calls=%async_computation.17 | async-start | bytes 147456 | tf_op jit(solution)/shard_map/reduce_scatter | solution.py:156
  (9 other events, 8.2 us)
Sparse Core Ops, SparseCore 0:
  51.2 45.8 all-gather.4
  98.8 51.7 all-gather.2
  229.9 108.9 reduce-scatter.16
  343.4 113.2 reduce-scatter.12
  460.8 125.8 reduce-scatter.8
  591.4 125.6 reduce-scatter.20
  720.1 38.2 reduce-scatter.18
  761.6 38.2 reduce-scatter.14
  802.9 38.3 reduce-scatter.10
  844.4 38.3 reduce-scatter.22
where the time goes:
time: 890 us
  waiting for transfers between devices  551 us (62%)
  blocking collectives  217 us (24%)
  matrix products  76.7 us (9%)
  local copies, waits for them, and re-layouts  18.8 us (2%)
  between operations  14.6 us (2%)
  other arithmetic  10.2 us (1%)
    reduce_scatter x1, waiting for transfers between devices, local(): lax.psum_scatter(terms[0], 'dp', scatter_dimension=1, tiled=True)  126 us
    reduce_scatter x1, waiting for transfers between devices, local(): lax.psum_scatter(terms[3], 'dp', scatter_dimension=1, tiled=True)  126 us
    reduce_scatter x1, waiting for transfers between devices, local(): lax.psum_scatter(terms[1], 'dp', scatter_dimension=1, tiled=True)  115 us
    all_gather x1, blocking collectives, local(): lax.all_gather(w_query, 'dp', axis=1, tiled=True)  45 us
    all_gather x1, blocking collectives, local(): lax.all_gather(w_out, 'dp', axis=1, tiled=True)  43.9 us
    reduce_scatter x1, waiting for transfers between devices, local(): lax.psum_scatter(partial_terms[0], 'node', scatter_dimension=0, tiled=True)  41.5 us
    reduce_scatter x1, waiting for transfers between devices, local(): lax.psum_scatter(partial_terms[1], 'node', scatter_dimension=0, tiled=True)  41.5 us
    reduce_scatter x1, waiting for transfers between devices, local(): lax.psum_scatter(partial_terms[3], 'node', scatter_dimension=0, tiled=True)  41.5 us
  transfers between devices with their start and end apart: 10, of which 8 were waited for; matrix products, arithmetic and copies ran while one was open for 10% of the time, Pallas kernels for 0%

commit v1 on v0

--- a/solution.py
+++ b/solution.py
@@ -38,19 +38,75 @@
     return jnp.einsum("td,tf->df", left, right, preferred_element_type=jnp.float32)
 
 
+AXES = ("xh", "z", "c", "xl", "y")
+SIZES = (2, 8, 2, 2, 4)
+
+
+def shift(block, axis, size, step):
+    return lax.ppermute(block, axis, [(i, (i - step) % size) for i in range(size)])
+
+
+def swap(block, axis):
+    return lax.ppermute(block, axis, [(0, 1), (1, 0)])
+
+
+def gather_blocks(block):
+    mine = lax.all_to_all(
+        jnp.broadcast_to(block[None], (16,) + block.shape), ("xh", "z"), 0, 0, tiled=True
+    )
+    own = jnp.stack([mine, swap(mine, "xl")])
+    round_y = [own, shift(own, "y", 4, 1), shift(own, "y", 4, 2), shift(own, "y", 4, 3)]
+    return [round_y, [swap(part, "c") for part in round_y]]
+
+
+def scatter_blocks(keep, send):
+    f32 = jnp.float32
+    summed = []
+    for step in range(4):
+        arrived = swap(send[step], "c")
+        summed.append((keep[step].astype(f32) + arrived.astype(f32)).astype(jnp.bfloat16))
+    arrived = [shift(summed[step], "y", 4, -step) for step in (1, 2, 3)]
+    total = summed[0].astype(f32) + sum(part.astype(f32) for part in arrived)
+    total = total.astype(jnp.bfloat16)
+    pair = (total[0].astype(f32) + swap(total[1], "xl").astype(f32)).astype(jnp.bfloat16)
+    parts = lax.all_to_all(pair, ("xh", "z"), 0, 0, tiled=True)
+    return jnp.sum(parts.astype(f32), axis=0)
+
+
+def pack(w_query, w_key, w_value, w_out):
+    return jnp.concatenate([w_query.T, w_key.T, w_value.T, w_out.T], axis=0)
+
+
+def whole(blocks):
+    c, xl, y = (lax.axis_index(name) for name in ("c", "xl", "y"))
+    every = jnp.stack([jnp.stack(row) for row in blocks])
+    every = jnp.take(every, (jnp.arange(2) - c) % 2, axis=0)
+    every = jnp.take(every, (jnp.arange(4) - y) % 4, axis=1)
+    every = jnp.take(every, (jnp.arange(2) - xl) % 2, axis=2)
+    every = every.transpose(2, 1, 5, 3, 0, 4)
+    every = every.reshape(1024, 32, 80)
+    return (
+        every[..., :32].reshape(1024, 1024),
+        every[..., 32:40].reshape(1024, 256),
+        every[..., 40:48].reshape(1024, 256),
+        every[..., 48:].reshape(1024, 1024),
+    )
+
+
+def spread(terms):
+    c, xl, y = (lax.axis_index(name) for name in ("c", "xl", "y"))
+    every = jnp.concatenate(
+        [term.astype(jnp.bfloat16).reshape(1024, 32, -1) for term in terms], axis=-1
+    )
+    every = every.reshape(2, 4, 128, 16, 2, 80).transpose(4, 1, 0, 3, 5, 2)
+    every = jnp.take(every, (jnp.arange(2) + c) % 2, axis=0)
+    every = jnp.take(every, (jnp.arange(4) + y) % 4, axis=1)
+    return jnp.take(every, (jnp.arange(2) + xl) % 2, axis=2)
+
+
 def local(hidden, norm_gain, w_query, w_key, w_value, w_out, doc_lengths, cotangent):
-    secondary = (
-        lax.all_gather(w_query, "dp", axis=1, tiled=True),
-        lax.all_gather(w_key, "dp", axis=1, tiled=True),
-        lax.all_gather(w_value, "dp", axis=1, tiled=True),
-        lax.all_gather(w_out, "dp", axis=1, tiled=True),
-    )
-    query_full, key_full, value_full, out_full = (
-        lax.all_gather(secondary[0], "node", axis=0, tiled=True),
-        lax.all_gather(secondary[1], "node", axis=0, tiled=True),
-        lax.all_gather(secondary[2], "node", axis=0, tiled=True),
-        lax.all_gather(secondary[3], "node", axis=0, tiled=True),
-    )
+    blocks = gather_blocks(pack(w_query, w_key, w_value, w_out))
+    query_full, key_full, value_full, out_full = whole(blocks)
     batch = doc_lengths.shape[0]
     length = SEQ_LEN
     q_heads = query_full.shape[1] // HD
@@ -90,15 +146,9 @@
     output = (rows + jnp.dot(mixed, out_full, preferred_element_type=jnp.float32)).astype(
         jnp.bfloat16
     )
-    query_back, key_back, value_back, out_back = (
-        lax.all_gather(secondary[0], "node", axis=0, tiled=True),
-        lax.all_gather(secondary[1], "node", axis=0, tiled=True),
-        lax.all_gather(secondary[2], "node", axis=0, tiled=True),
-        lax.all_gather(secondary[3], "node", axis=0, tiled=True),
-    )
     term_out = token_sum(mixed, cotangent)
     d_mixed = jnp.einsum(
-        "tf,df->td", cotangent, out_back, preferred_element_type=jnp.float32
+        "tf,df->td", cotangent, out_full, preferred_element_type=jnp.float32
     ).astype(jnp.bfloat16)
     mixed_heads = d_mixed.reshape(batch, length, kv_heads, group_size, HD)
     d_prob = jnp.einsum(
@@ -130,12 +180,12 @@
     term_query = token_sum(normed, d_query)
     term_key = token_sum(normed, d_key)
     term_value = token_sum(normed, d_value)
-    d_normed = jnp.einsum("tf,df->td", d_query, query_back, preferred_element_type=jnp.float32)
+    d_normed = jnp.einsum("tf,df->td", d_query, query_full, preferred_element_type=jnp.float32)
     d_normed = d_normed + jnp.einsum(
-        "tf,df->td", d_key, key_back, preferred_element_type=jnp.float32
+        "tf,df->td", d_key, key_full, preferred_element_type=jnp.float32
     )
     d_normed = d_normed + jnp.einsum(
-        "tf,df->td", d_value, value_back, preferred_element_type=jnp.float32
+        "tf,df->td", d_value, value_full, preferred_element_type=jnp.float32
     )
     d_unit = d_normed * norm_gain
     grad_hidden = (
@@ -143,43 +193,26 @@
         + inverse * (d_unit - unit_rows * jnp.mean(d_unit * unit_rows, axis=-1, keepdims=True))
     ).astype(jnp.bfloat16)
     terms = (term_query, term_key, term_value, term_out)
-    partial_terms = (
-        lax.psum_scatter(terms[0], "dp", scatter_dimension=1, tiled=True),
-        lax.psum_scatter(terms[1], "dp", scatter_dimension=1, tiled=True),
-        lax.psum_scatter(terms[2], "dp", scatter_dimension=1, tiled=True),
-        lax.psum_scatter(terms[3], "dp", scatter_dimension=1, tiled=True),
-    )
-    owned = (
-        lax.psum_scatter(partial_terms[0], "node", scatter_dimension=0, tiled=True),
-        lax.psum_scatter(partial_terms[1], "node", scatter_dimension=0, tiled=True),
-        lax.psum_scatter(partial_terms[2], "node", scatter_dimension=0, tiled=True),
-        lax.psum_scatter(partial_terms[3], "node", scatter_dimension=0, tiled=True),
-    )
-    return (output, grad_hidden, owned[0], owned[1], owned[2], owned[3])
+    every = spread(terms)
+    owned = scatter_blocks(every[0], every[1])
+    return (
+        output,
+        grad_hidden,
+        owned[:32].T,
+        owned[32:40].T,
+        owned[40:48].T,
+        owned[48:].T,
+    )
 
 
 def solution(mesh):
-    placed = (
-        P(("dp", "node"), None),
-        P(),
-        P("node", "dp"),
-        P("node", "dp"),
-        P("node", "dp"),
-        P("node", "dp"),
-        P(("dp", "node"), None),
-        P(("dp", "node"), None),
-    )
+    wide = jax.sharding.Mesh(mesh.devices.reshape(SIZES), AXES)
+    dp, node = ("xh", "z", "c"), ("xl", "y")
+    tokens, weight = P(AXES, None), P(node, dp)
     return jax.shard_map(
         local,
-        mesh=mesh,
-        in_specs=placed,
-        out_specs=(
-            P(("dp", "node"), None),
-            P(("dp", "node"), None),
-            P("node", "dp"),
-            P("node", "dp"),
-            P("node", "dp"),
-            P("node", "dp"),
-        ),
+        mesh=wide,
+        in_specs=(tokens, P(), weight, weight, weight, weight, tokens, tokens),
+        out_specs=(tokens, tokens, weight, weight, weight, weight),
         check_vma=False,
     )

time: 890 us -> 369 us (0.41)
  waiting for transfers between devices: 551 us -> 86.1 us
  blocking collectives: 217 us -> 0 us
  local copies, waits for them, and re-layouts: 18.8 us -> 118 us
  other arithmetic: 10.2 us -> 65.3 us
  starting transfers between devices: 0.67 us -> 32.5 us
  matrix products: 76.7 us -> 59.8 us
  between operations: 14.6 us -> 1.39 us
    reduce_scatter x8 -> x0, waiting for transfers between devices: 551 us -> none  [the longest x1 126 us: local(): lax.psum_scatter(terms[0], 'dp', scatter_dimension=1, tiled=True)]
    all_gather x6 -> x0, blocking collectives: 217 us -> none  [the longest x1 45 us: local(): lax.all_gather(w_query, 'dp', axis=1, tiled=True)]
    ppermute x0 -> x16, waiting for transfers between devices: none -> 68.3 us  [the longest x6 51.9 us: shift(): lax.ppermute(block, axis, [(i, (i - step) % size) for i in range(size)])]
    another operation x2 -> x22, local copies, waits for them, and re-layouts: 0.17 us -> 51.2 us  [the longest x6 16.2 us: whole(): every = jnp.take(every, (jnp.arange(2) - c) % 2, axis=0)]
    select_n x0 -> x6, other arithmetic: none -> 24.8 us  [the longest x2 5.45 us: spread(): every = jnp.take(every, (jnp.arange(4) + y) % 4, axis=1)]
    transpose x0 -> x2, other arithmetic: none -> 19.9 us  [the longest x1 16.8 us: spread(): every = every.reshape(2, 4, 128, 16, 2, 80).transpose(4, 1, 0, 3, 5, 2)]
    all_to_all x0 -> x2, starting transfers between devices: none -> 19.4 us  [the longest x1 11 us: gather_blocks(): lax.all_to_all(jnp.broadcast_to(block[None], (16,) + block.shape), ('xh',...]
    all_to_all x0 -> x2, waiting for transfers between devices: none -> 17.9 us  [the longest x1 11.1 us: gather_blocks(): lax.all_to_all(jnp.broadcast_to(block[None], (16,) + block.shape), ('xh',...]
  transfers between devices with their start and end apart: 10 -> 18, of which waited for: 8 -> 11; matrix products, arithmetic and copies ran while one was open for 10% -> 4% of each run, Pallas kernels for 0% -> 0%
where the time goes in v1:
time: 369 us; the launch traced here: 363 us
  local copies, waits for them, and re-layouts  118 us (32%)
  waiting for transfers between devices  86.1 us (23%)
  other arithmetic  65.3 us (18%)
  matrix products  59.8 us (16%)
  starting transfers between devices  32.5 us (9%)
    ppermute x6, waiting for transfers between devices, shift(): lax.ppermute(block, axis, [(i, (i - step) % size) for i in range(size)])  51.9 us
    transpose x1, other arithmetic, spread(): every = every.reshape(2, 4, 128, 16, 2, 80).transpose(4, 1, 0, 3, 5, 2)  16.8 us
    ppermute x10, waiting for transfers between devices, swap(): return lax.ppermute(block, axis, [(0, 1), (1, 0)])  16.4 us
    another operation x6, local copies, waits for them, and re-layouts, whole(): every = jnp.take(every, (jnp.arange(2) - c) % 2, axis=0)  16.2 us
    another operation x6, local copies, waits for them, and re-layouts, whole(): every = jnp.take(every, (jnp.arange(2) - xl) % 2, axis=2)  16 us
    dot_general x1, matrix products, local(): jnp.einsum('bkgqs,bskd->bqkgd', d_score, key_rot, preferred_element_type=...  14.6 us
    dot_general x1, matrix products, local(): jnp.einsum('bkgqs,bqkgd->bskd', d_score, grouped, preferred_element_type=...  13.8 us
    concatenate x4, local copies, waits for them, and re-layouts, spread(): jnp.concatenate([term.astype(jnp.bfloat16).reshape(1024, 32, -1) for term...  12.3 us
  transfers between devices with their start and end apart: 18, of which 11 were waited for; matrix products, arithmetic and copies ran while one was open for 4% of the time, Pallas kernels for 0%

profile of v1, /device:TPU:32, one launch (start us, length us, event | category | flops | bytes accessed | tf_op | source)
XLA Modules:
  0.0 363.4 jit_solution(412965458995461794)
XLA Ops:
  2.2 11.0 %all-to-all-start = ((bf16[16,80,128]{2,1,0:T(8,128)(2,1)}), bf16[16,80,128]{2,1,0:T(8,128)(2,1)S(1)}, u32[]{:S(2)}, u32[]{:S(2)}) async-start(bf16[16,80,128]{2,1,0:T(8,128)(2,1)} %broadcast_in_dim.41), calls=%async_computation | async-start | bytes 655360 | tf_op jit(solution)/shard_map/all_to_all | solution.py:54
  14.8 11.1 %all-to-all-done = bf16[16,80,128]{2,1,0:T(8,128)(2,1)S(1)} async-done(((bf16[16,80,128]{2,1,0:T(8,128)(2,1)}), bf16[16,80,128]{2,1,0:T(8,128)(2,1)S(1)}, u32[]{:S(2)}, u32[]{:S(2)}) %all-to-all-start) | async-done | bytes 327712 | tf_op jit(solution)/shard_map/all_to_all | solution.py:54
  41.0 11.1 %collective-permute-done.3 = bf16[2,16,80,128]{3,2,1,0:T(8,128)(2,1)S(1)} collective-permute-done((bf16[2,16,80,128]{3,2,1,0:T(8,128)(2,1)}, bf16[2,16,80,128]{3,2,1,0:T(8,128)(2,1)S(1)}, u32[]{:S(2)}, u32[]{:S(2)}) %collective-permute-start.3) | collective-permute-done | bytes 655392 | tf_op jit(solution)/shard_map/ppermute | solution.py:46
  52.1 12.3 %collective-permute-done.2 = bf16[2,16,80,128]{3,2,1,0:T(8,128)(2,1)} collective-permute-done((bf16[2,16,80,128]{3,2,1,0:T(8,128)(2,1)}, bf16[2,16,80,128]{3,2,1,0:T(8,128)(2,1)}, u32[]{:S(2)}, u32[]{:S(2)}) %collective-permute-start.2) | collective-permute-done | bytes 655392 | tf_op jit(solution)/shard_map/ppermute | solution.py:46
  77.3 9.4 %while.8 = (s32[]{:T(128)}, bf16[2,4,2,16,80,128]{5,4,3,2,1,0:T(8,128)(2,1)}, s32[2,1]{0,1:T(1,128)S(1)}, bf16[2,4,2,16,80,128]{5,4,3,2,1,0:T(8,128)(2,1)}, s32[]{:T(128)}) while((s32[]{:T(128)}, bf16[2,4,2,16,80,128]{5,4,3,2,1,0:T(8,128)(2,1)}, s32[2,1]{0,1:T(1,128)S(1)}, bf16[2,4,2,16,80,128]{5,4,3,2,1,0:T(8,128)(2,1)}, s32[]{:T(128)}) %tuple.87), condition=%wide.while_cond, body=%wide.while_body.sunk | while | flops 2 | bytes 5243477 | solution.py:83
  86.7 5.4 %broadcast_select_fusion.1 = bf16[2,4,2,16,80,128]{5,4,3,2,1,0:T(8,128)(2,1)} fusion(bf16[2,4,2,16,80,128]{5,4,3,2,1,0:T(8,128)(2,1)} %get-tuple-element.37, pred[2]{0:T(512)(128)(4,1)S(1)} %get-tuple-element.128), kind=kLoop, calls=%fused_computation.31 | loop fusion | flops 2621440 | bytes 10485762 | tf_op jit(solution)/shard_map/jit(_take)/select_n | solution.py:83
  92.1 6.1 %gather_fusion = bf16[4,2,2,16,80,128]{5,4,3,2,1,0:T(8,128)(2,1)} fusion(bf16[2,4,2,16,80,128]{5,4,3,2,1,0:T(8,128)(2,1)} %broadcast_select_fusion.1, s32[1024]{0:T(1024)S(1)} %pad_clamp_fusion.1), kind=kCustom, calls=%fused_computation.clone | custom fusion | bytes 10485776 | tf_op jit(solution)/shard_map/jit(_take)/gather | solution.py:84
  98.2 5.4 %select_bitcast_fusion.3 = bf16[2,4,2,16,80,128]{5,4,3,2,0,1:T(8,128)(2,1)} fusion(bf16[4,2,2,16,80,128]{5,4,3,2,1,0:T(8,128)(2,1)} %gather_fusion, pred[4]{0:T(512)(128)(4,1)S(1)} %get-tuple-element.134), kind=kLoop, calls=%fused_computation.29 | loop fusion | flops 2621440 | bytes 10485764 | tf_op jit(solution)/shard_map/jit(_take)/select_n | solution.py:84
  107.0 9.4 %while.9 = (s32[]{:T(128)}, bf16[2,4,2,16,80,128]{5,4,3,2,0,1:T(8,128)(2,1)}, s32[2,1]{0,1:T(1,128)S(1)}, bf16[2,2,4,16,80,128]{5,4,3,2,1,0:T(8,128)(2,1)}, s32[]{:T(128)}) while((s32[]{:T(128)}, bf16[2,4,2,16,80,128]{5,4,3,2,0,1:T(8,128)(2,1)}, s32[2,1]{0,1:T(1,128)S(1)}, bf16[2,2,4,16,80,128]{5,4,3,2,1,0:T(8,128)(2,1)}, s32[]{:T(128)}) %tuple.90), condition=%wide.while_cond.1, body=%wide.while_body.1.sunk | while | flops 2 | bytes 5243477 | solution.py:85
  119.4 6.4 %copy.62 = bf16[2,4,128,16,2,80]{2,1,0,5,4,3:T(4,128)(2,1)} copy(bf16[2,4,128,16,2,80]{2,5,3,1,4,0:T(8,128)(2,1)S(1)} %select_bitcast_fusion.2) | data formatting | bytes 10485760 | tf_op jit(solution)/shard_map/transpose | solution.py:86
  125.8 9.5 %reshape.226 = bf16[1024,32,80]{0,2,1:T(8,128)(2,1)} reshape(bf16[2,4,128,16,2,80]{2,1,0,5,4,3:T(4,128)(2,1)} %copy.62) | data formatting | bytes 10485760 | tf_op jit(solution)/shard_map/reshape | solution.py:87
  135.3 5.2 %fusion.83 = (bf16[1024,32,32]{0,2,1:T(8,128)(2,1)}, bf16[1024,32,32]{0,2,1:T(8,128)(2,1)}) fusion(bf16[1024,32,80]{0,2,1:T(8,128)(2,1)} %reshape.226), kind=kLoop, calls=%fused_computation.180 | loop fusion | bytes 8388608 | tf_op jit(solution)/shard_map/slice | solution.py:92
  163.9 14.6 %fusion.10 = f32[2,4,64,4,256]{4,2,3,1,0:T(8,128)} fusion(f32[2,4,256,256,4]{3,2,4,1,0:T(8,128)} %fusion.48, bf16[2,256,4,32]{1,3,2,0:T(8,128)(2,1)} %get-tuple-element.115, bf16[2,256,4,32]{1,3,2,0:T(8,128)(2,1)} %get-tuple-element.114, f32[2,4,256,256,4]{3,2,4,1,0:T(8,128)} %copy-done.24, f32[2,4,4,256]{3,2,1,0:T(4,128)S(1)} %get-tuple-element.123, ...), kind=kOutput, calls=%fused_computation.34 | convolution fusion | flops 292036864 | bytes 19300352 | tf_op jit(solution)/shard_map/bkgqs,bskd->bqkgd/dot_general | solution.py:159
  178.5 13.8 %fusion.40 = f32[2,256,4,64]{1,3,2,0:T(8,128)} fusion(f32[2,4,256,256,4]{3,2,4,1,0:T(8,128)} %fusion.48, bf16[2,256,4,4,32]{1,4,3,2,0:T(8,128)(2,1)S(1)} %bitcast.319, bf16[2,256,4,4,32]{1,4,3,2,0:T(8,128)(2,1)S(1)} %bitcast.317, f32[2,4,256,256,4]{3,2,4,1,0:T(8,128)} %copy-done.24, f32[2,4,4,256]{3,2,1,0:T(4,128)S(1)} %get-tuple-element.123, ...), kind=kOutput, calls=%fused_computation.75 | convolution fusion | flops 293609728 | bytes 18513920 | tf_op jit(solution)/shard_map/bkgqs,bqkgd->bskd/dot_general | solution.py:168
  224.1 16.8 %maximum_bitcast_fusion = bf16[2,4,2,16,80,128]{5,1,2,4,0,3:T(4,128)(2,1)} fusion(bf16[2,4,128,16,2,32]{2,1,0,5,4,3:T(4,128)(2,1)S(1)} %copy-done.4, bf16[2,4,128,16,2,8]{2,1,0,5,4,3:T(4,128)(2,1)} %concatenate.43, bf16[2,4,128,16,2,8]{2,1,0,5,4,3:T(4,128)(2,1)} %concatenate.42, bf16[2,4,128,16,2,32]{2,1,0,5,4,3:T(4,128)(2,1)} %concatenate.41), kind=kLoop, calls=%fused_computation.25 | loop fusion | flops 7864320 | bytes 10485760 | tf_op jit(solution)/shard_map/transpose | solution.py:101
  244.3 14.4 %while.10 = (s32[]{:T(128)}, bf16[2,4,2,16,80,128]{5,1,2,4,0,3:T(4,128)(2,1)}, s32[2,1]{0,1:T(1,128)S(1)}, bf16[2,4,2,16,80,128]{5,4,3,2,1,0:T(8,128)(2,1)}, s32[]{:T(128)}) while((s32[]{:T(128)}, bf16[2,4,2,16,80,128]{5,1,2,4,0,3:T(4,128)(2,1)}, s32[2,1]{0,1:T(1,128)S(1)}, bf16[2,4,2,16,80,128]{5,4,3,2,1,0:T(8,128)(2,1)}, s32[]{:T(128)}) %tuple.93), condition=%wide.while_cond.clone, body=%wide.while_body.clone.sunk | while | flops 2 | bytes 52428944 | solution.py:102
  258.8 5.4 %broadcast_select_fusion = bf16[2,4,2,16,80,128]{5,4,3,2,1,0:T(8,128)(2,1)} fusion(bf16[2,4,2,16,80,128]{5,4,3,2,1,0:T(8,128)(2,1)} %get-tuple-element.39, pred[2]{0:T(512)(128)(4,1)S(1)} %get-tuple-element.127), kind=kLoop, calls=%fused_computation.30 | loop fusion | flops 2621440 | bytes 10485762 | tf_op jit(solution)/shard_map/jit(_take)/select_n | solution.py:102
  264.2 6.1 %gather_fusion.1 = bf16[4,2,2,16,80,128]{5,4,3,2,1,0:T(8,128)(2,1)} fusion(bf16[2,4,2,16,80,128]{5,4,3,2,1,0:T(8,128)(2,1)} %broadcast_select_fusion, s32[1024]{0:T(1024)S(1)} %pad_clamp_fusion), kind=kCustom, calls=%fused_computation.1.clone | custom fusion | bytes 10485776 | tf_op jit(solution)/shard_map/jit(_take)/gather | solution.py:103
  270.3 5.4 %select_bitcast_fusion.1 = bf16[2,4,2,16,80,128]{5,4,3,2,0,1:T(8,128)(2,1)} fusion(bf16[4,2,2,16,80,128]{5,4,3,2,1,0:T(8,128)(2,1)} %gather_fusion.1, pred[4]{0:T(512)(128)(4,1)S(1)} %get-tuple-element.133), kind=kLoop, calls=%fused_computation.27 | loop fusion | flops 2621440 | bytes 10485764 | tf_op jit(solution)/shard_map/jit(_take)/select_n | solution.py:103
  279.1 9.4 %while.11 = (s32[]{:T(128)}, bf16[2,4,2,16,80,128]{5,4,3,2,0,1:T(8,128)(2,1)}, s32[2,1]{0,1:T(1,128)S(1)}, bf16[2,2,4,16,80,128]{5,4,3,2,1,0:T(8,128)(2,1)}, s32[]{:T(128)}) while((s32[]{:T(128)}, bf16[2,4,2,16,80,128]{5,4,3,2,0,1:T(8,128)(2,1)}, s32[2,1]{0,1:T(1,128)S(1)}, bf16[2,2,4,16,80,128]{5,4,3,2,1,0:T(8,128)(2,1)}, ...), condition=%wide.while_cond.1.clone, body=%wide.while_body.1.clone.sunk | while | flops 2 | bytes 5243477 | solution.py:104
  302.0 24.9 %collective-permute-done.14 = bf16[2,16,80,128]{3,2,1,0:T(8,128)(2,1)S(1)} collective-permute-done((bf16[2,16,80,128]{3,2,1,0:T(8,128)(2,1)S(1)}, bf16[2,16,80,128]{3,2,1,0:T(8,128)(2,1)S(1)}, u32[]{:S(2)}, u32[]{:S(2)}) %collective-permute-start.14) | collective-permute-done | bytes 655392 | tf_op jit(solution)/shard_map/ppermute | solution.py:46
  332.5 8.2 %collective-permute-done.15 = bf16[16,80,128]{2,1,0:T(8,128)(2,1)S(1)} collective-permute-done((bf16[16,80,128]{2,1,0:T(8,128)(2,1)S(1)}, bf16[16,80,128]{2,1,0:T(8,128)(2,1)S(1)}, u32[]{:S(2)}, u32[]{:S(2)}) %collective-permute-start.15) | collective-permute-done | bytes 327712 | tf_op jit(solution)/shard_map/ppermute | solution.py:50
  341.6 8.4 %all-to-all-start.1 = ((bf16[16,80,128]{2,1,0:T(8,128)(2,1)}), bf16[16,80,128]{2,1,0:T(8,128)(2,1)S(1)}, u32[]{:S(2)}, u32[]{:S(2)}) async-start(bf16[16,80,128]{2,1,0:T(8,128)(2,1)} %fusion.51), calls=%async_computation.1 | async-start | bytes 655360 | tf_op jit(solution)/shard_map/all_to_all | solution.py:72
  355.1 6.8 %all-to-all-done.1 = bf16[16,80,128]{2,1,0:T(8,128)(2,1)S(1)} async-done(((bf16[16,80,128]{2,1,0:T(8,128)(2,1)}), bf16[16,80,128]{2,1,0:T(8,128)(2,1)S(1)}, u32[]{:S(2)}, u32[]{:S(2)}) %all-to-all-start.1) | async-done | bytes 327712 | tf_op jit(solution)/shard_map/all_to_all | solution.py:72
  (187 shorter events, 167.9 us)
Async XLA Ops:
  2.2 23.7 %all-to-all-start = ((bf16[16,80,128]{2,1,0:T(8,128)(2,1)}), bf16[16,80,128]{2,1,0:T(8,128)(2,1)S(1)}, u32[]{:S(2)}, u32[]{:S(2)}) async-start(bf16[16,80,128]{2,1,0:T(8,128)(2,1)} %broadcast_in_dim.41), calls=%async_computation | async-start | bytes 655360 | tf_op jit(solution)/shard_map/all_to_all | solution.py:54
  25.9 7.3 %collective-permute-start = (bf16[16,80,128]{2,1,0:T(8,128)(2,1)S(1)}, bf16[16,80,128]{2,1,0:T(8,128)(2,1)S(1)}, u32[]{:S(2)}, u32[]{:S(2)}) collective-permute-start(bf16[16,80,128]{2,1,0:T(8,128)(2,1)S(1)} %all-to-all-done), channel_id=1, source_target_pairs={{0,4},{4,0},{1,5},{5,1},{2,6},{6,2},{3,7},{7,3},{8,12},{12,8},{9,1... | collective-permute-start | bytes 983048 | tf_op jit(solution)/shard_map/ppermute | solution.py:50
  34.1 18.0 %collective-permute-start.3 = (bf16[2,16,80,128]{3,2,1,0:T(8,128)(2,1)}, bf16[2,16,80,128]{3,2,1,0:T(8,128)(2,1)S(1)}, u32[]{:S(2)}, u32[]{:S(2)}) collective-permute-start(bf16[2,16,80,128]{3,2,1,0:T(8,128)(2,1)} %get-tuple-element.111), channel_id=1, source_target_pairs={{0,1},{1,2},{2,3},{3,0},{4,5},{5,6},{6,7},{7,4},{8,9},{9,10},{10,1... | collective-permute-start | bytes 1966088 | tf_op jit(solution)/shard_map/ppermute | solution.py:46
  35.7 28.7 %collective-permute-start.2 = (bf16[2,16,80,128]{3,2,1,0:T(8,128)(2,1)}, bf16[2,16,80,128]{3,2,1,0:T(8,128)(2,1)}, u32[]{:S(2)}, u32[]{:S(2)}) collective-permute-start(bf16[2,16,80,128]{3,2,1,0:T(8,128)(2,1)} %get-tuple-element.111), channel_id=1, source_target_pairs={{0,2},{1,3},{2,0},{3,1},{4,6},{5,7},{6,4},{7,5},{8,10},{9,11},{10,... | collective-permute-start | bytes 1966088 | tf_op jit(solution)/shard_map/ppermute | solution.py:46
  38.6 25.8 %collective-permute-start.1 = (bf16[2,16,80,128]{3,2,1,0:T(8,128)(2,1)}, bf16[2,16,80,128]{3,2,1,0:T(8,128)(2,1)}, u32[]{:S(2)}, u32[]{:S(2)}) collective-permute-start(bf16[2,16,80,128]{3,2,1,0:T(8,128)(2,1)} %get-tuple-element.111), channel_id=1, source_target_pairs={{0,3},{1,0},{2,1},{3,2},{4,7},{5,4},{6,5},{7,6},{8,11},{9,8},{10,9... | collective-permute-start | bytes 1966088 | tf_op jit(solution)/shard_map/ppermute | solution.py:46
  40.0 31.2 %copy-start.19 = (f32[512]{0:T(512)}, f32[512]{0:T(512)S(1)}, u32[]{:S(2)}) copy-start(f32[512]{0:T(512)S(1)} %add_rsqrt_fusion) | copy-start | bytes 6148
  41.0 28.1 %collective-permute-start.4 = (bf16[2,16,80,128]{3,2,1,0:T(8,128)(2,1)}, bf16[2,16,80,128]{3,2,1,0:T(8,128)(2,1)}, u32[]{:S(2)}, u32[]{:S(2)}) collective-permute-start(bf16[2,16,80,128]{3,2,1,0:T(8,128)(2,1)} %get-tuple-element.111), channel_id=1, source_target_pairs={{0,8},{8,0},{1,9},{9,1},{2,10},{10,2},{3,11},{11,3},{4,12},{12,4},... | collective-permute-start | bytes 1966088 | tf_op jit(solution)/shard_map/ppermute | solution.py:50
  52.1 17.0 %collective-permute-start.7 = (bf16[2,16,80,128]{3,2,1,0:T(8,128)(2,1)S(1)}, bf16[2,16,80,128]{3,2,1,0:T(8,128)(2,1)}, u32[]{:S(2)}, u32[]{:S(2)}) collective-permute-start(bf16[2,16,80,128]{3,2,1,0:T(8,128)(2,1)S(1)} %collective-permute-done.3), channel_id=1, source_target_pairs={{0,8},{8,0},{1,9},{9,1},{2,10},{10,2},{3,11},{11,3},{4,12},{12,4},... | collective-permute-start | bytes 1966088 | tf_op jit(solution)/shard_map/ppermute | solution.py:50
  64.4 4.7 %collective-permute-start.6 = (bf16[2,16,80,128]{3,2,1,0:T(8,128)(2,1)}, bf16[2,16,80,128]{3,2,1,0:T(8,128)(2,1)}, u32[]{:S(2)}, u32[]{:S(2)}) collective-permute-start(bf16[2,16,80,128]{3,2,1,0:T(8,128)(2,1)} %collective-permute-done.2), channel_id=1, source_target_pairs={{0,8},{8,0},{1,9},{9,1},{2,10},{10,2},{3,11},{11,3},{4,12},{12,4},... | collective-permute-start | bytes 1966088 | tf_op jit(solution)/shard_map/ppermute | solution.py:50
  64.4 4.7 %collective-permute-start.5 = (bf16[2,16,80,128]{3,2,1,0:T(8,128)(2,1)}, bf16[2,16,80,128]{3,2,1,0:T(8,128)(2,1)}, u32[]{:S(2)}, u32[]{:S(2)}) collective-permute-start(bf16[2,16,80,128]{3,2,1,0:T(8,128)(2,1)} %collective-permute-done.1), channel_id=1, source_target_pairs={{0,8},{8,0},{1,9},{9,1},{2,10},{10,2},{3,11},{11,3},{4,12},{12,4},... | collective-permute-start | bytes 1966088 | tf_op jit(solution)/shard_map/ppermute | solution.py:50
  178.5 15.2 %copy-start.17 = (bf16[2,256,4,64]{1,3,2,0:T(8,128)(2,1)S(1)}, bf16[2,256,4,64]{1,3,2,0:T(8,128)(2,1)}, u32[]{:S(2)}) copy-start(bf16[2,256,4,64]{1,3,2,0:T(8,128)(2,1)} %fusion.44) | copy-start | bytes 786436
  196.3 14.8 %copy-start.6 = (bf16[32,8,2,256]{3,1,2,0:T(8,128)(2,1)}, bf16[32,8,2,256]{3,1,2,0:T(8,128)(2,1)S(1)}, u32[]{:S(2)}) copy-start(bf16[32,8,2,256]{3,1,2,0:T(8,128)(2,1)S(1)} %copy.115) | copy-start | bytes 786436
  291.8 2.2 collective-permute-start.9
  291.9 3.0 collective-permute-start.11
  292.4 3.5 collective-permute-start.13
  292.5 9.5 %collective-permute-start.8 = (bf16[2,16,80,128]{3,2,1,0:T(8,128)(2,1)S(1)}, bf16[2,16,80,128]{3,2,1,0:T(8,128)(2,1)S(1)}, u32[]{:S(2)}, u32[]{:S(2)}) collective-permute-start(bf16[2,16,80,128]{3,2,1,0:T(8,128)(2,1)S(1)} %get-tuple-element.97), channel_id=1, source_target_pairs={{0,8},{8,0},{1,9},{9,1},{2,10},{10,2},{3,11},{11,3},{4,12},{12,4},... | collective-permute-start | bytes 1966088 | tf_op jit(solution)/shard_map/ppermute | solution.py:50
  296.3 30.5 %collective-permute-start.14 = (bf16[2,16,80,128]{3,2,1,0:T(8,128)(2,1)S(1)}, bf16[2,16,80,128]{3,2,1,0:T(8,128)(2,1)S(1)}, u32[]{:S(2)}, u32[]{:S(2)}) collective-permute-start(bf16[2,16,80,128]{3,2,1,0:T(8,128)(2,1)S(1)} %get-tuple-element.103), channel_id=1, source_target_pairs={{0,3},{1,0},{2,1},{3,2},{4,7},{5,4},{6,5},{7,6},{8,11},{9,8},{10,9... | collective-permute-start | bytes 1966088 | tf_op jit(solution)/shard_map/ppermute | solution.py:46
  298.3 28.6 %collective-permute-start.12 = (bf16[2,16,80,128]{3,2,1,0:T(8,128)(2,1)S(1)}, bf16[2,16,80,128]{3,2,1,0:T(8,128)(2,1)S(1)}, u32[]{:S(2)}, u32[]{:S(2)}) collective-permute-start(bf16[2,16,80,128]{3,2,1,0:T(8,128)(2,1)S(1)} %get-tuple-element.102), channel_id=1, source_target_pairs={{0,2},{1,3},{2,0},{3,1},{4,6},{5,7},{6,4},{7,5},{8,10},{9,11},{10,... | collective-permute-start | bytes 1966088 | tf_op jit(solution)/shard_map/ppermute | solution.py:46
  299.4 31.1 %collective-permute-start.10 = (bf16[2,16,80,128]{3,2,1,0:T(8,128)(2,1)S(1)}, bf16[2,16,80,128]{3,2,1,0:T(8,128)(2,1)S(1)}, u32[]{:S(2)}, u32[]{:S(2)}) collective-permute-start(bf16[2,16,80,128]{3,2,1,0:T(8,128)(2,1)S(1)} %get-tuple-element.101), channel_id=1, source_target_pairs={{0,1},{1,2},{2,3},{3,0},{4,5},{5,6},{6,7},{7,4},{8,9},{9,10},{10,1... | collective-permute-start | bytes 1966088 | tf_op jit(solution)/shard_map/ppermute | solution.py:46
  300.7 31.0 %copy-start.3 = (bf16[512,1024]{1,0:T(8,128)(2,1)S(1)}, bf16[512,1024]{1,0:T(8,128)(2,1)}, u32[]{:S(2)}) copy-start(bf16[512,1024]{1,0:T(8,128)(2,1)} %param.14) | copy-start | bytes 3145732
  300.7 31.0 %copy-start.20 = (f32[512]{0:T(512)S(1)}, f32[512]{0:T(512)}, u32[]{:S(2)}) copy-start(f32[512]{0:T(512)} %copy-done.19) | copy-start | bytes 6148
  300.7 31.0 %copy-start.21 = (f32[1024]{0:T(1024)S(1)}, f32[1024]{0:T(1024)}, u32[]{:S(2)}) copy-start(f32[1024]{0:T(1024)} %param.15) | copy-start | bytes 12292
  331.0 9.7 %collective-permute-start.15 = (bf16[16,80,128]{2,1,0:T(8,128)(2,1)S(1)}, bf16[16,80,128]{2,1,0:T(8,128)(2,1)S(1)}, u32[]{:S(2)}, u32[]{:S(2)}) collective-permute-start(bf16[16,80,128]{2,1,0:T(8,128)(2,1)S(1)} %slice_bitcast_fusion.11), channel_id=1, source_target_pairs={{0,4},{4,0},{1,5},{5,1},{2,6},{6,2},{3,7},{7,3},{8,12},{12,8},{9,1... | collective-permute-start | bytes 983048 | tf_op jit(solution)/shard_map/ppermute | solution.py:50
  341.6 20.4 %all-to-all-start.1 = ((bf16[16,80,128]{2,1,0:T(8,128)(2,1)}), bf16[16,80,128]{2,1,0:T(8,128)(2,1)S(1)}, u32[]{:S(2)}, u32[]{:S(2)}) async-start(bf16[16,80,128]{2,1,0:T(8,128)(2,1)} %fusion.51), calls=%async_computation.1 | async-start | bytes 655360 | tf_op jit(solution)/shard_map/all_to_all | solution.py:72
  (24 other events, 119.8 us)

commit v2 on v1

v2 whole, which is shorter than its diff:
```python
import functools

import jax
import jax.numpy as jnp
import numpy as np
from jax import lax
from jax.experimental import pallas as pl
from jax.experimental.pallas import tpu as pltpu
from jax.sharding import PartitionSpec as P

HD = 64
HALF = 32
SEQ = 256
D = 1024
KV = 256
GROUP = 4
TOKENS = 512

AXES = ("xh", "z", "c", "xl", "y")
SIZES = (2, 8, 2, 2, 4)
CHIPS = 16
ROWS = 80
BF = jnp.bfloat16
F32 = jnp.float32
VMEM_BYTES = 48 * 1024 * 1024
BLOCKED = -1e30


def tables():
    frequency = 500000.0 ** (-2.0 * np.arange(HALF) / HD)
    angles = np.tile(np.arange(SEQ), TOKENS // SEQ)[None, :] * frequency[:, None]
    return np.stack([np.cos(angles), np.sin(angles)]).astype(np.float32)


def dot(left, right):
    return jnp.dot(left, right, preferred_element_type=F32)


def shift(block, axis, size, step):
    return lax.ppermute(block, axis, [(i, (i - step) % size) for i in range(size)])


def swap(block, axis):
    return lax.ppermute(block, axis, [(0, 1), (1, 0)])


def gather_blocks(block):
    mine = lax.all_to_all(
        jnp.broadcast_to(block[None], (CHIPS, ROWS, 128)), ("xh", "z"), 0, 0, tiled=True
    )
    own = jnp.stack([mine, swap(mine, "xl")])
    pieces = [own, shift(own, "y", 4, 1), shift(own, "y", 4, 2), shift(own, "y", 4, 3)]
    return pieces + [swap(piece, "c") for piece in pieces]


def scatter_blocks(pieces):
    summed = []
    for step in range(4):
        arrived = swap(pieces[4 + step], "c")
        summed.append((pieces[step].astype(F32) + arrived.astype(F32)).astype(BF))
    total = summed[0].astype(F32)
    for step in (1, 2, 3):
        total = total + shift(summed[step], "y", 4, -step).astype(F32)
    total = total.astype(BF)
    pair = (total[0].astype(F32) + swap(total[1], "xl").astype(F32)).astype(BF)
    parts = lax.all_to_all(pair, ("xh", "z"), 0, 0, tiled=True)
    return jnp.sum(parts.astype(F32), axis=0)


def assembly(where, pieces, w_q, w_kv, w_o, sems):
    c, xl, y = where[0], where[1], where[2]
    copies = ([], [], [])
    for at in range(16):
        c_rel, y_rel, xl_rel = at // 8, (at // 2) % 4, at % 2
        source = pieces[c_rel * 4 + y_rel].at[xl_rel]
        core = lax.rem(c + c_rel, 2)
        node = lax.rem(xl + xl_rel, 2) * 4 + lax.rem(y + y_rel, 4)
        lanes = pl.ds(pl.multiple_of(node * 128, 128), 128)
        for part, (target, start, count) in enumerate(
            ((w_q, 0, 32), (w_kv, 32, 16), (w_o, 48, 32))
        ):
            copies[part].append(
                pltpu.make_async_copy(
                    source.at[:, pl.ds(start, count), :],
                    target.at[:, core, :, lanes],
                    sems.at[part, at],
                )
            )
    return copies


def begin(copies):
    for copy in copies:
        copy.start()


def finish(copies):
    for copy in copies:
        copy.wait()


def unit(rows):
    inverse = lax.rsqrt(jnp.mean(rows * rows, axis=-1, keepdims=True) + 1e-05)
    return rows * inverse, inverse


def attend(where, docs, gain, hidden, cot, table, *rest):
    pieces, rest = rest[:8], rest[8:]
    grads, (mix, dq_t, dkv_t), rest = rest[:8], rest[8:11], rest[11:]
    (w_q, w_kv, w_o, normed, normed_t, cot_t, dm_t, q_t, k_t, v_t, k_n, v_n) = rest[:12]
    (mix_t, dk_t, dv_t, bias, out, sems, out_sems) = rest[12:]
    copy_q, copy_kv, copy_o = assembly(where, pieces, w_q, w_kv, w_o, sems)
    begin(copy_o)
    begin(copy_q)
    begin(copy_kv)

    @pl.loop(0, TOKENS // 128)
    def _(step):
        at = pl.ds(pl.multiple_of(step * 128, 128), 128)
        value = (unit(hidden[at, :].astype(F32))[0] * gain[...]).astype(BF)
        normed[at, :] = value
        normed_t[:, at] = value.T
        cot_t[:, at] = cot[at, :].T

    for b in range(TOKENS // SEQ):
        places_q = lax.broadcasted_iota(jnp.int32, (1, SEQ), 1)
        places_s = lax.broadcasted_iota(jnp.int32, (SEQ, 1), 0)
        doc_q, doc_s, bound = jnp.zeros_like(places_q), jnp.zeros_like(places_s), 0
        for j in range(4):
            bound = bound + docs[b, j]
            doc_q = doc_q + (places_q >= bound).astype(jnp.int32)
            doc_s = doc_s + (places_s >= bound).astype(jnp.int32)
        allowed = jnp.logical_and(doc_q == doc_s, places_s <= places_q)
        bias[b] = jnp.where(allowed, 0.0, BLOCKED)

    finish(copy_o)
    for n in range(4):
        columns = w_o[:, :, :, pl.ds(n * 256, 256)].reshape(D, 256)
        dm_t[pl.ds(n * 256, 256), :] = dot(cot[...], columns).astype(BF).T

    cos, sin = table[0], table[1]
    finish(copy_q)
    for n in range(4):
        rows = w_q[pl.ds(n * 4, 4)].reshape(256, D)
        value = dot(rows, normed_t[...]) * 0.125
        for h in range(4):
            a, b = value[h * HD : h * HD + HALF], value[h * HD + HALF : (h + 1) * HD]
            q_t[pl.ds(n * 256 + h * HD, HALF), :] = (a * cos - b * sin).astype(BF)
            q_t[pl.ds(n * 256 + h * HD + HALF, HALF), :] = (a * sin + b * cos).astype(BF)
    finish(copy_kv)
    for n in range(4):
        rows = w_kv[pl.ds(n * 4, 4)].reshape(128, D)
        value = dot(rows, normed_t[...]).reshape(8, 2, 8, TOKENS)
        keys = value[:, 0].reshape(HD, TOKENS)
        a, b = keys[:HALF], keys[HALF:]
        keys = jnp.concatenate([a * cos - b * sin, a * sin + b * cos]).astype(BF)
        values = value[:, 1].reshape(HD, TOKENS).astype(BF)
        k_t[n] = keys
        v_t[n] = values
        k_n[n] = keys.T
        v_n[n] = values.T

    @pl.loop(0, 8)
    def _(step):
        head = lax.rem(step, 4)
        b = step // 4
        at = pl.ds(pl.multiple_of(b * SEQ, SEQ), SEQ)
        keys_n, values_n = k_n[head, at, :], v_n[head, at, :]
        keys_t, values_t = k_t[head, :, at], v_t[head, :, at]
        cos_b, sin_b = table[0, :, 0:SEQ] * 0.125, table[1, :, 0:SEQ] * 0.125
        d_keys = jnp.zeros((SEQ, HD), F32)
        d_values = jnp.zeros((SEQ, HD), F32)
        blank = jnp.zeros((128, 128), BF)
        for h in range(GROUP):
            rows = pl.ds(pl.multiple_of(head * 256 + h * HD, HD), HD)
            query = q_t[rows, at]
            d_mixed = dm_t[rows, at]
            scores = dot(keys_n, query)
            d_prob = dot(values_n, d_mixed)
            probs, d_scores = [], []
            for length, columns in ((128, slice(0, 128)), (256, slice(128, 256))):
                weight = jnp.exp(scores[:length, columns] + bias[b, pl.ds(0, length), columns])
                prob = weight * (1.0 / jnp.sum(weight, axis=0, keepdims=True))
                back = d_prob[:length, columns]
                inner = jnp.sum(prob * back, axis=0, keepdims=True)
                probs.append(prob.astype(BF))
                d_scores.append((prob * (back - inner)).astype(BF))
            prob = jnp.concatenate([jnp.concatenate([probs[0], blank]), probs[1]], axis=1)
            d_score = jnp.concatenate([jnp.concatenate([d_scores[0], blank]), d_scores[1]], axis=1)
            mix_t[rows, at] = dot(values_t, prob).astype(BF)
            value = dot(keys_t, d_score)
            a, c = value[:HALF], value[HALF:]
            dq_t[rows, at] = jnp.concatenate(
                [a * cos_b + c * sin_b, c * cos_b - a * sin_b]
            ).astype(BF)
            d_keys = d_keys + dot(d_score, query.T)
            d_values = d_values + dot(prob, d_mixed.T)
        value = d_keys.T
        a, c = value[:HALF], value[HALF:]
        cos_b, sin_b = table[0, :, 0:SEQ], table[1, :, 0:SEQ]
        dk_t[head, :, at] = jnp.concatenate([a * cos_b + c * sin_b, c * cos_b - a * sin_b])
        dv_t[head, :, at] = d_values.T

    for n in range(4):
        keys = dk_t[n].reshape(8, 1, 8, TOKENS)
        values = dv_t[n].reshape(8, 1, 8, TOKENS)
        both = jnp.concatenate([keys, values], axis=1).reshape(128, TOKENS)
        dkv_t[pl.ds(n * 128, 128), :] = both.astype(BF)
        mix[:, pl.ds(n * 256, 256)] = mix_t[pl.ds(n * 256, 256), :].T

    c, xl, y = where[0], where[1], where[2]
    for n in range(4):
        lanes = pl.ds(n * 256, 256)
        places = []
        for node in (2 * n, 2 * n + 1):
            places.append((lax.rem(node % 4 - y + 4, 4), lax.rem(node // 4 - xl + 2, 2)))
        for left, right, start, count in (
            (dq_t, normed, 0, 32),
            (dkv_t, normed, 32, 16),
            (cot_t, mix, 48, 32),
        ):
            size = left.shape[0] // 2
            for half in range(2):
                value = dot(left[pl.ds(half * size, size), :], right[:, lanes]).astype(BF)
                value = value.reshape(8, 2, count, 256)
                for core in range(2):
                    c_rel = lax.rem(core - c + 2, 2)
                    for i, (y_rel, xl_rel) in enumerate(places):
                        out[c_rel, y_rel, xl_rel, pl.ds(half * 8, 8), pl.ds(start, count), :] = (
                            value[:, core, :, i * 128 : (i + 1) * 128]
                        )
    copies = [
        pltpu.make_async_copy(out.at[at // 4, at % 4], grads[at], out_sems.at[at])
        for at in range(8)
    ]
    begin(copies)
    finish(copies)


def close(where, gain, hidden, cot, mix, dq_t, dkv_t, *rest):
    pieces, (output, grad_hidden), rest = rest[:8], rest[8:10], rest[10:]
    w_q, w_kv, w_o, dq, dkv, d_normed, sems = rest
    copy_q, copy_kv, copy_o = assembly(where, pieces, w_q, w_kv, w_o, sems)
    begin(copy_o)
    begin(copy_q)
    begin(copy_kv)
    for n in range(4):
        dq[:, pl.ds(n * 256, 256)] = dq_t[pl.ds(n * 256, 256), :].T
        dkv[:, pl.ds(n * 128, 128)] = dkv_t[pl.ds(n * 128, 128), :].T
    finish(copy_o)
    for n in range(4):
        lanes = pl.ds(n * 256, 256)
        rows = w_o[pl.ds(n * 4, 4)].reshape(256, D)
        value = lax.dot_general(
            mix[...], rows, (((1,), (1,)), ((), ())), preferred_element_type=F32
        )
        output[:, lanes] = (hidden[:, lanes].astype(F32) + value).astype(BF)
    finish(copy_q)
    finish(copy_kv)
    for n in range(4):
        lanes = pl.ds(n * 256, 256)
        value = dot(dq[...], w_q[:, :, :, lanes].reshape(D, 256))
        d_normed[:, lanes] = value + dot(dkv[...], w_kv[:, :, :, lanes].reshape(2 * KV, 256))

    @pl.loop(0, TOKENS // 64)
    def _(step):
        at = pl.ds(pl.multiple_of(step * 64, 64), 64)
        unit_rows, inverse = unit(hidden[at, :].astype(F32))
        d_unit = d_normed[at, :] * gain[...]
        middle = jnp.mean(d_unit * unit_rows, axis=-1, keepdims=True)
        grad_hidden[at, :] = (
            cot[at, :].astype(F32) + inverse * (d_unit - unit_rows * middle)
        ).astype(BF)


SMEM = pl.BlockSpec(memory_space=pltpu.SMEM)
VMEM = pl.BlockSpec(memory_space=pltpu.VMEM)
ANY = pl.BlockSpec(memory_space=pl.ANY)
PIECE = jax.ShapeDtypeStruct((2, CHIPS, ROWS, 128), BF)


def scratch(*shape, dtype=BF):
    return pltpu.VMEM(shape, dtype)


def weights_scratch():
    return [
        scratch(CHIPS, 2, 32, D),
        scratch(CHIPS, 2, 16, D),
        scratch(CHIPS, 2, 32, D),
    ]


def local(hidden, norm_gain, w_query, w_key, w_value, w_out, doc_lengths, cotangent):
    block = jnp.concatenate([w_query.T, w_key.T, w_value.T, w_out.T], axis=0)
    pieces = gather_blocks(block)
    where = jnp.stack([lax.axis_index(name) for name in ("c", "xl", "y")])
    gain = norm_gain.reshape(1, D)
    table = jnp.asarray(tables())
    shapes = [
        jax.ShapeDtypeStruct((TOKENS, D), BF),
        jax.ShapeDtypeStruct((D, TOKENS), BF),
        jax.ShapeDtypeStruct((2 * KV, TOKENS), BF),
    ]
    results = pl.pallas_call(
        attend,
        name="attend",
        out_shape=[PIECE] * 8 + shapes,
        in_specs=[SMEM, SMEM] + [VMEM] * 4 + [ANY] * 8,
        out_specs=[ANY] * 8 + [VMEM] * 3,
        scratch_shapes=weights_scratch()
        + [
            scratch(TOKENS, D),
            scratch(D, TOKENS),
            scratch(D, TOKENS),
            scratch(D, TOKENS),
            scratch(D, TOKENS),
            scratch(4, HD, TOKENS),
            scratch(4, HD, TOKENS),
            scratch(4, TOKENS, HD),
            scratch(4, TOKENS, HD),
            scratch(D, TOKENS),
            scratch(4, HD, TOKENS, dtype=F32),
            scratch(4, HD, TOKENS, dtype=F32),
            scratch(2, SEQ, SEQ, dtype=F32),
            scratch(2, 4, 2, CHIPS, ROWS, 128),
            pltpu.SemaphoreType.DMA((3, 16)),
            pltpu.SemaphoreType.DMA((8,)),
        ],
        compiler_params=pltpu.CompilerParams(vmem_limit_bytes=VMEM_BYTES),
        cost_estimate=pl.CostEstimate(
            flops=7 * 10**9, bytes_accessed=20 * 10**6, transcendentals=2 * 10**6
        ),
    )(where, doc_lengths, gain, hidden, cotangent, table, *pieces)
    grads, (mix, dq_t, dkv_t) = results[:8], results[8:]
    output, grad_hidden = pl.pallas_call(
        close,
        name="close",
        out_shape=[jax.ShapeDtypeStruct((TOKENS, D), BF)] * 2,
        in_specs=[SMEM] + [VMEM] * 6 + [ANY] * 8,
        out_specs=[VMEM] * 2,
        scratch_shapes=weights_scratch()
        + [
            scratch(TOKENS, D),
            scratch(TOKENS, 2 * KV),
            scratch(TOKENS, D, dtype=F32),
            pltpu.SemaphoreType.DMA((3, 16)),
        ],
        compiler_params=pltpu.CompilerParams(vmem_limit_bytes=VMEM_BYTES),
        cost_estimate=pl.CostEstimate(
            flops=3 * 10**9, bytes_accessed=15 * 10**6, transcendentals=0
        ),
    )(where, gain, hidden, cotangent, mix, dq_t, dkv_t, *pieces)
    owned = scatter_blocks(grads)
    return (
        output,
        grad_hidden,
        owned[:32].T,
        owned[32:40].T,
        owned[40:48].T,
        owned[48:].T,
    )


def solution(mesh):
    wide = jax.sharding.Mesh(mesh.devices.reshape(SIZES), AXES)
    dp, node = ("xh", "z", "c"), ("xl", "y")
    tokens, weight = P(AXES, None), P(node, dp)
    return jax.shard_map(
        local,
        mesh=wide,
        in_specs=(tokens, P(), weight, weight, weight, weight, tokens, tokens),
        out_specs=(tokens, tokens, weight, weight, weight, weight),
        check_vma=False,
    )
```

time: 369 us -> 162 us (0.44); the launches traced: 363 us -> 160 us
  local copies, waits for them, and re-layouts: 118 us -> 2.38 us
  other arithmetic: 65.3 us -> 3.66 us
  matrix products: 59.8 us -> 0 us
  Pallas kernels: 0 us -> 36.8 us
  blocking collectives: 0 us -> 23.7 us
  starting transfers between devices: 32.5 us -> 19.1 us
  waiting for transfers between devices: 86.1 us -> 74 us
    dot_general x18 -> x0, matrix products: 59.8 us -> none  [the longest x1 14.6 us: local(): jnp.einsum('bkgqs,bskd->bqkgd', d_score, key_rot, preferred_element_type=...]
    another operation x22 -> x0, local copies, waits for them, and re-layouts: 51.2 us -> none  [the longest x6 16.2 us: whole(): every = jnp.take(every, (jnp.arange(2) - c) % 2, axis=0)]
    pallas_call x0 -> x2, Pallas kernels: none -> 36.8 us  [the longest x1 26.5 us: local(): pl.pallas_call(attend, name='attend', out_shape=[PIECE] * 8 + shapes, in_...]
    select_n x6 -> x0, other arithmetic: 24.8 us -> none  [the longest x2 5.45 us: spread(): every = jnp.take(every, (jnp.arange(4) + y) % 4, axis=1)]
    all_to_all x0 -> x1, blocking collectives: none -> 23.7 us  [gather_blocks(): lax.all_to_all(jnp.broadcast_to(block[None], (CHIPS, ROWS, 128)), ('xh',...]
    transpose x2 -> x0, other arithmetic: 19.9 us -> none  [the longest x1 16.8 us: spread(): every = every.reshape(2, 4, 128, 16, 2, 80).transpose(4, 1, 0, 3, 5, 2)]
    gather x10 -> x0, local copies, waits for them, and re-layouts: 17 us -> none  [the longest x1 6.09 us: whole(): every = jnp.take(every, (jnp.arange(4) - y) % 4, axis=1)]
    concatenate x4 -> x0, local copies, waits for them, and re-layouts: 12.3 us -> none  [spread(): jnp.concatenate([term.astype(jnp.bfloat16).reshape(1024, 32, -1) for term...]
  transfers between devices with their start and end apart: 18 -> 17, of which waited for: 11 -> 10; matrix products, arithmetic and copies ran while one was open for 4% -> 0% of each run, Pallas kernels for 0% -> 6%
where the time goes in v2:
time: 162 us; the launch traced here: 160 us
  waiting for transfers between devices  74 us (46%)
  Pallas kernels  36.8 us (23%)
  blocking collectives  23.7 us (15%)
  starting transfers between devices  19.1 us (12%)
  other arithmetic  3.66 us (2%)
  local copies, waits for them, and re-layouts  2.38 us (1%)
    ppermute x6, waiting for transfers between devices, shift(): lax.ppermute(block, axis, [(i, (i - step) % size) for i in range(size)])  55.4 us
    pallas_call x1, Pallas kernels, local(): pl.pallas_call(attend, name='attend', out_shape=[PIECE] * 8 + shapes, in_...  26.5 us
    all_to_all x1, blocking collectives, gather_blocks(): lax.all_to_all(jnp.broadcast_to(block[None], (CHIPS, ROWS, 128)), ('xh',...  23.7 us
    ppermute x10, waiting for transfers between devices, swap(): return lax.ppermute(block, axis, [(0, 1), (1, 0)])  18.6 us
    pallas_call x1, Pallas kernels, local(): pl.pallas_call(close, name='close', out_shape=[jax.ShapeDtypeStruct((TOKE...  10.3 us
    all_to_all x1, starting transfers between devices, scatter_blocks(): parts = lax.all_to_all(pair, ('xh', 'z'), 0, 0, tiled=True)  8.35 us
    ppermute x6, starting transfers between devices, shift(): lax.ppermute(block, axis, [(i, (i - step) % size) for i in range(size)])  7.81 us
  transfers between devices with their start and end apart: 17, of which 10 were waited for; matrix products, arithmetic and copies ran while one was open for 0% of the time, Pallas kernels for 6%

profile of v2, /device:TPU:32, one launch (start us, length us, event | category | flops | bytes accessed | tf_op | source)
XLA Modules:
  0.0 160.5 jit_solution(2640111594958053180)
XLA Ops:
  0.6 0.8 pad_maximum_fusion.1
  1.5 23.7 %all_to_all.10 = bf16[16,80,128]{2,1,0:T(8,128)(2,1)S(1)} all-to-all(bf16[16,80,128]{2,1,0:T(8,128)(2,1)S(1)} %broadcast_in_dim.2), channel_id=1, replica_groups=mesh['xh'=2,'z'=8,'c'=2,'xl'=2,'y'=4] {'xh','z'}, dimensions={0} | all-to-all | bytes 655360 | tf_op jit(solution)/shard_map/all_to_all | solution.py:48
  25.7 6.7 %collective-permute-done = bf16[16,80,128]{2,1,0:T(8,128)(2,1)S(1)} collective-permute-done((bf16[16,80,128]{2,1,0:T(8,128)(2,1)S(1)}, bf16[16,80,128]{2,1,0:T(8,128)(2,1)S(1)}, u32[]{:S(2)}, u32[]{:S(2)}) %collective-permute-start) | collective-permute-done | bytes 327712 | tf_op jit(solution)/shard_map/ppermute | solution.py:44
  32.5 3.1 %collective-permute-start.1 = (bf16[2,16,80,128]{3,2,1,0:T(8,128)(2,1)S(1)}, bf16[2,16,80,128]{3,2,1,0:T(8,128)(2,1)S(1)}, u32[]{:S(2)}, u32[]{:S(2)}) collective-permute-start(bf16[2,16,80,128]{3,2,1,0:T(8,128)(2,1)S(1)} %pad_maximum_fusion.rest_0_), channel_id=1, source_target_pairs={{0,3},{1,0},{2,1},{3,2},{4,7},{5,4},{6,5},{7,6},{8,11},{9,8},{10,9... | collective-permute-start | bytes 1966088 | tf_op jit(solution)/shard_map/ppermute | solution.py:40
  35.6 0.6 collective-permute-start.2
  36.3 1.0 collective-permute-start.3
  37.2 23.4 %collective-permute-done.1.rest_1_ = bf16[2,16,80,128]{3,2,1,0:T(8,128)(2,1)S(1)} collective-permute-done((bf16[2,16,80,128]{3,2,1,0:T(8,128)(2,1)S(1)}, bf16[2,16,80,128]{3,2,1,0:T(8,128)(2,1)S(1)}, u32[]{:S(2)}, u32[]{:S(2)}) %collective-permute-start.1) | collective-permute-done | bytes 655392 | tf_op jit(solution)/shard_map/ppermute | solution.py:40
  61.1 3.2 %collective-permute-done.3.rest_3_ = bf16[2,16,80,128]{3,2,1,0:T(8,128)(2,1)S(1)} collective-permute-done((bf16[2,16,80,128]{3,2,1,0:T(8,128)(2,1)S(1)}, bf16[2,16,80,128]{3,2,1,0:T(8,128)(2,1)S(1)}, u32[]{:S(2)}, u32[]{:S(2)}) %collective-permute-start.3) | collective-permute-done | bytes 655392 | tf_op jit(solution)/shard_map/ppermute | solution.py:40
  64.4 2.1 %collective-permute-done.7.rest_7_ = bf16[2,16,80,128]{3,2,1,0:T(8,128)(2,1)} collective-permute-done((bf16[2,16,80,128]{3,2,1,0:T(8,128)(2,1)S(1)}, bf16[2,16,80,128]{3,2,1,0:T(8,128)(2,1)}, u32[]{:S(2)}, u32[]{:S(2)}) %collective-permute-start.7) | collective-permute-done | bytes 655392 | tf_op jit(solution)/shard_map/ppermute | solution.py:44
  66.6 26.5 %attend.1 = (bf16[2,16,80,128]{3,2,1,0:T(8,128)(2,1)S(1)}, bf16[2,16,80,128]{3,2,1,0:T(8,128)(2,1)S(1)}, bf16[2,16,80,128]{3,2,1,0:T(8,128)(2,1)S(1)}, bf16[2,16...) custom-call(s32[3]{0:T(128)S(1)} %pad_add_fusion.where, ...), custom_call_target="tpu_custom_call" | custom-call | flops 7000000000 | bytes 20000000 | tf_op jit(solution)/shard_map/attend/pallas_call | solution.py:305
  94.2 1.1 collective-permute-done.9
  95.6 0.7 collective-permute-done.11
  96.4 2.7 %collective-permute-start.12 = (bf16[2,16,80,128]{3,2,1,0:T(8,128)(2,1)S(1)}, bf16[2,16,80,128]{3,2,1,0:T(8,128)(2,1)S(1)}, u32[]{:S(2)}, u32[]{:S(2)}) collective-permute-start(bf16[2,16,80,128]{3,2,1,0:T(8,128)(2,1)S(1)} %add_convert_fusion.2), channel_id=1, source_target_pairs={{0,2},{1,3},{2,0},{3,1},{4,6},{5,7},{6,4},{7,5},{8,10},{9,11},{10,... | collective-permute-start | bytes 1966088 | tf_op jit(solution)/shard_map/ppermute | solution.py:40
  99.7 14.6 %collective-permute-done.10 = bf16[2,16,80,128]{3,2,1,0:T(8,128)(2,1)S(1)} collective-permute-done((bf16[2,16,80,128]{3,2,1,0:T(8,128)(2,1)S(1)}, bf16[2,16,80,128]{3,2,1,0:T(8,128)(2,1)S(1)}, u32[]{:S(2)}, u32[]{:S(2)}) %collective-permute-start.10) | collective-permute-done | bytes 655392 | tf_op jit(solution)/shard_map/ppermute | solution.py:40
  114.2 13.4 %collective-permute-done.12 = bf16[2,16,80,128]{3,2,1,0:T(8,128)(2,1)S(1)} collective-permute-done((bf16[2,16,80,128]{3,2,1,0:T(8,128)(2,1)S(1)}, bf16[2,16,80,128]{3,2,1,0:T(8,128)(2,1)S(1)}, u32[]{:S(2)}, u32[]{:S(2)}) %collective-permute-start.12) | collective-permute-done | bytes 655392 | tf_op jit(solution)/shard_map/ppermute | solution.py:40
  127.7 0.8 collective-permute-done.14
  129.0 0.7 collective-permute-start.15
  129.6 8.0 %collective-permute-done.15 = bf16[16,80,128]{2,1,0:T(8,128)(2,1)S(1)} collective-permute-done((bf16[16,80,128]{2,1,0:T(8,128)(2,1)S(1)}, bf16[16,80,128]{2,1,0:T(8,128)(2,1)S(1)}, u32[]{:S(2)}, u32[]{:S(2)}) %collective-permute-start.15) | collective-permute-done | bytes 327712 | tf_op jit(solution)/shard_map/ppermute | solution.py:44
  137.7 0.8 fusion
  138.5 8.3 %all-to-all-start.1 = ((bf16[16,80,128]{2,1,0:T(8,128)(2,1)}), bf16[16,80,128]{2,1,0:T(8,128)(2,1)}, u32[]{:S(2)}, u32[]{:S(2)}) async-start(bf16[16,80,128]{2,1,0:T(8,128)(2,1)} %fusion), calls=%async_computation.1 | async-start | bytes 655360 | tf_op jit(solution)/shard_map/all_to_all | solution.py:66
  146.9 1.0 copy-done.14
  147.9 10.3 %close.1 = (bf16[512,1024]{1,0:T(8,128)(2,1)}, bf16[512,1024]{1,0:T(8,128)(2,1)}) custom-call(s32[3]{0:T(128)S(1)} %pad_add_fusion.where, f32[1,1024]{1,0:T(1,128)S(1)} %bitcast.26, bf16[512,1024]{1,0:T(8,128)(2,1)} %hidden.3, bf16[512,1024]{1,0:T(8,128)(2,1)} %cot.3, bf16[512,1024]{1,0:T(8,128)(2,1)} %get-tuple-element.19.mix, ...), custom_call_target="tpu_custom_call" | custom-call | flops 3000000000 | bytes 15000000 | tf_op jit(solution)/shard_map/close/pallas_call | solution.py:336
  158.2 1.0 convert_reduce_fusion
  159.3 0.6 slice_bitcast_fusion.2
  (56 shorter events, 4.5 us)
Async XLA Ops:
  1.4 65.2 %copy-start.10 = (f32[1024]{0:T(1024)S(1)}, f32[1024]{0:T(1024)}, u32[]{:S(2)}) copy-start(f32[1024]{0:T(1024)} %param.10) | copy-start | bytes 12292
  1.4 65.2 %copy-start.11 = (s32[2,4]{1,0:T(2,128)S(1)}, s32[2,4]{1,0:T(2,128)}, u32[]{:S(2)}) copy-start(s32[2,4]{1,0:T(2,128)} %docs.1) | copy-start | bytes 100
  1.5 65.2 %copy-start.12 = (f32[2,32,512]{2,1,0:T(8,128)S(1)}, f32[2,32,512]{2,1,0:T(8,128)}, u32[]{:S(2)}) copy-start(f32[2,32,512]{2,1,0:T(8,128)} %constant.16.clone.table) | copy-start | bytes 393220
  25.1 7.3 %collective-permute-start = (bf16[16,80,128]{2,1,0:T(8,128)(2,1)S(1)}, bf16[16,80,128]{2,1,0:T(8,128)(2,1)S(1)}, u32[]{:S(2)}, u32[]{:S(2)}) collective-permute-start(bf16[16,80,128]{2,1,0:T(8,128)(2,1)S(1)} %all_to_all.10), channel_id=1, source_target_pairs={{0,4},{4,0},{1,5},{5,1},{2,6},{6,2},{3,7},{7,3},{8,12},{12,8},{9,1... | collective-permute-start | bytes 983048 | tf_op jit(solution)/shard_map/ppermute | solution.py:44
  32.5 34.0 %copy-start = (bf16[2,16,80,128]{3,2,1,0:T(8,128)(2,1)}, bf16[2,16,80,128]{3,2,1,0:T(8,128)(2,1)S(1)}, u32[]{:S(2)}) copy-start(bf16[2,16,80,128]{3,2,1,0:T(8,128)(2,1)S(1)} %pad_maximum_fusion.rest_0_) | copy-start | bytes 1966084
  32.5 28.1 %collective-permute-start.1 = (bf16[2,16,80,128]{3,2,1,0:T(8,128)(2,1)S(1)}, bf16[2,16,80,128]{3,2,1,0:T(8,128)(2,1)S(1)}, u32[]{:S(2)}, u32[]{:S(2)}) collective-permute-start(bf16[2,16,80,128]{3,2,1,0:T(8,128)(2,1)S(1)} %pad_maximum_fusion.rest_0_), channel_id=1, source_target_pairs={{0,3},{1,0},{2,1},{3,2},{4,7},{5,4},{6,5},{7,6},{8,11},{9,8},{10,9... | collective-permute-start | bytes 1966088 | tf_op jit(solution)/shard_map/ppermute | solution.py:40
  35.6 25.0 %collective-permute-start.2 = (bf16[2,16,80,128]{3,2,1,0:T(8,128)(2,1)S(1)}, bf16[2,16,80,128]{3,2,1,0:T(8,128)(2,1)S(1)}, u32[]{:S(2)}, u32[]{:S(2)}) collective-permute-start(bf16[2,16,80,128]{3,2,1,0:T(8,128)(2,1)S(1)} %pad_maximum_fusion.rest_0_), channel_id=1, source_target_pairs={{0,2},{1,3},{2,0},{3,1},{4,6},{5,7},{6,4},{7,5},{8,10},{9,11},{10,... | collective-permute-start | bytes 1966088 | tf_op jit(solution)/shard_map/ppermute | solution.py:40
  36.3 28.1 %collective-permute-start.3 = (bf16[2,16,80,128]{3,2,1,0:T(8,128)(2,1)S(1)}, bf16[2,16,80,128]{3,2,1,0:T(8,128)(2,1)S(1)}, u32[]{:S(2)}, u32[]{:S(2)}) collective-permute-start(bf16[2,16,80,128]{3,2,1,0:T(8,128)(2,1)S(1)} %pad_maximum_fusion.rest_0_), channel_id=1, source_target_pairs={{0,1},{1,2},{2,3},{3,0},{4,5},{5,6},{6,7},{7,4},{8,9},{9,10},{10,1... | collective-permute-start | bytes 1966088 | tf_op jit(solution)/shard_map/ppermute | solution.py:40
  37.2 27.2 %collective-permute-start.4 = (bf16[2,16,80,128]{3,2,1,0:T(8,128)(2,1)S(1)}, bf16[2,16,80,128]{3,2,1,0:T(8,128)(2,1)S(1)}, u32[]{:S(2)}, u32[]{:S(2)}) collective-permute-start(bf16[2,16,80,128]{3,2,1,0:T(8,128)(2,1)S(1)} %pad_maximum_fusion.rest_0_), channel_id=1, source_target_pairs={{0,8},{8,0},{1,9},{9,1},{2,10},{10,2},{3,11},{11,3},{4,12},{12,4},... | collective-permute-start | bytes 1966088 | tf_op jit(solution)/shard_map/ppermute | solution.py:44
  60.6 3.8 %collective-permute-start.5 = (bf16[2,16,80,128]{3,2,1,0:T(8,128)(2,1)S(1)}, bf16[2,16,80,128]{3,2,1,0:T(8,128)(2,1)}, u32[]{:S(2)}, u32[]{:S(2)}) collective-permute-start(bf16[2,16,80,128]{3,2,1,0:T(8,128)(2,1)S(1)} %collective-permute-done.1.rest_1_), channel_id=1, source_target_pairs={{0,8},{8,0},{1,9},{9,1},{2,10},{10,2},{3,11},{11,3},{4,12},{12,4},... | collective-permute-start | bytes 1966088 | tf_op jit(solution)/shard_map/ppermute | solution.py:44
  60.6 3.8 %collective-permute-start.6 = (bf16[2,16,80,128]{3,2,1,0:T(8,128)(2,1)S(1)}, bf16[2,16,80,128]{3,2,1,0:T(8,128)(2,1)}, u32[]{:S(2)}, u32[]{:S(2)}) collective-permute-start(bf16[2,16,80,128]{3,2,1,0:T(8,128)(2,1)S(1)} %collective-permute-done.2.rest_2_), channel_id=1, source_target_pairs={{0,8},{8,0},{1,9},{9,1},{2,10},{10,2},{3,11},{11,3},{4,12},{12,4},... | collective-permute-start | bytes 1966088 | tf_op jit(solution)/shard_map/ppermute | solution.py:44
  64.3 2.2 %collective-permute-start.7 = (bf16[2,16,80,128]{3,2,1,0:T(8,128)(2,1)S(1)}, bf16[2,16,80,128]{3,2,1,0:T(8,128)(2,1)}, u32[]{:S(2)}, u32[]{:S(2)}) collective-permute-start(bf16[2,16,80,128]{3,2,1,0:T(8,128)(2,1)S(1)} %collective-permute-done.3.rest_3_), channel_id=1, source_target_pairs={{0,8},{8,0},{1,9},{9,1},{2,10},{10,2},{3,11},{11,3},{4,12},{12,4},... | collective-permute-start | bytes 1966088 | tf_op jit(solution)/shard_map/ppermute | solution.py:44
  93.1 2.2 %collective-permute-start.9 = (bf16[2,16,80,128]{3,2,1,0:T(8,128)(2,1)S(1)}, bf16[2,16,80,128]{3,2,1,0:T(8,128)(2,1)S(1)}, u32[]{:S(2)}, u32[]{:S(2)}) collective-permute-start(bf16[2,16,80,128]{3,2,1,0:T(8,128)(2,1)S(1)} %get-tuple-element.27), channel_id=1, source_target_pairs={{0,8},{8,0},{1,9},{9,1},{2,10},{10,2},{3,11},{11,3},{4,12},{12,4},... | collective-permute-start | bytes 1966088 | tf_op jit(solution)/shard_map/ppermute | solution.py:44
  93.3 2.9 %collective-permute-start.11 = (bf16[2,16,80,128]{3,2,1,0:T(8,128)(2,1)S(1)}, bf16[2,16,80,128]{3,2,1,0:T(8,128)(2,1)S(1)}, u32[]{:S(2)}, u32[]{:S(2)}) collective-permute-start(bf16[2,16,80,128]{3,2,1,0:T(8,128)(2,1)S(1)} %get-tuple-element.29), channel_id=1, source_target_pairs={{0,8},{8,0},{1,9},{9,1},{2,10},{10,2},{3,11},{11,3},{4,12},{12,4},... | collective-permute-start | bytes 1966088 | tf_op jit(solution)/shard_map/ppermute | solution.py:44
  93.7 5.4 %collective-permute-start.13 = (bf16[2,16,80,128]{3,2,1,0:T(8,128)(2,1)S(1)}, bf16[2,16,80,128]{3,2,1,0:T(8,128)(2,1)S(1)}, u32[]{:S(2)}, u32[]{:S(2)}) collective-permute-start(bf16[2,16,80,128]{3,2,1,0:T(8,128)(2,1)S(1)} %get-tuple-element.31), channel_id=1, source_target_pairs={{0,8},{8,0},{1,9},{9,1},{2,10},{10,2},{3,11},{11,3},{4,12},{12,4},... | collective-permute-start | bytes 1966088 | tf_op jit(solution)/shard_map/ppermute | solution.py:44
  93.8 5.8 %collective-permute-start.8 = (bf16[2,16,80,128]{3,2,1,0:T(8,128)(2,1)S(1)}, bf16[2,16,80,128]{3,2,1,0:T(8,128)(2,1)S(1)}, u32[]{:S(2)}, u32[]{:S(2)}) collective-permute-start(bf16[2,16,80,128]{3,2,1,0:T(8,128)(2,1)S(1)} %get-tuple-element.25), channel_id=1, source_target_pairs={{0,8},{8,0},{1,9},{9,1},{2,10},{10,2},{3,11},{11,3},{4,12},{12,4},... | collective-permute-start | bytes 1966088 | tf_op jit(solution)/shard_map/ppermute | solution.py:44
  95.5 18.8 %collective-permute-start.10 = (bf16[2,16,80,128]{3,2,1,0:T(8,128)(2,1)S(1)}, bf16[2,16,80,128]{3,2,1,0:T(8,128)(2,1)S(1)}, u32[]{:S(2)}, u32[]{:S(2)}) collective-permute-start(bf16[2,16,80,128]{3,2,1,0:T(8,128)(2,1)S(1)} %add_convert_fusion.3), channel_id=1, source_target_pairs={{0,1},{1,2},{2,3},{3,0},{4,5},{5,6},{6,7},{7,4},{8,9},{9,10},{10,1... | collective-permute-start | bytes 1966088 | tf_op jit(solution)/shard_map/ppermute | solution.py:40
  96.4 31.2 %collective-permute-start.12 = (bf16[2,16,80,128]{3,2,1,0:T(8,128)(2,1)S(1)}, bf16[2,16,80,128]{3,2,1,0:T(8,128)(2,1)S(1)}, u32[]{:S(2)}, u32[]{:S(2)}) collective-permute-start(bf16[2,16,80,128]{3,2,1,0:T(8,128)(2,1)S(1)} %add_convert_fusion.2), channel_id=1, source_target_pairs={{0,2},{1,3},{2,0},{3,1},{4,6},{5,7},{6,4},{7,5},{8,10},{9,11},{10,... | collective-permute-start | bytes 1966088 | tf_op jit(solution)/shard_map/ppermute | solution.py:40
  99.3 29.1 %collective-permute-start.14 = (bf16[2,16,80,128]{3,2,1,0:T(8,128)(2,1)S(1)}, bf16[2,16,80,128]{3,2,1,0:T(8,128)(2,1)S(1)}, u32[]{:S(2)}, u32[]{:S(2)}) collective-permute-start(bf16[2,16,80,128]{3,2,1,0:T(8,128)(2,1)S(1)} %add_convert_fusion.1), channel_id=1, source_target_pairs={{0,3},{1,0},{2,1},{3,2},{4,7},{5,4},{6,5},{7,6},{8,11},{9,8},{10,9... | collective-permute-start | bytes 1966088 | tf_op jit(solution)/shard_map/ppermute | solution.py:40
  128.5 18.3 %copy-start.7 = (bf16[2,16,80,128]{3,2,1,0:T(8,128)(2,1)S(1)}, bf16[2,16,80,128]{3,2,1,0:T(8,128)(2,1)}, u32[]{:S(2)}) copy-start(bf16[2,16,80,128]{3,2,1,0:T(8,128)(2,1)} %copy-done.6) | copy-start | bytes 1966084
  128.5 18.3 %copy-start.9 = (bf16[2,16,80,128]{3,2,1,0:T(8,128)(2,1)S(1)}, bf16[2,16,80,128]{3,2,1,0:T(8,128)(2,1)}, u32[]{:S(2)}) copy-start(bf16[2,16,80,128]{3,2,1,0:T(8,128)(2,1)} %copy-done.8) | copy-start | bytes 1966084
  128.9 17.9 %copy-start.1 = (bf16[2,16,80,128]{3,2,1,0:T(8,128)(2,1)S(1)}, bf16[2,16,80,128]{3,2,1,0:T(8,128)(2,1)}, u32[]{:S(2)}) copy-start(bf16[2,16,80,128]{3,2,1,0:T(8,128)(2,1)} %copy-done) | copy-start | bytes 1966084
  129.0 8.7 %collective-permute-start.15 = (bf16[16,80,128]{2,1,0:T(8,128)(2,1)S(1)}, bf16[16,80,128]{2,1,0:T(8,128)(2,1)S(1)}, u32[]{:S(2)}, u32[]{:S(2)}) collective-permute-start(bf16[16,80,128]{2,1,0:T(8,128)(2,1)S(1)} %slice_bitcast_fusion), channel_id=1, source_target_pairs={{0,4},{4,0},{1,5},{5,1},{2,6},{6,2},{3,7},{7,3},{8,12},{12,8},{9,1... | collective-permute-start | bytes 983048 | tf_op jit(solution)/shard_map/ppermute | solution.py:44
  138.5 19.8 %all-to-all-start.1 = ((bf16[16,80,128]{2,1,0:T(8,128)(2,1)}), bf16[16,80,128]{2,1,0:T(8,128)(2,1)}, u32[]{:S(2)}, u32[]{:S(2)}) async-start(bf16[16,80,128]{2,1,0:T(8,128)(2,1)} %fusion), calls=%async_computation.1 | async-start | bytes 655360 | tf_op jit(solution)/shard_map/all_to_all | solution.py:66
  (8 other events, 56.5 us)

commit v3 on v2

--- a/solution.py
+++ b/solution.py
@@ -1,4 +1,4 @@
-import functools
+import itertools
 
 import jax
 import jax.numpy as jnp
@@ -17,8 +17,8 @@
 TOKENS = 512
 
 AXES = ("xh", "z", "c", "xl", "y")
+X = ("xh", "xl")
 SIZES = (2, 8, 2, 2, 4)
-CHIPS = 16
 ROWS = 80
 BF = jnp.bfloat16
 F32 = jnp.float32
@@ -36,53 +36,61 @@
     return jnp.dot(left, right, preferred_element_type=F32)
 
 
-def shift(block, axis, size, step):
-    return lax.ppermute(block, axis, [(i, (i - step) % size) for i in range(size)])
-
-
-def swap(block, axis):
-    return lax.ppermute(block, axis, [(0, 1), (1, 0)])
+def flat(xh, z, c, xl, y):
+    return (((xh * 8 + z) * 2 + c) * 2 + xl) * 4 + y
+
+
+def shift(block, along_x, step):
+    pairs = []
+    for x, z, c, y in itertools.product(range(4), range(8), range(2), range(4)):
+        from_x, from_y = ((x + step) % 4, y) if c == along_x else (x, (y + step) % 4)
+        source = flat(from_x // 2, z, c, from_x % 2, from_y)
+        pairs.append((source, flat(x // 2, z, c, x % 2, y)))
+    return lax.ppermute(block, AXES, pairs)
+
+
+def swap(block):
+    return lax.ppermute(block, "c", [(0, 1), (1, 0)])
 
 
 def gather_blocks(block):
-    mine = lax.all_to_all(
-        jnp.broadcast_to(block[None], (CHIPS, ROWS, 128)), ("xh", "z"), 0, 0, tiled=True
-    )
-    own = jnp.stack([mine, swap(mine, "xl")])
-    pieces = [own, shift(own, "y", 4, 1), shift(own, "y", 4, 2), shift(own, "y", 4, 3)]
-    return pieces + [swap(piece, "c") for piece in pieces]
+    mine = lax.all_to_all(jnp.broadcast_to(block[None], (8, ROWS, 128)), "z", 0, 0, tiled=True)
+    first = jnp.stack([mine] + [shift(mine, 0, step) for step in (1, 2, 3)])
+    pieces = [first] + [shift(first, 1, step) for step in (1, 2, 3)]
+    return pieces + [swap(piece) for piece in pieces]
 
 
 def scatter_blocks(pieces):
-    summed = []
-    for step in range(4):
-        arrived = swap(pieces[4 + step], "c")
-        summed.append((pieces[step].astype(F32) + arrived.astype(F32)).astype(BF))
-    total = summed[0].astype(F32)
-    for step in (1, 2, 3):
-        total = total + shift(summed[step], "y", 4, -step).astype(F32)
-    total = total.astype(BF)
-    pair = (total[0].astype(F32) + swap(total[1], "xl").astype(F32)).astype(BF)
-    parts = lax.all_to_all(pair, ("xh", "z"), 0, 0, tiled=True)
+    summed = [
+        (pieces[i].astype(F32) + swap(pieces[4 + i]).astype(F32)).astype(BF) for i in range(4)
+    ]
+    for along_x in (1, 0):
+        total = summed[0].astype(F32)
+        for step in (1, 2, 3):
+            total = total + shift(summed[step], along_x, -step).astype(F32)
+        summed = total.astype(BF)
+    parts = lax.all_to_all(summed, "z", 0, 0, tiled=True)
     return jnp.sum(parts.astype(F32), axis=0)
 
 
 def assembly(where, pieces, w_q, w_kv, w_o, sems):
-    c, xl, y = where[0], where[1], where[2]
+    c, x, y = where[0], where[1], where[2]
     copies = ([], [], [])
-    for at in range(16):
-        c_rel, y_rel, xl_rel = at // 8, (at // 2) % 4, at % 2
-        source = pieces[c_rel * 4 + y_rel].at[xl_rel]
+    for at in range(32):
+        c_rel, second, first = at // 16, (at // 4) % 4, at % 4
         core = lax.rem(c + c_rel, 2)
-        node = lax.rem(xl + xl_rel, 2) * 4 + lax.rem(y + y_rel, 4)
+        chip_x = lax.rem(x + first + core * (second - first), 4)
+        chip_y = lax.rem(y + second + core * (first - second), 4)
+        high, node = chip_x // 2, lax.rem(chip_x, 2) * 4 + chip_y
         lanes = pl.ds(pl.multiple_of(node * 128, 128), 128)
+        source = pieces[c_rel * 4 + second].at[first]
         for part, (target, start, count) in enumerate(
             ((w_q, 0, 32), (w_kv, 32, 16), (w_o, 48, 32))
         ):
             copies[part].append(
                 pltpu.make_async_copy(
                     source.at[:, pl.ds(start, count), :],
-                    target.at[:, core, :, lanes],
+                    target.at[high, :, core, :, lanes],
                     sems.at[part, at],
                 )
             )
@@ -135,13 +143,13 @@
 
     finish(copy_o)
     for n in range(4):
-        columns = w_o[:, :, :, pl.ds(n * 256, 256)].reshape(D, 256)
+        columns = w_o[:, :, :, :, pl.ds(n * 256, 256)].reshape(D, 256)
         dm_t[pl.ds(n * 256, 256), :] = dot(cot[...], columns).astype(BF).T
 
     cos, sin = table[0], table[1]
     finish(copy_q)
     for n in range(4):
-        rows = w_q[pl.ds(n * 4, 4)].reshape(256, D)
+        rows = w_q[n // 2, pl.ds(n % 2 * 4, 4)].reshape(256, D)
         value = dot(rows, normed_t[...]) * 0.125
         for h in range(4):
             a, b = value[h * HD : h * HD + HALF], value[h * HD + HALF : (h + 1) * HD]
@@ -149,7 +157,7 @@
             q_t[pl.ds(n * 256 + h * HD + HALF, HALF), :] = (a * sin + b * cos).astype(BF)
     finish(copy_kv)
     for n in range(4):
-        rows = w_kv[pl.ds(n * 4, 4)].reshape(128, D)
+        rows = w_kv[n // 2, pl.ds(n % 2 * 4, 4)].reshape(128, D)
         value = dot(rows, normed_t[...]).reshape(8, 2, 8, TOKENS)
         keys = value[:, 0].reshape(HD, TOKENS)
         a, b = keys[:HALF], keys[HALF:]
@@ -208,25 +216,24 @@
         dkv_t[pl.ds(n * 128, 128), :] = both.astype(BF)
         mix[:, pl.ds(n * 256, 256)] = mix_t[pl.ds(n * 256, 256), :].T
 
-    c, xl, y = where[0], where[1], where[2]
+    c, x, y = where[0], where[1], where[2]
     for n in range(4):
         lanes = pl.ds(n * 256, 256)
-        places = []
-        for node in (2 * n, 2 * n + 1):
-            places.append((lax.rem(node % 4 - y + 4, 4), lax.rem(node // 4 - xl + 2, 2)))
         for left, right, start, count in (
             (dq_t, normed, 0, 32),
             (dkv_t, normed, 32, 16),
             (cot_t, mix, 48, 32),
         ):
             size = left.shape[0] // 2
-            for half in range(2):
-                value = dot(left[pl.ds(half * size, size), :], right[:, lanes]).astype(BF)
+            for high in range(2):
+                value = dot(left[pl.ds(high * size, size), :], right[:, lanes]).astype(BF)
                 value = value.reshape(8, 2, count, 256)
-                for core in range(2):
-                    c_rel = lax.rem(core - c + 2, 2)
-                    for i, (y_rel, xl_rel) in enumerate(places):
-                        out[c_rel, y_rel, xl_rel, pl.ds(half * 8, 8), pl.ds(start, count), :] = (
+                x_rel = lax.rem(high * 2 + n // 2 - x + 4, 4)
+                for i in range(2):
+                    y_rel = lax.rem(n % 2 * 2 + i - y + 4, 4)
+                    for core, (second, first) in enumerate(((y_rel, x_rel), (x_rel, y_rel))):
+                        c_rel = lax.rem(core - c + 2, 2)
+                        out[c_rel, second, first, :, pl.ds(start, count), :] = (
                             value[:, core, :, i * 128 : (i + 1) * 128]
                         )
     copies = [
@@ -250,7 +257,7 @@
     finish(copy_o)
     for n in range(4):
         lanes = pl.ds(n * 256, 256)
-        rows = w_o[pl.ds(n * 4, 4)].reshape(256, D)
+        rows = w_o[n // 2, pl.ds(n % 2 * 4, 4)].reshape(256, D)
         value = lax.dot_general(
             mix[...], rows, (((1,), (1,)), ((), ())), preferred_element_type=F32
         )
@@ -259,8 +266,8 @@
     finish(copy_kv)
     for n in range(4):
         lanes = pl.ds(n * 256, 256)
-        value = dot(dq[...], w_q[:, :, :, lanes].reshape(D, 256))
-        d_normed[:, lanes] = value + dot(dkv[...], w_kv[:, :, :, lanes].reshape(2 * KV, 256))
+        value = dot(dq[...], w_q[:, :, :, :, lanes].reshape(D, 256))
+        d_normed[:, lanes] = value + dot(dkv[...], w_kv[:, :, :, :, lanes].reshape(2 * KV, 256))
 
     @pl.loop(0, TOKENS // 64)
     def _(step):
@@ -276,7 +283,7 @@
 SMEM = pl.BlockSpec(memory_space=pltpu.SMEM)
 VMEM = pl.BlockSpec(memory_space=pltpu.VMEM)
 ANY = pl.BlockSpec(memory_space=pl.ANY)
-PIECE = jax.ShapeDtypeStruct((2, CHIPS, ROWS, 128), BF)
+PIECE = jax.ShapeDtypeStruct((4, 8, ROWS, 128), BF)
 
 
 def scratch(*shape, dtype=BF):
@@ -285,16 +292,16 @@
 
 def weights_scratch():
     return [
-        scratch(CHIPS, 2, 32, D),
-        scratch(CHIPS, 2, 16, D),
-        scratch(CHIPS, 2, 32, D),
+        scratch(2, 8, 2, 32, D),
+        scratch(2, 8, 2, 16, D),
+        scratch(2, 8, 2, 32, D),
     ]
 
 
 def local(hidden, norm_gain, w_query, w_key, w_value, w_out, doc_lengths, cotangent):
     block = jnp.concatenate([w_query.T, w_key.T, w_value.T, w_out.T], axis=0)
     pieces = gather_blocks(block)
-    where = jnp.stack([lax.axis_index(name) for name in ("c", "xl", "y")])
+    where = jnp.stack([lax.axis_index(name) for name in ("c", X, "y")])
     gain = norm_gain.reshape(1, D)
     table = jnp.asarray(tables())
     shapes = [
@@ -323,8 +330,8 @@
             scratch(4, HD, TOKENS, dtype=F32),
             scratch(4, HD, TOKENS, dtype=F32),
             scratch(2, SEQ, SEQ, dtype=F32),
-            scratch(2, 4, 2, CHIPS, ROWS, 128),
-            pltpu.SemaphoreType.DMA((3, 16)),
+            scratch(2, 4, 4, 8, ROWS, 128),
+            pltpu.SemaphoreType.DMA((3, 32)),
             pltpu.SemaphoreType.DMA((8,)),
         ],
         compiler_params=pltpu.CompilerParams(vmem_limit_bytes=VMEM_BYTES),
@@ -344,7 +351,7 @@
             scratch(TOKENS, D),
             scratch(TOKENS, 2 * KV),
             scratch(TOKENS, D, dtype=F32),
-            pltpu.SemaphoreType.DMA((3, 16)),
+            pltpu.SemaphoreType.DMA((3, 32)),
         ],
         compiler_params=pltpu.CompilerParams(vmem_limit_bytes=VMEM_BYTES),
         cost_estimate=pl.CostEstimate(

time: 162 us -> 132 us (0.81); the launches traced: 160 us -> 132 us
  waiting for transfers between devices: 74 us -> 44.5 us
  starting transfers between devices: 19.1 us -> 26.3 us
  blocking collectives: 23.7 us -> 16.7 us
  Pallas kernels: 36.8 us -> 38.6 us
    ppermute x16 -> x20, waiting for transfers between devices: 74 us -> 44.5 us  [the longest x12 40.7 us: shift(): return lax.ppermute(block, AXES, pairs)]
    ppermute x16 -> x20, starting transfers between devices: 10.7 us -> 21.5 us  [the longest x12 19.9 us: shift(): return lax.ppermute(block, AXES, pairs)]
    all_to_all x1, blocking collectives: 23.7 us -> 16.7 us  [gather_blocks(): lax.all_to_all(jnp.broadcast_to(block[None], (8, ROWS, 128)), 'z', 0, 0,...]
    all_to_all x1, starting transfers between devices: 8.35 us -> 4.75 us  [scatter_blocks(): parts = lax.all_to_all(summed, 'z', 0, 0, tiled=True)]
  transfers between devices with their start and end apart: 17 -> 21, of which waited for: 10 -> 12; matrix products, arithmetic and copies ran while one was open for 0% -> 0% of each run, Pallas kernels for 6% -> 8%
where the time goes in v3:
time: 132 us
  waiting for transfers between devices  44.5 us (34%)
  Pallas kernels  38.6 us (29%)
  starting transfers between devices  26.3 us (20%)
  blocking collectives  16.7 us (13%)
  other arithmetic  2.71 us (2%)
  local copies, waits for them, and re-layouts  2.37 us (2%)
    ppermute x12, waiting for transfers between devices, shift(): return lax.ppermute(block, AXES, pairs)  40.7 us
    pallas_call x1, Pallas kernels, local(): pl.pallas_call(attend, name='attend', out_shape=[PIECE] * 8 + shapes, in_...  27.5 us
    ppermute x12, starting transfers between devices, shift(): return lax.ppermute(block, AXES, pairs)  19.9 us
    all_to_all x1, blocking collectives, gather_blocks(): lax.all_to_all(jnp.broadcast_to(block[None], (8, ROWS, 128)), 'z', 0, 0,...  16.7 us
    pallas_call x1, Pallas kernels, local(): pl.pallas_call(close, name='close', out_shape=[jax.ShapeDtypeStruct((TOKE...  11.1 us
    all_to_all x1, starting transfers between devices, scatter_blocks(): parts = lax.all_to_all(summed, 'z', 0, 0, tiled=True)  4.75 us
    ppermute x8, waiting for transfers between devices, swap(): return lax.ppermute(block, 'c', [(0, 1), (1, 0)])  3.88 us
  transfers between devices with their start and end apart: 21, of which 12 were waited for; matrix products, arithmetic and copies ran while one was open for 0% of the time, Pallas kernels for 8%

profile of v3, /device:TPU:32, one launch (start us, length us, event | category | flops | bytes accessed | tf_op | source)
XLA Modules:
  0.0 132.1 jit_solution(12524564171082330439)
XLA Ops:
  0.7 0.8 pad_maximum_fusion.1
  1.5 16.7 %all_to_all.10 = bf16[8,80,128]{2,1,0:T(8,128)(2,1)S(1)} all-to-all(bf16[8,80,128]{2,1,0:T(8,128)(2,1)S(1)} %broadcast_in_dim.2), channel_id=1, replica_groups=mesh['xh'=2,'z'=8,'c'=2,'xl'=2,'y'=4] {'z'}, dimensions={0} | all-to-all | bytes 327680 | tf_op jit(solution)/shard_map/all_to_all | solution.py:57
  18.2 3.0 %collective-permute-start.1 = (bf16[8,80,128]{2,1,0:T(8,128)(2,1)S(1)}, bf16[8,80,128]{2,1,0:T(8,128)(2,1)S(1)}, u32[]{:S(2)}, u32[]{:S(2)}) collective-permute-start(bf16[8,80,128]{2,1,0:T(8,128)(2,1)S(1)} %all_to_all.10), channel_id=1, source_target_pairs={{128,0},{129,1},{130,2},{131,3},{10,8},{11,9},{8,10},{9,11},{144,1... | collective-permute-start | bytes 491528 | tf_op jit(solution)/shard_map/ppermute | solution.py:49
  21.8 2.6 %collective-permute-start = (bf16[8,80,128]{2,1,0:T(8,128)(2,1)S(1)}, bf16[8,80,128]{2,1,0:T(8,128)(2,1)S(1)}, u32[]{:S(2)}, u32[]{:S(2)}) collective-permute-start(bf16[8,80,128]{2,1,0:T(8,128)(2,1)S(1)} %all_to_all.10), channel_id=1, source_target_pairs={{4,0},{5,1},{6,2},{7,3},{9,8},{10,9},{11,10},{8,11},{20,16},{21,17... | collective-permute-start | bytes 491528 | tf_op jit(solution)/shard_map/ppermute | solution.py:49
  25.0 2.7 %collective-permute-done.2 = bf16[8,80,128]{2,1,0:T(8,128)(2,1)S(1)} collective-permute-done((bf16[8,80,128]{2,1,0:T(8,128)(2,1)S(1)}, bf16[8,80,128]{2,1,0:T(8,128)(2,1)S(1)}, u32[]{:S(2)}, u32[]{:S(2)}) %collective-permute-start.2) | collective-permute-done | bytes 163872 | tf_op jit(solution)/shard_map/ppermute | solution.py:49
  27.8 3.1 %collective-permute-start.3 = (bf16[4,8,80,128]{3,2,1,0:T(8,128)(2,1)S(1)}, bf16[4,8,80,128]{3,2,1,0:T(8,128)(2,1)S(1)}, u32[]{:S(2)}, u32[]{:S(2)}) collective-permute-start(bf16[4,8,80,128]{3,2,1,0:T(8,128)(2,1)S(1)} %pad_maximum_fusion.rest_0_), channel_id=1, source_target_pairs={{1,0},{2,1},{3,2},{0,3},{12,8},{13,9},{14,10},{15,11},{17,16},{18,... | collective-permute-start | bytes 1966088 | tf_op jit(solution)/shard_map/ppermute | solution.py:49
  30.9 1.0 collective-permute-start.4
  32.0 1.3 collective-permute-start.5
  33.3 12.8 %collective-permute-done.3.rest_1_ = bf16[4,8,80,128]{3,2,1,0:T(8,128)(2,1)S(1)} collective-permute-done((bf16[4,8,80,128]{3,2,1,0:T(8,128)(2,1)S(1)}, bf16[4,8,80,128]{3,2,1,0:T(8,128)(2,1)S(1)}, u32[]{:S(2)}, u32[]{:S(2)}) %collective-permute-start.3) | collective-permute-done | bytes 655392 | tf_op jit(solution)/shard_map/ppermute | solution.py:49
  46.6 3.5 %collective-permute-done.5.rest_3_ = bf16[4,8,80,128]{3,2,1,0:T(8,128)(2,1)S(1)} collective-permute-done((bf16[4,8,80,128]{3,2,1,0:T(8,128)(2,1)S(1)}, bf16[4,8,80,128]{3,2,1,0:T(8,128)(2,1)S(1)}, u32[]{:S(2)}, u32[]{:S(2)}) %collective-permute-start.5) | collective-permute-done | bytes 655392 | tf_op jit(solution)/shard_map/ppermute | solution.py:49
  50.2 2.1 %collective-permute-done.9.rest_7_ = bf16[4,8,80,128]{3,2,1,0:T(8,128)(2,1)} collective-permute-done((bf16[4,8,80,128]{3,2,1,0:T(8,128)(2,1)S(1)}, bf16[4,8,80,128]{3,2,1,0:T(8,128)(2,1)}, u32[]{:S(2)}, u32[]{:S(2)}) %collective-permute-start.9) | collective-permute-done | bytes 655392 | tf_op jit(solution)/shard_map/ppermute | solution.py:53
  52.3 27.5 %attend.1 = (bf16[4,8,80,128]{3,2,1,0:T(8,128)(2,1)S(1)}, bf16[4,8,80,128]{3,2,1,0:T(8,128)(2,1)S(1)}, bf16[4,8,80,128]{3,2,1,0:T(8,128)(2,1)S(1)}, bf16[4,8,80,...) custom-call(s32[3]{0:T(128)S(1)} %pad_add_fusion.where, ...), custom_call_target="tpu_custom_call" | custom-call | flops 7000000000 | bytes 20000000 | tf_op jit(solution)/shard_map/attend/pallas_call | solution.py:312
  81.0 1.1 collective-permute-done.11
  83.2 2.7 %collective-permute-start.14 = (bf16[4,8,80,128]{3,2,1,0:T(8,128)(2,1)S(1)}, bf16[4,8,80,128]{3,2,1,0:T(8,128)(2,1)S(1)}, u32[]{:S(2)}, u32[]{:S(2)}) collective-permute-start(bf16[4,8,80,128]{3,2,1,0:T(8,128)(2,1)S(1)} %add_convert_fusion.2), channel_id=1, source_target_pairs={{2,0},{3,1},{0,2},{1,3},{136,8},{137,9},{138,10},{139,11},{18,16},... | collective-permute-start | bytes 1966088 | tf_op jit(solution)/shard_map/ppermute | solution.py:49
  86.1 0.7 collective-permute-start.16
  86.7 14.4 %collective-permute-done.12 = bf16[4,8,80,128]{3,2,1,0:T(8,128)(2,1)S(1)} collective-permute-done((bf16[4,8,80,128]{3,2,1,0:T(8,128)(2,1)S(1)}, bf16[4,8,80,128]{3,2,1,0:T(8,128)(2,1)S(1)}, u32[]{:S(2)}, u32[]{:S(2)}) %collective-permute-start.12) | collective-permute-done | bytes 655392 | tf_op jit(solution)/shard_map/ppermute | solution.py:49
  101.1 1.4 %collective-permute-done.16 = bf16[4,8,80,128]{3,2,1,0:T(8,128)(2,1)S(1)} collective-permute-done((bf16[4,8,80,128]{3,2,1,0:T(8,128)(2,1)S(1)}, bf16[4,8,80,128]{3,2,1,0:T(8,128)(2,1)S(1)}, u32[]{:S(2)}, u32[]{:S(2)}) %collective-permute-start.16) | collective-permute-done | bytes 655392 | tf_op jit(solution)/shard_map/ppermute | solution.py:49
  103.7 4.1 %collective-permute-start.18 = (bf16[8,80,128]{2,1,0:T(8,128)(2,1)S(1)}, bf16[8,80,128]{2,1,0:T(8,128)(2,1)S(1)}, u32[]{:S(2)}, u32[]{:S(2)}) collective-permute-start(bf16[8,80,128]{2,1,0:T(8,128)(2,1)S(1)} %get-tuple-element.34), channel_id=1, source_target_pairs={{128,0},{129,1},{130,2},{131,3},{10,8},{11,9},{8,10},{9,11},{144,1... | collective-permute-start | bytes 491528 | tf_op jit(solution)/shard_map/ppermute | solution.py:49
  107.8 1.8 %collective-permute-done.17 = bf16[8,80,128]{2,1,0:T(8,128)(2,1)S(1)} collective-permute-done((bf16[8,80,128]{2,1,0:T(8,128)(2,1)S(1)}, bf16[8,80,128]{2,1,0:T(8,128)(2,1)S(1)}, u32[]{:S(2)}, u32[]{:S(2)}) %collective-permute-start.17) | collective-permute-done | bytes 163872 | tf_op jit(solution)/shard_map/ppermute | solution.py:49
  109.7 3.2 %collective-permute-done.18 = bf16[8,80,128]{2,1,0:T(8,128)(2,1)S(1)} collective-permute-done((bf16[8,80,128]{2,1,0:T(8,128)(2,1)S(1)}, bf16[8,80,128]{2,1,0:T(8,128)(2,1)S(1)}, u32[]{:S(2)}, u32[]{:S(2)}) %collective-permute-start.18) | collective-permute-done | bytes 163872 | tf_op jit(solution)/shard_map/ppermute | solution.py:49
  113.1 0.8 fusion.2
  113.9 4.7 %all-to-all-start.1 = ((bf16[8,80,128]{2,1,0:T(8,128)(2,1)}), bf16[8,80,128]{2,1,0:T(8,128)(2,1)S(1)}, u32[]{:S(2)}, u32[]{:S(2)}) async-start(bf16[8,80,128]{2,1,0:T(8,128)(2,1)} %fusion.2), calls=%async_computation.1 | async-start | bytes 327680 | tf_op jit(solution)/shard_map/all_to_all | solution.py:72
  118.7 1.0 copy-done.14
  119.7 11.1 %close.1 = (bf16[512,1024]{1,0:T(8,128)(2,1)}, bf16[512,1024]{1,0:T(8,128)(2,1)}) custom-call(s32[3]{0:T(128)S(1)} %pad_add_fusion.where, f32[1,1024]{1,0:T(1,128)S(1)} %bitcast.32, bf16[512,1024]{1,0:T(8,128)(2,1)} %hidden.3, bf16[512,1024]{1,0:T(8,128)(2,1)} %cot.3, bf16[512,1024]{1,0:T(8,128)(2,1)} %get-tuple-element.19.mix, ...), custom_call_target="tpu_custom_call" | custom-call | flops 3000000000 | bytes 15000000 | tf_op jit(solution)/shard_map/close/pallas_call | solution.py:343
  (64 shorter events, 7.0 us)
Async XLA Ops:
  0.6 51.7 %copy-start.12 = (f32[2,32,512]{2,1,0:T(8,128)S(1)}, f32[2,32,512]{2,1,0:T(8,128)}, u32[]{:S(2)}) copy-start(f32[2,32,512]{2,1,0:T(8,128)} %constant.22.clone.table) | copy-start | bytes 393220
  0.6 51.7 %copy-start.10 = (f32[1024]{0:T(1024)S(1)}, f32[1024]{0:T(1024)}, u32[]{:S(2)}) copy-start(f32[1024]{0:T(1024)} %param.10) | copy-start | bytes 12292
  0.7 51.7 %copy-start.11 = (s32[2,4]{1,0:T(2,128)S(1)}, s32[2,4]{1,0:T(2,128)}, u32[]{:S(2)}) copy-start(s32[2,4]{1,0:T(2,128)} %docs.1) | copy-start | bytes 100
  18.2 6.8 %collective-permute-start.1 = (bf16[8,80,128]{2,1,0:T(8,128)(2,1)S(1)}, bf16[8,80,128]{2,1,0:T(8,128)(2,1)S(1)}, u32[]{:S(2)}, u32[]{:S(2)}) collective-permute-start(bf16[8,80,128]{2,1,0:T(8,128)(2,1)S(1)} %all_to_all.10), channel_id=1, source_target_pairs={{128,0},{129,1},{130,2},{131,3},{10,8},{11,9},{8,10},{9,11},{144,1... | collective-permute-start | bytes 491528 | tf_op jit(solution)/shard_map/ppermute | solution.py:49
  21.2 6.5 %collective-permute-start.2 = (bf16[8,80,128]{2,1,0:T(8,128)(2,1)S(1)}, bf16[8,80,128]{2,1,0:T(8,128)(2,1)S(1)}, u32[]{:S(2)}, u32[]{:S(2)}) collective-permute-start(bf16[8,80,128]{2,1,0:T(8,128)(2,1)S(1)} %all_to_all.10), channel_id=1, source_target_pairs={{132,0},{133,1},{134,2},{135,3},{11,8},{8,9},{9,10},{10,11},{148,1... | collective-permute-start | bytes 491528 | tf_op jit(solution)/shard_map/ppermute | solution.py:49
  21.8 5.9 %collective-permute-start = (bf16[8,80,128]{2,1,0:T(8,128)(2,1)S(1)}, bf16[8,80,128]{2,1,0:T(8,128)(2,1)S(1)}, u32[]{:S(2)}, u32[]{:S(2)}) collective-permute-start(bf16[8,80,128]{2,1,0:T(8,128)(2,1)S(1)} %all_to_all.10), channel_id=1, source_target_pairs={{4,0},{5,1},{6,2},{7,3},{9,8},{10,9},{11,10},{8,11},{20,16},{21,17... | collective-permute-start | bytes 491528 | tf_op jit(solution)/shard_map/ppermute | solution.py:49
  27.8 18.2 %collective-permute-start.3 = (bf16[4,8,80,128]{3,2,1,0:T(8,128)(2,1)S(1)}, bf16[4,8,80,128]{3,2,1,0:T(8,128)(2,1)S(1)}, u32[]{:S(2)}, u32[]{:S(2)}) collective-permute-start(bf16[4,8,80,128]{3,2,1,0:T(8,128)(2,1)S(1)} %pad_maximum_fusion.rest_0_), channel_id=1, source_target_pairs={{1,0},{2,1},{3,2},{0,3},{12,8},{13,9},{14,10},{15,11},{17,16},{18,... | collective-permute-start | bytes 1966088 | tf_op jit(solution)/shard_map/ppermute | solution.py:49
  30.9 15.1 %collective-permute-start.4 = (bf16[4,8,80,128]{3,2,1,0:T(8,128)(2,1)S(1)}, bf16[4,8,80,128]{3,2,1,0:T(8,128)(2,1)S(1)}, u32[]{:S(2)}, u32[]{:S(2)}) collective-permute-start(bf16[4,8,80,128]{3,2,1,0:T(8,128)(2,1)S(1)} %pad_maximum_fusion.rest_0_), channel_id=1, source_target_pairs={{2,0},{3,1},{0,2},{1,3},{136,8},{137,9},{138,10},{139,11},{18,16},... | collective-permute-start | bytes 1966088 | tf_op jit(solution)/shard_map/ppermute | solution.py:49
  32.0 18.1 %collective-permute-start.5 = (bf16[4,8,80,128]{3,2,1,0:T(8,128)(2,1)S(1)}, bf16[4,8,80,128]{3,2,1,0:T(8,128)(2,1)S(1)}, u32[]{:S(2)}, u32[]{:S(2)}) collective-permute-start(bf16[4,8,80,128]{3,2,1,0:T(8,128)(2,1)S(1)} %pad_maximum_fusion.rest_0_), channel_id=1, source_target_pairs={{3,0},{0,1},{1,2},{2,3},{140,8},{141,9},{142,10},{143,11},{19,16},... | collective-permute-start | bytes 1966088 | tf_op jit(solution)/shard_map/ppermute | solution.py:49
  33.3 16.9 %collective-permute-start.6 = (bf16[4,8,80,128]{3,2,1,0:T(8,128)(2,1)S(1)}, bf16[4,8,80,128]{3,2,1,0:T(8,128)(2,1)S(1)}, u32[]{:S(2)}, u32[]{:S(2)}) collective-permute-start(bf16[4,8,80,128]{3,2,1,0:T(8,128)(2,1)S(1)} %pad_maximum_fusion.rest_0_), channel_id=1, source_target_pairs={{0,8},{8,0},{1,9},{9,1},{2,10},{10,2},{3,11},{11,3},{4,12},{12,4},... | collective-permute-start | bytes 1966088 | tf_op jit(solution)/shard_map/ppermute | solution.py:53
  46.1 4.1 %collective-permute-start.7 = (bf16[4,8,80,128]{3,2,1,0:T(8,128)(2,1)S(1)}, bf16[4,8,80,128]{3,2,1,0:T(8,128)(2,1)}, u32[]{:S(2)}, u32[]{:S(2)}) collective-permute-start(bf16[4,8,80,128]{3,2,1,0:T(8,128)(2,1)S(1)} %collective-permute-done.3.rest_1_), channel_id=1, source_target_pairs={{0,8},{8,0},{1,9},{9,1},{2,10},{10,2},{3,11},{11,3},{4,12},{12,4},... | collective-permute-start | bytes 1966088 | tf_op jit(solution)/shard_map/ppermute | solution.py:53
  46.1 4.1 %collective-permute-start.8 = (bf16[4,8,80,128]{3,2,1,0:T(8,128)(2,1)S(1)}, bf16[4,8,80,128]{3,2,1,0:T(8,128)(2,1)}, u32[]{:S(2)}, u32[]{:S(2)}) collective-permute-start(bf16[4,8,80,128]{3,2,1,0:T(8,128)(2,1)S(1)} %collective-permute-done.4.rest_2_), channel_id=1, source_target_pairs={{0,8},{8,0},{1,9},{9,1},{2,10},{10,2},{3,11},{11,3},{4,12},{12,4},... | collective-permute-start | bytes 1966088 | tf_op jit(solution)/shard_map/ppermute | solution.py:53
  50.1 2.2 %collective-permute-start.9 = (bf16[4,8,80,128]{3,2,1,0:T(8,128)(2,1)S(1)}, bf16[4,8,80,128]{3,2,1,0:T(8,128)(2,1)}, u32[]{:S(2)}, u32[]{:S(2)}) collective-permute-start(bf16[4,8,80,128]{3,2,1,0:T(8,128)(2,1)S(1)} %collective-permute-done.5.rest_3_), channel_id=1, source_target_pairs={{0,8},{8,0},{1,9},{9,1},{2,10},{10,2},{3,11},{11,3},{4,12},{12,4},... | collective-permute-start | bytes 1966088 | tf_op jit(solution)/shard_map/ppermute | solution.py:53
  79.9 2.2 %collective-permute-start.11 = (bf16[4,8,80,128]{3,2,1,0:T(8,128)(2,1)S(1)}, bf16[4,8,80,128]{3,2,1,0:T(8,128)(2,1)S(1)}, u32[]{:S(2)}, u32[]{:S(2)}) collective-permute-start(bf16[4,8,80,128]{3,2,1,0:T(8,128)(2,1)S(1)} %get-tuple-element.27), channel_id=1, source_target_pairs={{0,8},{8,0},{1,9},{9,1},{2,10},{10,2},{3,11},{11,3},{4,12},{12,4},... | collective-permute-start | bytes 1966088 | tf_op jit(solution)/shard_map/ppermute | solution.py:53
  80.1 2.9 %collective-permute-start.13 = (bf16[4,8,80,128]{3,2,1,0:T(8,128)(2,1)S(1)}, bf16[4,8,80,128]{3,2,1,0:T(8,128)(2,1)S(1)}, u32[]{:S(2)}, u32[]{:S(2)}) collective-permute-start(bf16[4,8,80,128]{3,2,1,0:T(8,128)(2,1)S(1)} %get-tuple-element.29), channel_id=1, source_target_pairs={{0,8},{8,0},{1,9},{9,1},{2,10},{10,2},{3,11},{11,3},{4,12},{12,4},... | collective-permute-start | bytes 1966088 | tf_op jit(solution)/shard_map/ppermute | solution.py:53
  80.5 5.4 %collective-permute-start.15 = (bf16[4,8,80,128]{3,2,1,0:T(8,128)(2,1)S(1)}, bf16[4,8,80,128]{3,2,1,0:T(8,128)(2,1)S(1)}, u32[]{:S(2)}, u32[]{:S(2)}) collective-permute-start(bf16[4,8,80,128]{3,2,1,0:T(8,128)(2,1)S(1)} %get-tuple-element.31), channel_id=1, source_target_pairs={{0,8},{8,0},{1,9},{9,1},{2,10},{10,2},{3,11},{11,3},{4,12},{12,4},... | collective-permute-start | bytes 1966088 | tf_op jit(solution)/shard_map/ppermute | solution.py:53
  80.6 6.1 %collective-permute-start.10 = (bf16[4,8,80,128]{3,2,1,0:T(8,128)(2,1)S(1)}, bf16[4,8,80,128]{3,2,1,0:T(8,128)(2,1)S(1)}, u32[]{:S(2)}, u32[]{:S(2)}) collective-permute-start(bf16[4,8,80,128]{3,2,1,0:T(8,128)(2,1)S(1)} %get-tuple-element.25), channel_id=1, source_target_pairs={{0,8},{8,0},{1,9},{9,1},{2,10},{10,2},{3,11},{11,3},{4,12},{12,4},... | collective-permute-start | bytes 1966088 | tf_op jit(solution)/shard_map/ppermute | solution.py:53
  82.2 18.9 %collective-permute-start.12 = (bf16[4,8,80,128]{3,2,1,0:T(8,128)(2,1)S(1)}, bf16[4,8,80,128]{3,2,1,0:T(8,128)(2,1)S(1)}, u32[]{:S(2)}, u32[]{:S(2)}) collective-permute-start(bf16[4,8,80,128]{3,2,1,0:T(8,128)(2,1)S(1)} %add_convert_fusion.3), channel_id=1, source_target_pairs={{3,0},{0,1},{1,2},{2,3},{140,8},{141,9},{142,10},{143,11},{19,16},... | collective-permute-start | bytes 1966088 | tf_op jit(solution)/shard_map/ppermute | solution.py:49
  83.2 18.0 %collective-permute-start.14 = (bf16[4,8,80,128]{3,2,1,0:T(8,128)(2,1)S(1)}, bf16[4,8,80,128]{3,2,1,0:T(8,128)(2,1)S(1)}, u32[]{:S(2)}, u32[]{:S(2)}) collective-permute-start(bf16[4,8,80,128]{3,2,1,0:T(8,128)(2,1)S(1)} %add_convert_fusion.2), channel_id=1, source_target_pairs={{2,0},{3,1},{0,2},{1,3},{136,8},{137,9},{138,10},{139,11},{18,16},... | collective-permute-start | bytes 1966088 | tf_op jit(solution)/shard_map/ppermute | solution.py:49
  86.1 16.5 %collective-permute-start.16 = (bf16[4,8,80,128]{3,2,1,0:T(8,128)(2,1)S(1)}, bf16[4,8,80,128]{3,2,1,0:T(8,128)(2,1)S(1)}, u32[]{:S(2)}, u32[]{:S(2)}) collective-permute-start(bf16[4,8,80,128]{3,2,1,0:T(8,128)(2,1)S(1)} %add_convert_fusion.1), channel_id=1, source_target_pairs={{1,0},{2,1},{3,2},{0,3},{12,8},{13,9},{14,10},{15,11},{17,16},{18,... | collective-permute-start | bytes 1966088 | tf_op jit(solution)/shard_map/ppermute | solution.py:49
  103.1 6.6 %collective-permute-start.17 = (bf16[8,80,128]{2,1,0:T(8,128)(2,1)S(1)}, bf16[8,80,128]{2,1,0:T(8,128)(2,1)S(1)}, u32[]{:S(2)}, u32[]{:S(2)}) collective-permute-start(bf16[8,80,128]{2,1,0:T(8,128)(2,1)S(1)} %get-tuple-element.32), channel_id=1, source_target_pairs={{132,0},{133,1},{134,2},{135,3},{11,8},{8,9},{9,10},{10,11},{148,1... | collective-permute-start | bytes 491528 | tf_op jit(solution)/shard_map/ppermute | solution.py:49
  103.7 9.1 %collective-permute-start.18 = (bf16[8,80,128]{2,1,0:T(8,128)(2,1)S(1)}, bf16[8,80,128]{2,1,0:T(8,128)(2,1)S(1)}, u32[]{:S(2)}, u32[]{:S(2)}) collective-permute-start(bf16[8,80,128]{2,1,0:T(8,128)(2,1)S(1)} %get-tuple-element.34), channel_id=1, source_target_pairs={{128,0},{129,1},{130,2},{131,3},{10,8},{11,9},{8,10},{9,11},{144,1... | collective-permute-start | bytes 491528 | tf_op jit(solution)/shard_map/ppermute | solution.py:49
  107.8 5.3 %collective-permute-start.19 = (bf16[8,80,128]{2,1,0:T(8,128)(2,1)S(1)}, bf16[8,80,128]{2,1,0:T(8,128)(2,1)S(1)}, u32[]{:S(2)}, u32[]{:S(2)}) collective-permute-start(bf16[8,80,128]{2,1,0:T(8,128)(2,1)S(1)} %get-tuple-element.33), channel_id=1, source_target_pairs={{4,0},{5,1},{6,2},{7,3},{9,8},{10,9},{11,10},{8,11},{20,16},{21,17... | collective-permute-start | bytes 491528 | tf_op jit(solution)/shard_map/ppermute | solution.py:49
  113.9 17.0 %all-to-all-start.1 = ((bf16[8,80,128]{2,1,0:T(8,128)(2,1)}), bf16[8,80,128]{2,1,0:T(8,128)(2,1)S(1)}, u32[]{:S(2)}, u32[]{:S(2)}) async-start(bf16[8,80,128]{2,1,0:T(8,128)(2,1)} %fusion.2), calls=%async_computation.1 | async-start | bytes 327680 | tf_op jit(solution)/shard_map/all_to_all | solution.py:72
  (12 other events, 125.0 us)

commit v4 on v3

--- a/solution.py
+++ b/solution.py
@@ -22,7 +22,7 @@
 ROWS = 80
 BF = jnp.bfloat16
 F32 = jnp.float32
-VMEM_BYTES = 48 * 1024 * 1024
+VMEM_BYTES = 40 * 1024 * 1024
 BLOCKED = -1e30
 
 
@@ -60,7 +60,7 @@
     return pieces + [swap(piece) for piece in pieces]
 
 
-def scatter_blocks(pieces):
+def scatter_blocks(pieces, beside):
     summed = [
         (pieces[i].astype(F32) + swap(pieces[4 + i]).astype(F32)).astype(BF) for i in range(4)
     ]
@@ -68,9 +68,9 @@
         total = summed[0].astype(F32)
         for step in (1, 2, 3):
             total = total + shift(summed[step], along_x, -step).astype(F32)
-        summed = total.astype(BF)
+        summed, beside = lax.optimization_barrier((total.astype(BF), beside))
     parts = lax.all_to_all(summed, "z", 0, 0, tiled=True)
-    return jnp.sum(parts.astype(F32), axis=0)
+    return jnp.sum(parts.astype(F32), axis=0), beside
 
 
 def assembly(where, pieces, w_q, w_kv, w_o, sems):
@@ -116,7 +116,7 @@
     pieces, rest = rest[:8], rest[8:]
     grads, (mix, dq_t, dkv_t), rest = rest[:8], rest[8:11], rest[11:]
     (w_q, w_kv, w_o, normed, normed_t, cot_t, dm_t, q_t, k_t, v_t, k_n, v_n) = rest[:12]
-    (mix_t, dk_t, dv_t, bias, out, sems, out_sems) = rest[12:]
+    (mix_t, dk_t, dv_t, bias, out, sems) = rest[12:]
     copy_q, copy_kv, copy_o = assembly(where, pieces, w_q, w_kv, w_o, sems)
     begin(copy_o)
     begin(copy_q)
@@ -168,7 +168,7 @@
         k_n[n] = keys.T
         v_n[n] = values.T
 
-    @pl.loop(0, 8)
+    @pl.loop(0, 8, unroll=2)
     def _(step):
         head = lax.rem(step, 4)
         b = step // 4
@@ -179,30 +179,36 @@
         d_keys = jnp.zeros((SEQ, HD), F32)
         d_values = jnp.zeros((SEQ, HD), F32)
         blank = jnp.zeros((128, 128), BF)
+        places = [pl.ds(pl.multiple_of(head * 256 + h * HD, HD), HD) for h in range(GROUP)]
+        queries = [q_t[rows, at] for rows in places]
+        d_mixeds = [dm_t[rows, at] for rows in places]
+        scores = [dot(keys_n, query) for query in queries]
+        d_probs = [dot(values_n, d_mixed) for d_mixed in d_mixeds]
+        both = []
         for h in range(GROUP):
-            rows = pl.ds(pl.multiple_of(head * 256 + h * HD, HD), HD)
-            query = q_t[rows, at]
-            d_mixed = dm_t[rows, at]
-            scores = dot(keys_n, query)
-            d_prob = dot(values_n, d_mixed)
             probs, d_scores = [], []
             for length, columns in ((128, slice(0, 128)), (256, slice(128, 256))):
-                weight = jnp.exp(scores[:length, columns] + bias[b, pl.ds(0, length), columns])
+                weight = jnp.exp(scores[h][:length, columns] + bias[b, pl.ds(0, length), columns])
                 prob = weight * (1.0 / jnp.sum(weight, axis=0, keepdims=True))
-                back = d_prob[:length, columns]
+                back = d_probs[h][:length, columns]
                 inner = jnp.sum(prob * back, axis=0, keepdims=True)
                 probs.append(prob.astype(BF))
                 d_scores.append((prob * (back - inner)).astype(BF))
-            prob = jnp.concatenate([jnp.concatenate([probs[0], blank]), probs[1]], axis=1)
-            d_score = jnp.concatenate([jnp.concatenate([d_scores[0], blank]), d_scores[1]], axis=1)
+            both.append([
+                jnp.concatenate([jnp.concatenate([part[0], blank]), part[1]], axis=1)
+                for part in (probs, d_scores)
+            ])
+        for h in range(GROUP):
+            prob, d_score = both[h]
+            rows = places[h]
             mix_t[rows, at] = dot(values_t, prob).astype(BF)
             value = dot(keys_t, d_score)
             a, c = value[:HALF], value[HALF:]
             dq_t[rows, at] = jnp.concatenate(
                 [a * cos_b + c * sin_b, c * cos_b - a * sin_b]
             ).astype(BF)
-            d_keys = d_keys + dot(d_score, query.T)
-            d_values = d_values + dot(prob, d_mixed.T)
+            d_keys = d_keys + dot(d_score, queries[h].T)
+            d_values = d_values + dot(prob, d_mixeds[h].T)
         value = d_keys.T
         a, c = value[:HALF], value[HALF:]
         cos_b, sin_b = table[0, :, 0:SEQ], table[1, :, 0:SEQ]
@@ -216,7 +222,6 @@
         dkv_t[pl.ds(n * 128, 128), :] = both.astype(BF)
         mix[:, pl.ds(n * 256, 256)] = mix_t[pl.ds(n * 256, 256), :].T
 
-    c, x, y = where[0], where[1], where[2]
     for n in range(4):
         lanes = pl.ds(n * 256, 256)
         for left, right, start, count in (
@@ -228,20 +233,17 @@
             for high in range(2):
                 value = dot(left[pl.ds(high * size, size), :], right[:, lanes]).astype(BF)
                 value = value.reshape(8, 2, count, 256)
-                x_rel = lax.rem(high * 2 + n // 2 - x + 4, 4)
-                for i in range(2):
-                    y_rel = lax.rem(n % 2 * 2 + i - y + 4, 4)
-                    for core, (second, first) in enumerate(((y_rel, x_rel), (x_rel, y_rel))):
-                        c_rel = lax.rem(core - c + 2, 2)
-                        out[c_rel, second, first, :, pl.ds(start, count), :] = (
-                            value[:, core, :, i * 128 : (i + 1) * 128]
-                        )
-    copies = [
-        pltpu.make_async_copy(out.at[at // 4, at % 4], grads[at], out_sems.at[at])
-        for at in range(8)
-    ]
-    begin(copies)
-    finish(copies)
+                for core, i in itertools.product(range(2), range(2)):
+                    out[core, high * 2 + n // 2, n % 2 * 2 + i, :, pl.ds(start, count), :] = (
+                        value[:, core, :, i * 128 : (i + 1) * 128]
+                    )
+    c, x, y = where[0], where[1], where[2]
+    for at in range(32):
+        c_rel, second, first = at // 16, (at // 4) % 4, at % 4
+        core = lax.rem(c + c_rel, 2)
+        chip_x = lax.rem(x + first + core * (second - first), 4)
+        chip_y = lax.rem(y + second + core * (first - second), 4)
+        grads[c_rel * 4 + second][first] = out[core, chip_x, chip_y]
 
 
 def close(where, gain, hidden, cot, mix, dq_t, dkv_t, *rest):
@@ -314,7 +316,7 @@
         name="attend",
         out_shape=[PIECE] * 8 + shapes,
         in_specs=[SMEM, SMEM] + [VMEM] * 4 + [ANY] * 8,
-        out_specs=[ANY] * 8 + [VMEM] * 3,
+        out_specs=[VMEM] * 11,
         scratch_shapes=weights_scratch()
         + [
             scratch(TOKENS, D),
@@ -332,7 +334,6 @@
             scratch(2, SEQ, SEQ, dtype=F32),
             scratch(2, 4, 4, 8, ROWS, 128),
             pltpu.SemaphoreType.DMA((3, 32)),
-            pltpu.SemaphoreType.DMA((8,)),
         ],
         compiler_params=pltpu.CompilerParams(vmem_limit_bytes=VMEM_BYTES),
         cost_estimate=pl.CostEstimate(
@@ -340,7 +341,7 @@
         ),
     )(where, doc_lengths, gain, hidden, cotangent, table, *pieces)
     grads, (mix, dq_t, dkv_t) = results[:8], results[8:]
-    output, grad_hidden = pl.pallas_call(
+    beside = pl.pallas_call(
         close,
         name="close",
         out_shape=[jax.ShapeDtypeStruct((TOKENS, D), BF)] * 2,
@@ -358,7 +359,7 @@
             flops=3 * 10**9, bytes_accessed=15 * 10**6, transcendentals=0
         ),
     )(where, gain, hidden, cotangent, mix, dq_t, dkv_t, *pieces)
-    owned = scatter_blocks(grads)
+    owned, (output, grad_hidden) = scatter_blocks(grads, tuple(beside))
     return (
         output,
         grad_hidden,

time: 132 us -> 120 us (0.909)
  blocking collectives: 16.7 us -> 28.7 us
  Pallas kernels: 38.6 us -> 27.8 us
  starting transfers between devices: 26.3 us -> 20 us
  waiting for transfers between devices: 44.5 us -> 39.1 us
    all_to_all x0 -> x1, blocking collectives: none -> 12 us  [scatter_blocks(): parts = lax.all_to_all(summed, 'z', 0, 0, tiled=True)]
    pallas_call x1, Pallas kernels: 27.5 us -> 18.4 us  [local(): pl.pallas_call(attend, name='attend', out_shape=[PIECE] * 8 + shapes, in_...]
    ppermute x12, waiting for transfers between devices: 40.7 us -> 35.7 us  [shift(): return lax.ppermute(block, AXES, pairs)]
    all_to_all x1 -> x0, starting transfers between devices: 4.75 us -> none  [scatter_blocks(): parts = lax.all_to_all(summed, 'z', 0, 0, tiled=True)]
    pallas_call x1, Pallas kernels: 11.1 us -> 9.38 us  [local(): pl.pallas_call(close, name='close', out_shape=[jax.ShapeDtypeStruct((TOKE...]
    ppermute x12, starting transfers between devices: 19.9 us -> 18.3 us  [shift(): return lax.ppermute(block, AXES, pairs)]
  transfers between devices with their start and end apart: 21 -> 20, of which waited for: 12 -> 12; matrix products, arithmetic and copies ran while one was open for 0% -> 1% of each run, Pallas kernels for 8% -> 8%
where the time goes in v4:
time: 120 us
  waiting for transfers between devices  39.1 us (33%)
  blocking collectives  28.7 us (24%)
  Pallas kernels  27.8 us (23%)
  starting transfers between devices  20 us (17%)
  other arithmetic  2.09 us (2%)
  local copies, waits for them, and re-layouts  1.3 us (1%)
    ppermute x12, waiting for transfers between devices, shift(): return lax.ppermute(block, AXES, pairs)  35.7 us
    pallas_call x1, Pallas kernels, local(): pl.pallas_call(attend, name='attend', out_shape=[PIECE] * 8 + shapes, in_...  18.4 us
    ppermute x12, starting transfers between devices, shift(): return lax.ppermute(block, AXES, pairs)  18.3 us
    all_to_all x1, blocking collectives, gather_blocks(): lax.all_to_all(jnp.broadcast_to(block[None], (8, ROWS, 128)), 'z', 0, 0,...  16.7 us
    all_to_all x1, blocking collectives, scatter_blocks(): parts = lax.all_to_all(summed, 'z', 0, 0, tiled=True)  12 us
    pallas_call x1, Pallas kernels, local(): pl.pallas_call(close, name='close', out_shape=[jax.ShapeDtypeStruct((TOKE...  9.38 us
    ppermute x8, waiting for transfers between devices, swap(): return lax.ppermute(block, 'c', [(0, 1), (1, 0)])  3.44 us
  transfers between devices with their start and end apart: 20, of which 12 were waited for; matrix products, arithmetic and copies ran while one was open for 1% of the time, Pallas kernels for 8%

profile of v4, /device:TPU:32, one launch (start us, length us, event | category | flops | bytes accessed | tf_op | source)
XLA Modules:
  0.0 119.7 jit_solution(2783642585825407082)
XLA Ops:
  1.5 16.7 %all_to_all.10 = bf16[8,80,128]{2,1,0:T(8,128)(2,1)S(1)} all-to-all(bf16[8,80,128]{2,1,0:T(8,128)(2,1)S(1)} %broadcast_in_dim.2), channel_id=1, replica_groups=mesh['xh'=2,'z'=8,'c'=2,'xl'=2,'y'=4] {'z'}, dimensions={0} | all-to-all | bytes 327680 | tf_op jit(solution)/shard_map/all_to_all | solution.py:57
  18.2 1.5 %collective-permute-start.2 = (bf16[8,80,128]{2,1,0:T(8,128)(2,1)S(1)}, bf16[8,80,128]{2,1,0:T(8,128)(2,1)S(1)}, u32[]{:S(2)}, u32[]{:S(2)}) collective-permute-start(bf16[8,80,128]{2,1,0:T(8,128)(2,1)S(1)} %all_to_all.10), channel_id=1, source_target_pairs={{132,0},{133,1},{134,2},{135,3},{11,8},{8,9},{9,10},{10,11},{148,1... | collective-permute-start | bytes 491528 | tf_op jit(solution)/shard_map/ppermute | solution.py:49
  19.7 2.7 %collective-permute-start.1 = (bf16[8,80,128]{2,1,0:T(8,128)(2,1)S(1)}, bf16[8,80,128]{2,1,0:T(8,128)(2,1)S(1)}, u32[]{:S(2)}, u32[]{:S(2)}) collective-permute-start(bf16[8,80,128]{2,1,0:T(8,128)(2,1)S(1)} %all_to_all.10), channel_id=1, source_target_pairs={{128,0},{129,1},{130,2},{131,3},{10,8},{11,9},{8,10},{9,11},{144,1... | collective-permute-start | bytes 491528 | tf_op jit(solution)/shard_map/ppermute | solution.py:49
  22.4 1.4 %collective-permute-start = (bf16[8,80,128]{2,1,0:T(8,128)(2,1)S(1)}, bf16[8,80,128]{2,1,0:T(8,128)(2,1)S(1)}, u32[]{:S(2)}, u32[]{:S(2)}) collective-permute-start(bf16[8,80,128]{2,1,0:T(8,128)(2,1)S(1)} %all_to_all.10), channel_id=1, source_target_pairs={{4,0},{5,1},{6,2},{7,3},{9,8},{10,9},{11,10},{8,11},{20,16},{21,17... | collective-permute-start | bytes 491528 | tf_op jit(solution)/shard_map/ppermute | solution.py:49
  23.9 0.9 collective-permute-done.2
  24.8 2.7 %collective-permute-done.1 = bf16[8,80,128]{2,1,0:T(8,128)(2,1)S(1)} collective-permute-done((bf16[8,80,128]{2,1,0:T(8,128)(2,1)S(1)}, bf16[8,80,128]{2,1,0:T(8,128)(2,1)S(1)}, u32[]{:S(2)}, u32[]{:S(2)}) %collective-permute-start.1) | collective-permute-done | bytes 163872 | tf_op jit(solution)/shard_map/ppermute | solution.py:49
  28.0 3.6 %collective-permute-start.3 = (bf16[4,8,80,128]{3,2,1,0:T(8,128)(2,1)S(1)}, bf16[4,8,80,128]{3,2,1,0:T(8,128)(2,1)S(1)}, u32[]{:S(2)}, u32[]{:S(2)}) collective-permute-start(bf16[4,8,80,128]{3,2,1,0:T(8,128)(2,1)S(1)} %pad_maximum_fusion.rest_0_), channel_id=1, source_target_pairs={{1,0},{2,1},{3,2},{0,3},{12,8},{13,9},{14,10},{15,11},{17,16},{18,... | collective-permute-start | bytes 1966088 | tf_op jit(solution)/shard_map/ppermute | solution.py:49
  31.8 1.2 collective-permute-start.5
  33.0 13.7 %collective-permute-done.3.rest_1_ = bf16[4,8,80,128]{3,2,1,0:T(8,128)(2,1)S(1)} collective-permute-done((bf16[4,8,80,128]{3,2,1,0:T(8,128)(2,1)S(1)}, bf16[4,8,80,128]{3,2,1,0:T(8,128)(2,1)S(1)}, u32[]{:S(2)}, u32[]{:S(2)}) %collective-permute-start.3) | collective-permute-done | bytes 655392 | tf_op jit(solution)/shard_map/ppermute | solution.py:49
  47.2 3.6 %collective-permute-done.5.rest_3_ = bf16[4,8,80,128]{3,2,1,0:T(8,128)(2,1)} collective-permute-done((bf16[4,8,80,128]{3,2,1,0:T(8,128)(2,1)S(1)}, bf16[4,8,80,128]{3,2,1,0:T(8,128)(2,1)}, u32[]{:S(2)}, u32[]{:S(2)}) %collective-permute-start.5) | collective-permute-done | bytes 655392 | tf_op jit(solution)/shard_map/ppermute | solution.py:49
  50.9 2.3 %collective-permute-done.9.rest_7_ = bf16[4,8,80,128]{3,2,1,0:T(8,128)(2,1)} collective-permute-done((bf16[4,8,80,128]{3,2,1,0:T(8,128)(2,1)}, bf16[4,8,80,128]{3,2,1,0:T(8,128)(2,1)}, u32[]{:S(2)}, u32[]{:S(2)}) %collective-permute-start.9) | collective-permute-done | bytes 655392 | tf_op jit(solution)/shard_map/ppermute | solution.py:53
  53.2 18.4 %attend.1 = (bf16[4,8,80,128]{3,2,1,0:T(8,128)(2,1)S(1)}, bf16[4,8,80,128]{3,2,1,0:T(8,128)(2,1)S(1)}, bf16[4,8,80,128]{3,2,1,0:T(8,128)(2,1)S(1)}, bf16[4,8,80,...) custom-call(s32[3]{0:T(128)S(1)} %pad_add_fusion.where, ...), custom_call_target="tpu_custom_call" | custom-call | flops 7000000000 | bytes 20000000 | tf_op jit(solution)/shard_map/attend/pallas_call | solution.py:314
  72.8 1.1 collective-permute-done.15
  74.0 1.6 %collective-permute-start.16 = (bf16[4,8,80,128]{3,2,1,0:T(8,128)(2,1)S(1)}, bf16[4,8,80,128]{3,2,1,0:T(8,128)(2,1)S(1)}, u32[]{:S(2)}, u32[]{:S(2)}) collective-permute-start(bf16[4,8,80,128]{3,2,1,0:T(8,128)(2,1)S(1)} %add_convert_fusion.1), channel_id=1, source_target_pairs={{1,0},{2,1},{3,2},{0,3},{12,8},{13,9},{14,10},{15,11},{17,16},{18,... | collective-permute-start | bytes 1966088 | tf_op jit(solution)/shard_map/ppermute | solution.py:49
  76.3 1.6 %collective-permute-start.12 = (bf16[4,8,80,128]{3,2,1,0:T(8,128)(2,1)S(1)}, bf16[4,8,80,128]{3,2,1,0:T(8,128)(2,1)S(1)}, u32[]{:S(2)}, u32[]{:S(2)}) collective-permute-start(bf16[4,8,80,128]{3,2,1,0:T(8,128)(2,1)S(1)} %add_convert_fusion.3), channel_id=1, source_target_pairs={{3,0},{0,1},{1,2},{2,3},{140,8},{141,9},{142,10},{143,11},{19,16},... | collective-permute-start | bytes 1966088 | tf_op jit(solution)/shard_map/ppermute | solution.py:49
  77.9 9.4 %close.1 = (bf16[512,1024]{1,0:T(8,128)(2,1)}, bf16[512,1024]{1,0:T(8,128)(2,1)}) custom-call(s32[3]{0:T(128)S(1)} %pad_add_fusion.where, f32[1,1024]{1,0:T(1,128)S(1)} %bitcast.30, bf16[512,1024]{1,0:T(8,128)(2,1)S(1)} %copy-done, bf16[512,1024]{1,0:T(8,128)(2,1)S(1)} %copy-done.1, bf16[512,1024]{1,0:T(8,128)(2,1)S(1)} %get-tuple-element.33.mix, ...), custom_call_target="tpu_custom_call" | custom-call | flops 3000000000 | bytes 15000000 | tf_op jit(solution)/shard_map/close/pallas_call | solution.py:344
  87.3 1.0 collective-permute-done.14
  88.3 6.9 %collective-permute-done.12 = bf16[4,8,80,128]{3,2,1,0:T(8,128)(2,1)S(1)} collective-permute-done((bf16[4,8,80,128]{3,2,1,0:T(8,128)(2,1)S(1)}, bf16[4,8,80,128]{3,2,1,0:T(8,128)(2,1)S(1)}, u32[]{:S(2)}, u32[]{:S(2)}) %collective-permute-start.12) | collective-permute-done | bytes 655392 | tf_op jit(solution)/shard_map/ppermute | solution.py:49
  95.7 2.1 %collective-permute-start.19 = (bf16[8,80,128]{2,1,0:T(8,128)(2,1)S(1)}, bf16[8,80,128]{2,1,0:T(8,128)(2,1)S(1)}, u32[]{:S(2)}, u32[]{:S(2)}) collective-permute-start(bf16[8,80,128]{2,1,0:T(8,128)(2,1)S(1)} %get-tuple-element.45), channel_id=1, source_target_pairs={{4,0},{5,1},{6,2},{7,3},{9,8},{10,9},{11,10},{8,11},{20,16},{21,17... | collective-permute-start | bytes 491528 | tf_op jit(solution)/shard_map/ppermute | solution.py:49
  97.8 2.0 %collective-permute-start.18 = (bf16[8,80,128]{2,1,0:T(8,128)(2,1)S(1)}, bf16[8,80,128]{2,1,0:T(8,128)(2,1)S(1)}, u32[]{:S(2)}, u32[]{:S(2)}) collective-permute-start(bf16[8,80,128]{2,1,0:T(8,128)(2,1)S(1)} %get-tuple-element.46), channel_id=1, source_target_pairs={{128,0},{129,1},{130,2},{131,3},{10,8},{11,9},{8,10},{9,11},{144,1... | collective-permute-start | bytes 491528 | tf_op jit(solution)/shard_map/ppermute | solution.py:49
  99.9 2.6 %collective-permute-done.19 = bf16[8,80,128]{2,1,0:T(8,128)(2,1)S(1)} collective-permute-done((bf16[8,80,128]{2,1,0:T(8,128)(2,1)S(1)}, bf16[8,80,128]{2,1,0:T(8,128)(2,1)S(1)}, u32[]{:S(2)}, u32[]{:S(2)}) %collective-permute-start.19) | collective-permute-done | bytes 163872 | tf_op jit(solution)/shard_map/ppermute | solution.py:49
  102.4 2.2 %collective-permute-done.18 = bf16[8,80,128]{2,1,0:T(8,128)(2,1)S(1)} collective-permute-done((bf16[8,80,128]{2,1,0:T(8,128)(2,1)S(1)}, bf16[8,80,128]{2,1,0:T(8,128)(2,1)S(1)}, u32[]{:S(2)}, u32[]{:S(2)}) %collective-permute-start.18) | collective-permute-done | bytes 163872 | tf_op jit(solution)/shard_map/ppermute | solution.py:49
  104.6 1.8 %collective-permute-done.17 = bf16[8,80,128]{2,1,0:T(8,128)(2,1)S(1)} collective-permute-done((bf16[8,80,128]{2,1,0:T(8,128)(2,1)S(1)}, bf16[8,80,128]{2,1,0:T(8,128)(2,1)S(1)}, u32[]{:S(2)}, u32[]{:S(2)}) %collective-permute-start.17) | collective-permute-done | bytes 163872 | tf_op jit(solution)/shard_map/ppermute | solution.py:49
  106.5 12.0 %all_to_all.11 = bf16[8,80,128]{2,1,0:T(8,128)(2,1)S(1)} all-to-all(bf16[8,80,128]{2,1,0:T(8,128)(2,1)S(1)} %fusion.2), channel_id=1, replica_groups=mesh['xh'=2,'z'=8,'c'=2,'xl'=2,'y'=4] {'z'}, dimensions={0} | all-to-all | bytes 327680 | tf_op jit(solution)/shard_map/all_to_all | solution.py:72
  (43 shorter events, 6.0 us)
Async XLA Ops:
  0.6 52.6 %copy-start.4 = (f32[2,32,512]{2,1,0:T(8,128)S(1)}, f32[2,32,512]{2,1,0:T(8,128)}, u32[]{:S(2)}) copy-start(f32[2,32,512]{2,1,0:T(8,128)} %constant.22.clone.table) | copy-start | bytes 393220
  0.6 52.6 %copy-start.3 = (s32[2,4]{1,0:T(2,128)S(1)}, s32[2,4]{1,0:T(2,128)}, u32[]{:S(2)}) copy-start(s32[2,4]{1,0:T(2,128)} %docs.1) | copy-start | bytes 100
  0.7 52.6 %copy-start.2 = (f32[1024]{0:T(1024)S(1)}, f32[1024]{0:T(1024)}, u32[]{:S(2)}) copy-start(f32[1024]{0:T(1024)} %param.10) | copy-start | bytes 12292
  0.7 52.5 %copy-start = (bf16[512,1024]{1,0:T(8,128)(2,1)S(1)}, bf16[512,1024]{1,0:T(8,128)(2,1)}, u32[]{:S(2)}) copy-start(bf16[512,1024]{1,0:T(8,128)(2,1)} %hidden.3) | copy-start | bytes 3145732
  18.2 6.5 %collective-permute-start.2 = (bf16[8,80,128]{2,1,0:T(8,128)(2,1)S(1)}, bf16[8,80,128]{2,1,0:T(8,128)(2,1)S(1)}, u32[]{:S(2)}, u32[]{:S(2)}) collective-permute-start(bf16[8,80,128]{2,1,0:T(8,128)(2,1)S(1)} %all_to_all.10), channel_id=1, source_target_pairs={{132,0},{133,1},{134,2},{135,3},{11,8},{8,9},{9,10},{10,11},{148,1... | collective-permute-start | bytes 491528 | tf_op jit(solution)/shard_map/ppermute | solution.py:49
  19.7 7.8 %collective-permute-start.1 = (bf16[8,80,128]{2,1,0:T(8,128)(2,1)S(1)}, bf16[8,80,128]{2,1,0:T(8,128)(2,1)S(1)}, u32[]{:S(2)}, u32[]{:S(2)}) collective-permute-start(bf16[8,80,128]{2,1,0:T(8,128)(2,1)S(1)} %all_to_all.10), channel_id=1, source_target_pairs={{128,0},{129,1},{130,2},{131,3},{10,8},{11,9},{8,10},{9,11},{144,1... | collective-permute-start | bytes 491528 | tf_op jit(solution)/shard_map/ppermute | solution.py:49
  22.4 5.4 %collective-permute-start = (bf16[8,80,128]{2,1,0:T(8,128)(2,1)S(1)}, bf16[8,80,128]{2,1,0:T(8,128)(2,1)S(1)}, u32[]{:S(2)}, u32[]{:S(2)}) collective-permute-start(bf16[8,80,128]{2,1,0:T(8,128)(2,1)S(1)} %all_to_all.10), channel_id=1, source_target_pairs={{4,0},{5,1},{6,2},{7,3},{9,8},{10,9},{11,10},{8,11},{20,16},{21,17... | collective-permute-start | bytes 491528 | tf_op jit(solution)/shard_map/ppermute | solution.py:49
  28.0 18.7 %collective-permute-start.3 = (bf16[4,8,80,128]{3,2,1,0:T(8,128)(2,1)S(1)}, bf16[4,8,80,128]{3,2,1,0:T(8,128)(2,1)S(1)}, u32[]{:S(2)}, u32[]{:S(2)}) collective-permute-start(bf16[4,8,80,128]{3,2,1,0:T(8,128)(2,1)S(1)} %pad_maximum_fusion.rest_0_), channel_id=1, source_target_pairs={{1,0},{2,1},{3,2},{0,3},{12,8},{13,9},{14,10},{15,11},{17,16},{18,... | collective-permute-start | bytes 1966088 | tf_op jit(solution)/shard_map/ppermute | solution.py:49
  31.6 15.1 %collective-permute-start.4 = (bf16[4,8,80,128]{3,2,1,0:T(8,128)(2,1)S(1)}, bf16[4,8,80,128]{3,2,1,0:T(8,128)(2,1)S(1)}, u32[]{:S(2)}, u32[]{:S(2)}) collective-permute-start(bf16[4,8,80,128]{3,2,1,0:T(8,128)(2,1)S(1)} %pad_maximum_fusion.rest_0_), channel_id=1, source_target_pairs={{2,0},{3,1},{0,2},{1,3},{136,8},{137,9},{138,10},{139,11},{18,16},... | collective-permute-start | bytes 1966088 | tf_op jit(solution)/shard_map/ppermute | solution.py:49
  31.8 18.9 %collective-permute-start.5 = (bf16[4,8,80,128]{3,2,1,0:T(8,128)(2,1)S(1)}, bf16[4,8,80,128]{3,2,1,0:T(8,128)(2,1)}, u32[]{:S(2)}, u32[]{:S(2)}) collective-permute-start(bf16[4,8,80,128]{3,2,1,0:T(8,128)(2,1)S(1)} %pad_maximum_fusion.rest_0_), channel_id=1, source_target_pairs={{3,0},{0,1},{1,2},{2,3},{140,8},{141,9},{142,10},{143,11},{19,16},... | collective-permute-start | bytes 1966088 | tf_op jit(solution)/shard_map/ppermute | solution.py:49
  33.0 17.8 %collective-permute-start.6 = (bf16[4,8,80,128]{3,2,1,0:T(8,128)(2,1)S(1)}, bf16[4,8,80,128]{3,2,1,0:T(8,128)(2,1)}, u32[]{:S(2)}, u32[]{:S(2)}) collective-permute-start(bf16[4,8,80,128]{3,2,1,0:T(8,128)(2,1)S(1)} %pad_maximum_fusion.rest_0_), channel_id=1, source_target_pairs={{0,8},{8,0},{1,9},{9,1},{2,10},{10,2},{3,11},{11,3},{4,12},{12,4},... | collective-permute-start | bytes 1966088 | tf_op jit(solution)/shard_map/ppermute | solution.py:53
  46.7 4.2 %collective-permute-start.7 = (bf16[4,8,80,128]{3,2,1,0:T(8,128)(2,1)S(1)}, bf16[4,8,80,128]{3,2,1,0:T(8,128)(2,1)}, u32[]{:S(2)}, u32[]{:S(2)}) collective-permute-start(bf16[4,8,80,128]{3,2,1,0:T(8,128)(2,1)S(1)} %collective-permute-done.3.rest_1_), channel_id=1, source_target_pairs={{0,8},{8,0},{1,9},{9,1},{2,10},{10,2},{3,11},{11,3},{4,12},{12,4},... | collective-permute-start | bytes 1966088 | tf_op jit(solution)/shard_map/ppermute | solution.py:53
  46.7 4.2 %collective-permute-start.8 = (bf16[4,8,80,128]{3,2,1,0:T(8,128)(2,1)S(1)}, bf16[4,8,80,128]{3,2,1,0:T(8,128)(2,1)}, u32[]{:S(2)}, u32[]{:S(2)}) collective-permute-start(bf16[4,8,80,128]{3,2,1,0:T(8,128)(2,1)S(1)} %collective-permute-done.4.rest_2_), channel_id=1, source_target_pairs={{0,8},{8,0},{1,9},{9,1},{2,10},{10,2},{3,11},{11,3},{4,12},{12,4},... | collective-permute-start | bytes 1966088 | tf_op jit(solution)/shard_map/ppermute | solution.py:53
  50.8 2.4 %collective-permute-start.9 = (bf16[4,8,80,128]{3,2,1,0:T(8,128)(2,1)}, bf16[4,8,80,128]{3,2,1,0:T(8,128)(2,1)}, u32[]{:S(2)}, u32[]{:S(2)}) collective-permute-start(bf16[4,8,80,128]{3,2,1,0:T(8,128)(2,1)} %collective-permute-done.5.rest_3_), channel_id=1, source_target_pairs={{0,8},{8,0},{1,9},{9,1},{2,10},{10,2},{3,11},{11,3},{4,12},{12,4},... | collective-permute-start | bytes 1966088 | tf_op jit(solution)/shard_map/ppermute | solution.py:53
  71.7 2.2 %collective-permute-start.15 = (bf16[4,8,80,128]{3,2,1,0:T(8,128)(2,1)S(1)}, bf16[4,8,80,128]{3,2,1,0:T(8,128)(2,1)S(1)}, u32[]{:S(2)}, u32[]{:S(2)}) collective-permute-start(bf16[4,8,80,128]{3,2,1,0:T(8,128)(2,1)S(1)} %get-tuple-element.32), channel_id=1, source_target_pairs={{0,8},{8,0},{1,9},{9,1},{2,10},{10,2},{3,11},{11,3},{4,12},{12,4},... | collective-permute-start | bytes 1966088 | tf_op jit(solution)/shard_map/ppermute | solution.py:53
  71.9 3.7 %collective-permute-start.13 = (bf16[4,8,80,128]{3,2,1,0:T(8,128)(2,1)S(1)}, bf16[4,8,80,128]{3,2,1,0:T(8,128)(2,1)S(1)}, u32[]{:S(2)}, u32[]{:S(2)}) collective-permute-start(bf16[4,8,80,128]{3,2,1,0:T(8,128)(2,1)S(1)} %get-tuple-element.30), channel_id=1, source_target_pairs={{0,8},{8,0},{1,9},{9,1},{2,10},{10,2},{3,11},{11,3},{4,12},{12,4},... | collective-permute-start | bytes 1966088 | tf_op jit(solution)/shard_map/ppermute | solution.py:53
  72.3 3.9 %collective-permute-start.11 = (bf16[4,8,80,128]{3,2,1,0:T(8,128)(2,1)S(1)}, bf16[4,8,80,128]{3,2,1,0:T(8,128)(2,1)S(1)}, u32[]{:S(2)}, u32[]{:S(2)}) collective-permute-start(bf16[4,8,80,128]{3,2,1,0:T(8,128)(2,1)S(1)} %get-tuple-element.28), channel_id=1, source_target_pairs={{0,8},{8,0},{1,9},{9,1},{2,10},{10,2},{3,11},{11,3},{4,12},{12,4},... | collective-permute-start | bytes 1966088 | tf_op jit(solution)/shard_map/ppermute | solution.py:53
  72.4 14.9 %collective-permute-start.10 = (bf16[4,8,80,128]{3,2,1,0:T(8,128)(2,1)S(1)}, bf16[4,8,80,128]{3,2,1,0:T(8,128)(2,1)S(1)}, u32[]{:S(2)}, u32[]{:S(2)}) collective-permute-start(bf16[4,8,80,128]{3,2,1,0:T(8,128)(2,1)S(1)} %get-tuple-element.26), channel_id=1, source_target_pairs={{0,8},{8,0},{1,9},{9,1},{2,10},{10,2},{3,11},{11,3},{4,12},{12,4},... | collective-permute-start | bytes 1966088 | tf_op jit(solution)/shard_map/ppermute | solution.py:53
  74.0 13.3 %collective-permute-start.16 = (bf16[4,8,80,128]{3,2,1,0:T(8,128)(2,1)S(1)}, bf16[4,8,80,128]{3,2,1,0:T(8,128)(2,1)S(1)}, u32[]{:S(2)}, u32[]{:S(2)}) collective-permute-start(bf16[4,8,80,128]{3,2,1,0:T(8,128)(2,1)S(1)} %add_convert_fusion.1), channel_id=1, source_target_pairs={{1,0},{2,1},{3,2},{0,3},{12,8},{13,9},{14,10},{15,11},{17,16},{18,... | collective-permute-start | bytes 1966088 | tf_op jit(solution)/shard_map/ppermute | solution.py:49
  75.8 12.5 %collective-permute-start.14 = (bf16[4,8,80,128]{3,2,1,0:T(8,128)(2,1)S(1)}, bf16[4,8,80,128]{3,2,1,0:T(8,128)(2,1)S(1)}, u32[]{:S(2)}, u32[]{:S(2)}) collective-permute-start(bf16[4,8,80,128]{3,2,1,0:T(8,128)(2,1)S(1)} %add_convert_fusion.2), channel_id=1, source_target_pairs={{2,0},{3,1},{0,2},{1,3},{136,8},{137,9},{138,10},{139,11},{18,16},... | collective-permute-start | bytes 1966088 | tf_op jit(solution)/shard_map/ppermute | solution.py:49
  76.3 18.9 %collective-permute-start.12 = (bf16[4,8,80,128]{3,2,1,0:T(8,128)(2,1)S(1)}, bf16[4,8,80,128]{3,2,1,0:T(8,128)(2,1)S(1)}, u32[]{:S(2)}, u32[]{:S(2)}) collective-permute-start(bf16[4,8,80,128]{3,2,1,0:T(8,128)(2,1)S(1)} %add_convert_fusion.3), channel_id=1, source_target_pairs={{3,0},{0,1},{1,2},{2,3},{140,8},{141,9},{142,10},{143,11},{19,16},... | collective-permute-start | bytes 1966088 | tf_op jit(solution)/shard_map/ppermute | solution.py:49
  95.7 6.7 %collective-permute-start.19 = (bf16[8,80,128]{2,1,0:T(8,128)(2,1)S(1)}, bf16[8,80,128]{2,1,0:T(8,128)(2,1)S(1)}, u32[]{:S(2)}, u32[]{:S(2)}) collective-permute-start(bf16[8,80,128]{2,1,0:T(8,128)(2,1)S(1)} %get-tuple-element.45), channel_id=1, source_target_pairs={{4,0},{5,1},{6,2},{7,3},{9,8},{10,9},{11,10},{8,11},{20,16},{21,17... | collective-permute-start | bytes 491528 | tf_op jit(solution)/shard_map/ppermute | solution.py:49
  97.8 6.8 %collective-permute-start.18 = (bf16[8,80,128]{2,1,0:T(8,128)(2,1)S(1)}, bf16[8,80,128]{2,1,0:T(8,128)(2,1)S(1)}, u32[]{:S(2)}, u32[]{:S(2)}) collective-permute-start(bf16[8,80,128]{2,1,0:T(8,128)(2,1)S(1)} %get-tuple-element.46), channel_id=1, source_target_pairs={{128,0},{129,1},{130,2},{131,3},{10,8},{11,9},{8,10},{9,11},{144,1... | collective-permute-start | bytes 491528 | tf_op jit(solution)/shard_map/ppermute | solution.py:49
  99.9 6.5 %collective-permute-start.17 = (bf16[8,80,128]{2,1,0:T(8,128)(2,1)S(1)}, bf16[8,80,128]{2,1,0:T(8,128)(2,1)S(1)}, u32[]{:S(2)}, u32[]{:S(2)}) collective-permute-start(bf16[8,80,128]{2,1,0:T(8,128)(2,1)S(1)} %get-tuple-element.44), channel_id=1, source_target_pairs={{132,0},{133,1},{134,2},{135,3},{11,8},{8,9},{9,10},{10,11},{148,1... | collective-permute-start | bytes 491528 | tf_op jit(solution)/shard_map/ppermute | solution.py:49
  (1 other events, 2.1 us)

commit v5 on v4

--- a/solution.py
+++ b/solution.py
@@ -53,11 +53,12 @@
     return lax.ppermute(block, "c", [(0, 1), (1, 0)])
 
 
-def gather_blocks(block):
+def gather_blocks(block, ready):
     mine = lax.all_to_all(jnp.broadcast_to(block[None], (8, ROWS, 128)), "z", 0, 0, tiled=True)
     first = jnp.stack([mine] + [shift(mine, 0, step) for step in (1, 2, 3)])
     pieces = [first] + [shift(first, 1, step) for step in (1, 2, 3)]
-    return pieces + [swap(piece) for piece in pieces]
+    pieces[3], ready = lax.optimization_barrier((pieces[3], ready))
+    return pieces + [swap(piece) for piece in pieces], ready
 
 
 def scatter_blocks(pieces, beside):
@@ -97,6 +98,21 @@
     return copies
 
 
+def assemble(where, pieces, w_q, w_kv, w_o):
+    c, x, y = where[0], where[1], where[2]
+    for at in range(32):
+        c_rel, second, first = at // 16, (at // 4) % 4, at % 4
+        core = lax.rem(c + c_rel, 2)
+        chip_x = lax.rem(x + first + core * (second - first), 4)
+        chip_y = lax.rem(y + second + core * (first - second), 4)
+        high, node = chip_x // 2, lax.rem(chip_x, 2) * 4 + chip_y
+        lanes = pl.ds(pl.multiple_of(node * 128, 128), 128)
+        piece = pieces[c_rel * 4 + second]
+        w_q[high, :, core, :, lanes] = piece[first, :, 0:32, :]
+        w_kv[high, :, core, :, lanes] = piece[first, :, 32:48, :]
+        w_o[high, :, core, :, lanes] = piece[first, :, 48:80, :]
+
+
 def begin(copies):
     for copy in copies:
         copy.start()
@@ -112,16 +128,7 @@
     return rows * inverse, inverse
 
 
-def attend(where, docs, gain, hidden, cot, table, *rest):
-    pieces, rest = rest[:8], rest[8:]
-    grads, (mix, dq_t, dkv_t), rest = rest[:8], rest[8:11], rest[11:]
-    (w_q, w_kv, w_o, normed, normed_t, cot_t, dm_t, q_t, k_t, v_t, k_n, v_n) = rest[:12]
-    (mix_t, dk_t, dv_t, bias, out, sems) = rest[12:]
-    copy_q, copy_kv, copy_o = assembly(where, pieces, w_q, w_kv, w_o, sems)
-    begin(copy_o)
-    begin(copy_q)
-    begin(copy_kv)
-
+def prepare(docs, gain, hidden, cot, normed, normed_t, cot_t, bias):
     @pl.loop(0, TOKENS // 128)
     def _(step):
         at = pl.ds(pl.multiple_of(step * 128, 128), 128)
@@ -141,13 +148,19 @@
         allowed = jnp.logical_and(doc_q == doc_s, places_s <= places_q)
         bias[b] = jnp.where(allowed, 0.0, BLOCKED)
 
-    finish(copy_o)
+
+def attend(where, cot, table, normed, normed_t, cot_t, bias, *rest):
+    pieces, rest = rest[:8], rest[8:]
+    grads, (mix, dq_t, dkv_t), rest = rest[:8], rest[8:11], rest[11:]
+    (w_q, w_kv, w_o, dm_t, q_t, k_t, v_t, k_n, v_n) = rest[:9]
+    (mix_t, dk_t, dv_t, out) = rest[9:]
+
+    assemble(where, pieces, w_q, w_kv, w_o)
     for n in range(4):
         columns = w_o[:, :, :, :, pl.ds(n * 256, 256)].reshape(D, 256)
         dm_t[pl.ds(n * 256, 256), :] = dot(cot[...], columns).astype(BF).T
 
     cos, sin = table[0], table[1]
-    finish(copy_q)
     for n in range(4):
         rows = w_q[n // 2, pl.ds(n % 2 * 4, 4)].reshape(256, D)
         value = dot(rows, normed_t[...]) * 0.125
@@ -155,7 +168,6 @@
             a, b = value[h * HD : h * HD + HALF], value[h * HD + HALF : (h + 1) * HD]
             q_t[pl.ds(n * 256 + h * HD, HALF), :] = (a * cos - b * sin).astype(BF)
             q_t[pl.ds(n * 256 + h * HD + HALF, HALF), :] = (a * sin + b * cos).astype(BF)
-    finish(copy_kv)
     for n in range(4):
         rows = w_kv[n // 2, pl.ds(n % 2 * 4, 4)].reshape(128, D)
         value = dot(rows, normed_t[...]).reshape(8, 2, 8, TOKENS)
@@ -302,7 +314,6 @@
 
 def local(hidden, norm_gain, w_query, w_key, w_value, w_out, doc_lengths, cotangent):
     block = jnp.concatenate([w_query.T, w_key.T, w_value.T, w_out.T], axis=0)
-    pieces = gather_blocks(block)
     where = jnp.stack([lax.axis_index(name) for name in ("c", X, "y")])
     gain = norm_gain.reshape(1, D)
     table = jnp.asarray(tables())
@@ -311,17 +322,28 @@
         jax.ShapeDtypeStruct((D, TOKENS), BF),
         jax.ShapeDtypeStruct((2 * KV, TOKENS), BF),
     ]
+    ready = pl.pallas_call(
+        prepare,
+        name="prepare",
+        out_shape=[
+            pltpu.VMEM((TOKENS, D), BF),
+            pltpu.VMEM((D, TOKENS), BF),
+            pltpu.VMEM((D, TOKENS), BF),
+            pltpu.VMEM((2, SEQ, SEQ), F32),
+        ],
+        in_specs=[SMEM, VMEM, VMEM, VMEM],
+        out_specs=[VMEM] * 4,
+        compiler_params=pltpu.CompilerParams(vmem_limit_bytes=VMEM_BYTES // 2),
+    )(doc_lengths, gain, hidden, cotangent)
+    pieces, ready = gather_blocks(block, tuple(ready))
     results = pl.pallas_call(
         attend,
         name="attend",
         out_shape=[PIECE] * 8 + shapes,
-        in_specs=[SMEM, SMEM] + [VMEM] * 4 + [ANY] * 8,
+        in_specs=[SMEM] + [VMEM] * 14,
         out_specs=[VMEM] * 11,
         scratch_shapes=weights_scratch()
         + [
-            scratch(TOKENS, D),
-            scratch(D, TOKENS),
-            scratch(D, TOKENS),
             scratch(D, TOKENS),
             scratch(D, TOKENS),
             scratch(4, HD, TOKENS),
@@ -331,15 +353,13 @@
             scratch(D, TOKENS),
             scratch(4, HD, TOKENS, dtype=F32),
             scratch(4, HD, TOKENS, dtype=F32),
-            scratch(2, SEQ, SEQ, dtype=F32),
             scratch(2, 4, 4, 8, ROWS, 128),
-            pltpu.SemaphoreType.DMA((3, 32)),
         ],
         compiler_params=pltpu.CompilerParams(vmem_limit_bytes=VMEM_BYTES),
         cost_estimate=pl.CostEstimate(
             flops=7 * 10**9, bytes_accessed=20 * 10**6, transcendentals=2 * 10**6
         ),
-    )(where, doc_lengths, gain, hidden, cotangent, table, *pieces)
+    )(where, cotangent, table, *ready, *[pltpu.with_memory_space_constraint(p, pltpu.VMEM) for p in pieces])
     grads, (mix, dq_t, dkv_t) = results[:8], results[8:]
     beside = pl.pallas_call(
         close,

time: 120 us -> 119 us (level); the launches traced: 120 us -> 117 us
  waiting for transfers between devices: 39.1 us -> 27 us
  local copies, waits for them, and re-layouts: 1.3 us -> 6.33 us
  starting transfers between devices: 20 us -> 23.2 us
    ppermute x12, waiting for transfers between devices: 35.7 us -> 22.4 us  [shift(): return lax.ppermute(block, AXES, pairs)]
    unnamed x10 -> x18, local copies, waits for them, and re-layouts: 0.03 us -> 5.05 us
    ppermute x12, starting transfers between devices: 18.3 us -> 21.6 us  [shift(): return lax.ppermute(block, AXES, pairs)]
    pallas_call x0 -> x1, Pallas kernels: none -> 1.95 us  [local(): pl.pallas_call(prepare, name='prepare', out_shape=[pltpu.VMEM((TOKENS, D)...]
  transfers between devices with their start and end apart: 20 -> 20, of which waited for: 12 -> 13; matrix products, arithmetic and copies ran while one was open for 1% -> 1% of each run, Pallas kernels for 8% -> 10%
where the time goes in v5:
time: 119 us; the launch traced here: 117 us
  Pallas kernels  29 us (24%)
  blocking collectives  28.5 us (24%)
  waiting for transfers between devices  27 us (23%)
  starting transfers between devices  23.2 us (19%)
  local copies, waits for them, and re-layouts  6.33 us (5%)
  other arithmetic  2.09 us (2%)
    ppermute x12, waiting for transfers between devices, shift(): return lax.ppermute(block, AXES, pairs)  22.4 us
    ppermute x12, starting transfers between devices, shift(): return lax.ppermute(block, AXES, pairs)  21.6 us
    pallas_call x1, Pallas kernels, local(): pl.pallas_call(attend, name='attend', out_shape=[PIECE] * 8 + shapes, in_...  17.7 us
    all_to_all x1, blocking collectives, gather_blocks(): lax.all_to_all(jnp.broadcast_to(block[None], (8, ROWS, 128)), 'z', 0, 0,...  16.7 us
    all_to_all x1, blocking collectives, scatter_blocks(): parts = lax.all_to_all(summed, 'z', 0, 0, tiled=True)  11.8 us
    pallas_call x1, Pallas kernels, local(): pl.pallas_call(close, name='close', out_shape=[jax.ShapeDtypeStruct((TOKE...  9.3 us
    unnamed x18, local copies, waits for them, and re-layouts  5.05 us
    ppermute x8, waiting for transfers between devices, swap(): return lax.ppermute(block, 'c', [(0, 1), (1, 0)])  4.59 us
  transfers between devices with their start and end apart: 20, of which 13 were waited for; matrix products, arithmetic and copies ran while one was open for 1% of the time, Pallas kernels for 10%

profile of v5, /device:TPU:32, one launch (start us, length us, event | category | flops | bytes accessed | tf_op | source)
XLA Modules:
  0.0 116.9 jit_solution(18112988619086252438)
XLA Ops:
  1.5 16.7 %all_to_all.10 = bf16[8,80,128]{2,1,0:T(8,128)(2,1)S(1)} all-to-all(bf16[8,80,128]{2,1,0:T(8,128)(2,1)S(1)} %broadcast_in_dim.2), channel_id=1, replica_groups=mesh['xh'=2,'z'=8,'c'=2,'xl'=2,'y'=4] {'z'}, dimensions={0} | all-to-all | bytes 327680 | tf_op jit(solution)/shard_map/all_to_all | solution.py:57
  18.2 1.5 %collective-permute-start.2 = (bf16[8,80,128]{2,1,0:T(8,128)(2,1)S(1)}, bf16[8,80,128]{2,1,0:T(8,128)(2,1)S(1)}, u32[]{:S(2)}, u32[]{:S(2)}) collective-permute-start(bf16[8,80,128]{2,1,0:T(8,128)(2,1)S(1)} %all_to_all.10), channel_id=1, source_target_pairs={{132,0},{133,1},{134,2},{135,3},{11,8},{8,9},{9,10},{10,11},{148,1... | collective-permute-start | bytes 491528 | tf_op jit(solution)/shard_map/ppermute | solution.py:49
  19.7 2.7 %collective-permute-start.1 = (bf16[8,80,128]{2,1,0:T(8,128)(2,1)S(1)}, bf16[8,80,128]{2,1,0:T(8,128)(2,1)S(1)}, u32[]{:S(2)}, u32[]{:S(2)}) collective-permute-start(bf16[8,80,128]{2,1,0:T(8,128)(2,1)S(1)} %all_to_all.10), channel_id=1, source_target_pairs={{128,0},{129,1},{130,2},{131,3},{10,8},{11,9},{8,10},{9,11},{144,1... | collective-permute-start | bytes 491528 | tf_op jit(solution)/shard_map/ppermute | solution.py:49
  22.4 1.4 %collective-permute-start = (bf16[8,80,128]{2,1,0:T(8,128)(2,1)S(1)}, bf16[8,80,128]{2,1,0:T(8,128)(2,1)S(1)}, u32[]{:S(2)}, u32[]{:S(2)}) collective-permute-start(bf16[8,80,128]{2,1,0:T(8,128)(2,1)S(1)} %all_to_all.10), channel_id=1, source_target_pairs={{4,0},{5,1},{6,2},{7,3},{9,8},{10,9},{11,10},{8,11},{20,16},{21,17... | collective-permute-start | bytes 491528 | tf_op jit(solution)/shard_map/ppermute | solution.py:49
  24.7 2.7 %collective-permute-done.1 = bf16[8,80,128]{2,1,0:T(8,128)(2,1)S(1)} collective-permute-done((bf16[8,80,128]{2,1,0:T(8,128)(2,1)S(1)}, bf16[8,80,128]{2,1,0:T(8,128)(2,1)S(1)}, u32[]{:S(2)}, u32[]{:S(2)}) %collective-permute-start.1) | collective-permute-done | bytes 163872 | tf_op jit(solution)/shard_map/ppermute | solution.py:49
  27.8 1.7 %collective-permute-start.3 = (bf16[4,8,80,128]{3,2,1,0:T(8,128)(2,1)S(1)}, bf16[4,8,80,128]{3,2,1,0:T(8,128)(2,1)S(1)}, u32[]{:S(2)}, u32[]{:S(2)}) collective-permute-start(bf16[4,8,80,128]{3,2,1,0:T(8,128)(2,1)S(1)} %pad_maximum_fusion.rest_0_), channel_id=1, source_target_pairs={{3,0},{0,1},{1,2},{2,3},{140,8},{141,9},{142,10},{143,11},{19,16},... | collective-permute-start | bytes 1966088 | tf_op jit(solution)/shard_map/ppermute | solution.py:49
  29.5 2.9 %collective-permute-start.5 = (bf16[4,8,80,128]{3,2,1,0:T(8,128)(2,1)S(1)}, bf16[4,8,80,128]{3,2,1,0:T(8,128)(2,1)S(1)}, u32[]{:S(2)}, u32[]{:S(2)}) collective-permute-start(bf16[4,8,80,128]{3,2,1,0:T(8,128)(2,1)S(1)} %pad_maximum_fusion.rest_0_), channel_id=1, source_target_pairs={{2,0},{3,1},{0,2},{1,3},{136,8},{137,9},{138,10},{139,11},{18,16},... | collective-permute-start | bytes 1966088 | tf_op jit(solution)/shard_map/ppermute | solution.py:49
  32.4 1.3 %collective-permute-start.4 = (bf16[4,8,80,128]{3,2,1,0:T(8,128)(2,1)S(1)}, bf16[4,8,80,128]{3,2,1,0:T(8,128)(2,1)}, u32[]{:S(2)}, u32[]{:S(2)}) collective-permute-start(bf16[4,8,80,128]{3,2,1,0:T(8,128)(2,1)S(1)} %pad_maximum_fusion.rest_0_), channel_id=1, source_target_pairs={{1,0},{2,1},{3,2},{0,3},{12,8},{13,9},{14,10},{15,11},{17,16},{18,... | collective-permute-start | bytes 1966088 | tf_op jit(solution)/shard_map/ppermute | solution.py:49
  33.8 1.2 %copy-done.1 = bf16[512,1024]{1,0:T(8,128)(2,1)S(1)} copy-done((bf16[512,1024]{1,0:T(8,128)(2,1)S(1)}, bf16[512,1024]{1,0:T(8,128)(2,1)}, u32[]{:S(2)}) %copy-start.1) | copy-done | bytes 1048600
  35.0 1.9 %prepare.1 = (bf16[512,1024]{1,0:T(8,128)(2,1)S(1)}, bf16[1024,512]{1,0:T(8,128)(2,1)S(1)}, bf16[1024,512]{1,0:T(8,128)(2,1)S(1)}, f32[2,256,256]{2,1,0:T(8,128)S(1)}) custom-call(s32[2,4]{1,0:T(2,128)S(1)} %copy-done.4, f32[1,1024]{1,0:T(1,128)S(1)} %bitcast.29, bf16[512,1024]{1,0:T(8,128)(2,1)S(1)} %copy-done, bf16[512,1024]{1,0:T(8,128)(2,1)S(1)} %copy-done.1), custom_call_target="tpu_custom_call" | custom-call | tf_op jit(solution)/shard_map/prepare/pallas_call | solution.py:325
  39.9 8.1 %collective-permute-done.5.rest_2_ = bf16[4,8,80,128]{3,2,1,0:T(8,128)(2,1)S(1)} collective-permute-done((bf16[4,8,80,128]{3,2,1,0:T(8,128)(2,1)S(1)}, bf16[4,8,80,128]{3,2,1,0:T(8,128)(2,1)S(1)}, u32[]{:S(2)}, u32[]{:S(2)}) %collective-permute-start.5) | collective-permute-done | bytes 655392 | tf_op jit(solution)/shard_map/ppermute | solution.py:49
  48.6 2.5 %collective-permute-done.8.rest_6_ = bf16[4,8,80,128]{3,2,1,0:T(8,128)(2,1)} collective-permute-done((bf16[4,8,80,128]{3,2,1,0:T(8,128)(2,1)S(1)}, bf16[4,8,80,128]{3,2,1,0:T(8,128)(2,1)}, u32[]{:S(2)}, u32[]{:S(2)}) %collective-permute-start.8) | collective-permute-done | bytes 655392 | tf_op jit(solution)/shard_map/ppermute | solution.py:53
  53.0 17.7 %attend.1 = (bf16[4,8,80,128]{3,2,1,0:T(8,128)(2,1)S(1)}, bf16[4,8,80,128]{3,2,1,0:T(8,128)(2,1)S(1)}, bf16[4,8,80,128]{3,2,1,0:T(8,128)(2,1)S(1)}, bf16[4,8,80,...) custom-call(s32[3]{0:T(128)S(1)} %pad_add_fusion.where, ...), custom_call_target="tpu_custom_call" | custom-call | flops 7000000000 | bytes 20000000 | tf_op jit(solution)/shard_map/attend/pallas_call | solution.py:339
  74.3 2.2 %collective-permute-start.14 = (bf16[4,8,80,128]{3,2,1,0:T(8,128)(2,1)S(1)}, bf16[4,8,80,128]{3,2,1,0:T(8,128)(2,1)S(1)}, u32[]{:S(2)}, u32[]{:S(2)}) collective-permute-start(bf16[4,8,80,128]{3,2,1,0:T(8,128)(2,1)S(1)} %add_convert_fusion.2), channel_id=1, source_target_pairs={{2,0},{3,1},{0,2},{1,3},{136,8},{137,9},{138,10},{139,11},{18,16},... | collective-permute-start | bytes 1966088 | tf_op jit(solution)/shard_map/ppermute | solution.py:49
  76.7 2.0 %collective-permute-start.16 = (bf16[4,8,80,128]{3,2,1,0:T(8,128)(2,1)S(1)}, bf16[4,8,80,128]{3,2,1,0:T(8,128)(2,1)S(1)}, u32[]{:S(2)}, u32[]{:S(2)}) collective-permute-start(bf16[4,8,80,128]{3,2,1,0:T(8,128)(2,1)S(1)} %add_convert_fusion.1), channel_id=1, source_target_pairs={{1,0},{2,1},{3,2},{0,3},{12,8},{13,9},{14,10},{15,11},{17,16},{18,... | collective-permute-start | bytes 1966088 | tf_op jit(solution)/shard_map/ppermute | solution.py:49
  78.8 9.3 %close.1 = (bf16[512,1024]{1,0:T(8,128)(2,1)}, bf16[512,1024]{1,0:T(8,128)(2,1)}) custom-call(s32[3]{0:T(128)S(1)} %pad_add_fusion.where, f32[1,1024]{1,0:T(1,128)S(1)} %bitcast.30, bf16[512,1024]{1,0:T(8,128)(2,1)S(1)} %copy-done, bf16[512,1024]{1,0:T(8,128)(2,1)S(1)} %copy-done.2, bf16[512,1024]{1,0:T(8,128)(2,1)S(1)} %get-tuple-element.51.mix, ...), custom_call_target="tpu_custom_call" | custom-call | flops 3000000000 | bytes 15000000 | tf_op jit(solution)/shard_map/close/pallas_call | solution.py:364
  88.1 3.9 %collective-permute-done.12 = bf16[4,8,80,128]{3,2,1,0:T(8,128)(2,1)S(1)} collective-permute-done((bf16[4,8,80,128]{3,2,1,0:T(8,128)(2,1)S(1)}, bf16[4,8,80,128]{3,2,1,0:T(8,128)(2,1)S(1)}, u32[]{:S(2)}, u32[]{:S(2)}) %collective-permute-start.12) | collective-permute-done | bytes 655392 | tf_op jit(solution)/shard_map/ppermute | solution.py:49
  92.0 1.2 %collective-permute-done.16 = bf16[4,8,80,128]{3,2,1,0:T(8,128)(2,1)S(1)} collective-permute-done((bf16[4,8,80,128]{3,2,1,0:T(8,128)(2,1)S(1)}, bf16[4,8,80,128]{3,2,1,0:T(8,128)(2,1)S(1)}, u32[]{:S(2)}, u32[]{:S(2)}) %collective-permute-start.16) | collective-permute-done | bytes 655392 | tf_op jit(solution)/shard_map/ppermute | solution.py:49
  93.6 1.7 %collective-permute-start.17 = (bf16[8,80,128]{2,1,0:T(8,128)(2,1)S(1)}, bf16[8,80,128]{2,1,0:T(8,128)(2,1)S(1)}, u32[]{:S(2)}, u32[]{:S(2)}) collective-permute-start(bf16[8,80,128]{2,1,0:T(8,128)(2,1)S(1)} %get-tuple-element.62), channel_id=1, source_target_pairs={{132,0},{133,1},{134,2},{135,3},{11,8},{8,9},{9,10},{10,11},{148,1... | collective-permute-start | bytes 491528 | tf_op jit(solution)/shard_map/ppermute | solution.py:49
  95.3 1.6 %collective-permute-start.19 = (bf16[8,80,128]{2,1,0:T(8,128)(2,1)S(1)}, bf16[8,80,128]{2,1,0:T(8,128)(2,1)S(1)}, u32[]{:S(2)}, u32[]{:S(2)}) collective-permute-start(bf16[8,80,128]{2,1,0:T(8,128)(2,1)S(1)} %get-tuple-element.63), channel_id=1, source_target_pairs={{4,0},{5,1},{6,2},{7,3},{9,8},{10,9},{11,10},{8,11},{20,16},{21,17... | collective-permute-start | bytes 491528 | tf_op jit(solution)/shard_map/ppermute | solution.py:49
  96.9 1.5 %collective-permute-start.18 = (bf16[8,80,128]{2,1,0:T(8,128)(2,1)S(1)}, bf16[8,80,128]{2,1,0:T(8,128)(2,1)S(1)}, u32[]{:S(2)}, u32[]{:S(2)}) collective-permute-start(bf16[8,80,128]{2,1,0:T(8,128)(2,1)S(1)} %get-tuple-element.64), channel_id=1, source_target_pairs={{128,0},{129,1},{130,2},{131,3},{10,8},{11,9},{8,10},{9,11},{144,1... | collective-permute-start | bytes 491528 | tf_op jit(solution)/shard_map/ppermute | solution.py:49
  98.4 1.8 %collective-permute-done.17 = bf16[8,80,128]{2,1,0:T(8,128)(2,1)S(1)} collective-permute-done((bf16[8,80,128]{2,1,0:T(8,128)(2,1)S(1)}, bf16[8,80,128]{2,1,0:T(8,128)(2,1)S(1)}, u32[]{:S(2)}, u32[]{:S(2)}) %collective-permute-start.17) | collective-permute-done | bytes 163872 | tf_op jit(solution)/shard_map/ppermute | solution.py:49
  100.7 3.1 %collective-permute-done.18 = bf16[8,80,128]{2,1,0:T(8,128)(2,1)S(1)} collective-permute-done((bf16[8,80,128]{2,1,0:T(8,128)(2,1)S(1)}, bf16[8,80,128]{2,1,0:T(8,128)(2,1)S(1)}, u32[]{:S(2)}, u32[]{:S(2)}) %collective-permute-start.18) | collective-permute-done | bytes 163872 | tf_op jit(solution)/shard_map/ppermute | solution.py:49
  103.9 11.8 %all_to_all.11 = bf16[8,80,128]{2,1,0:T(8,128)(2,1)S(1)} all-to-all(bf16[8,80,128]{2,1,0:T(8,128)(2,1)S(1)} %fusion.2), channel_id=1, replica_groups=mesh['xh'=2,'z'=8,'c'=2,'xl'=2,'y'=4] {'z'}, dimensions={0} | all-to-all | bytes 327680 | tf_op jit(solution)/shard_map/all_to_all | solution.py:73
  (52 shorter events, 13.5 us)
Async XLA Ops:
  0.6 33.1 %copy-start = (bf16[512,1024]{1,0:T(8,128)(2,1)S(1)}, bf16[512,1024]{1,0:T(8,128)(2,1)}, u32[]{:S(2)}) copy-start(bf16[512,1024]{1,0:T(8,128)(2,1)} %hidden.3) | copy-start | bytes 3145732
  0.6 33.1 %copy-start.4 = (s32[2,4]{1,0:T(2,128)S(1)}, s32[2,4]{1,0:T(2,128)}, u32[]{:S(2)}) copy-start(s32[2,4]{1,0:T(2,128)} %docs.1) | copy-start | bytes 100
  0.7 33.1 %copy-start.3 = (f32[1024]{0:T(1024)S(1)}, f32[1024]{0:T(1024)}, u32[]{:S(2)}) copy-start(f32[1024]{0:T(1024)} %param.10) | copy-start | bytes 12292
  18.2 6.5 %collective-permute-start.2 = (bf16[8,80,128]{2,1,0:T(8,128)(2,1)S(1)}, bf16[8,80,128]{2,1,0:T(8,128)(2,1)S(1)}, u32[]{:S(2)}, u32[]{:S(2)}) collective-permute-start(bf16[8,80,128]{2,1,0:T(8,128)(2,1)S(1)} %all_to_all.10), channel_id=1, source_target_pairs={{132,0},{133,1},{134,2},{135,3},{11,8},{8,9},{9,10},{10,11},{148,1... | collective-permute-start | bytes 491528 | tf_op jit(solution)/shard_map/ppermute | solution.py:49
  19.7 7.8 %collective-permute-start.1 = (bf16[8,80,128]{2,1,0:T(8,128)(2,1)S(1)}, bf16[8,80,128]{2,1,0:T(8,128)(2,1)S(1)}, u32[]{:S(2)}, u32[]{:S(2)}) collective-permute-start(bf16[8,80,128]{2,1,0:T(8,128)(2,1)S(1)} %all_to_all.10), channel_id=1, source_target_pairs={{128,0},{129,1},{130,2},{131,3},{10,8},{11,9},{8,10},{9,11},{144,1... | collective-permute-start | bytes 491528 | tf_op jit(solution)/shard_map/ppermute | solution.py:49
  22.4 5.3 %collective-permute-start = (bf16[8,80,128]{2,1,0:T(8,128)(2,1)S(1)}, bf16[8,80,128]{2,1,0:T(8,128)(2,1)S(1)}, u32[]{:S(2)}, u32[]{:S(2)}) collective-permute-start(bf16[8,80,128]{2,1,0:T(8,128)(2,1)S(1)} %all_to_all.10), channel_id=1, source_target_pairs={{4,0},{5,1},{6,2},{7,3},{9,8},{10,9},{11,10},{8,11},{20,16},{21,17... | collective-permute-start | bytes 491528 | tf_op jit(solution)/shard_map/ppermute | solution.py:49
  27.8 12.0 %collective-permute-start.3 = (bf16[4,8,80,128]{3,2,1,0:T(8,128)(2,1)S(1)}, bf16[4,8,80,128]{3,2,1,0:T(8,128)(2,1)S(1)}, u32[]{:S(2)}, u32[]{:S(2)}) collective-permute-start(bf16[4,8,80,128]{3,2,1,0:T(8,128)(2,1)S(1)} %pad_maximum_fusion.rest_0_), channel_id=1, source_target_pairs={{3,0},{0,1},{1,2},{2,3},{140,8},{141,9},{142,10},{143,11},{19,16},... | collective-permute-start | bytes 1966088 | tf_op jit(solution)/shard_map/ppermute | solution.py:49
  29.5 18.5 %collective-permute-start.5 = (bf16[4,8,80,128]{3,2,1,0:T(8,128)(2,1)S(1)}, bf16[4,8,80,128]{3,2,1,0:T(8,128)(2,1)S(1)}, u32[]{:S(2)}, u32[]{:S(2)}) collective-permute-start(bf16[4,8,80,128]{3,2,1,0:T(8,128)(2,1)S(1)} %pad_maximum_fusion.rest_0_), channel_id=1, source_target_pairs={{2,0},{3,1},{0,2},{1,3},{136,8},{137,9},{138,10},{139,11},{18,16},... | collective-permute-start | bytes 1966088 | tf_op jit(solution)/shard_map/ppermute | solution.py:49
  32.4 15.6 %collective-permute-start.4 = (bf16[4,8,80,128]{3,2,1,0:T(8,128)(2,1)S(1)}, bf16[4,8,80,128]{3,2,1,0:T(8,128)(2,1)}, u32[]{:S(2)}, u32[]{:S(2)}) collective-permute-start(bf16[4,8,80,128]{3,2,1,0:T(8,128)(2,1)S(1)} %pad_maximum_fusion.rest_0_), channel_id=1, source_target_pairs={{1,0},{2,1},{3,2},{0,3},{12,8},{13,9},{14,10},{15,11},{17,16},{18,... | collective-permute-start | bytes 1966088 | tf_op jit(solution)/shard_map/ppermute | solution.py:49
  39.9 8.7 %collective-permute-start.6 = (bf16[4,8,80,128]{3,2,1,0:T(8,128)(2,1)S(1)}, bf16[4,8,80,128]{3,2,1,0:T(8,128)(2,1)}, u32[]{:S(2)}, u32[]{:S(2)}) collective-permute-start(bf16[4,8,80,128]{3,2,1,0:T(8,128)(2,1)S(1)} %pad_maximum_fusion.rest_0_), channel_id=1, source_target_pairs={{0,8},{8,0},{1,9},{9,1},{2,10},{10,2},{3,11},{11,3},{4,12},{12,4},... | collective-permute-start | bytes 1966088 | tf_op jit(solution)/shard_map/ppermute | solution.py:53
  48.0 3.1 %collective-permute-start.8 = (bf16[4,8,80,128]{3,2,1,0:T(8,128)(2,1)S(1)}, bf16[4,8,80,128]{3,2,1,0:T(8,128)(2,1)}, u32[]{:S(2)}, u32[]{:S(2)}) collective-permute-start(bf16[4,8,80,128]{3,2,1,0:T(8,128)(2,1)S(1)} %collective-permute-done.5.rest_2_), channel_id=1, source_target_pairs={{0,8},{8,0},{1,9},{9,1},{2,10},{10,2},{3,11},{11,3},{4,12},{12,4},... | collective-permute-start | bytes 1966088 | tf_op jit(solution)/shard_map/ppermute | solution.py:53
  48.0 3.9 %collective-permute-start.7 = (bf16[4,8,80,128]{3,2,1,0:T(8,128)(2,1)}, bf16[4,8,80,128]{3,2,1,0:T(8,128)(2,1)}, u32[]{:S(2)}, u32[]{:S(2)}) collective-permute-start(bf16[4,8,80,128]{3,2,1,0:T(8,128)(2,1)} %collective-permute-done.4.rest_1_), channel_id=1, source_target_pairs={{0,8},{8,0},{1,9},{9,1},{2,10},{10,2},{3,11},{11,3},{4,12},{12,4},... | collective-permute-start | bytes 1966088 | tf_op jit(solution)/shard_map/ppermute | solution.py:53
  48.5 3.6 %collective-permute-start.9 = (bf16[4,8,80,128]{3,2,1,0:T(8,128)(2,1)S(1)}, bf16[4,8,80,128]{3,2,1,0:T(8,128)(2,1)}, u32[]{:S(2)}, u32[]{:S(2)}) collective-permute-start(bf16[4,8,80,128]{3,2,1,0:T(8,128)(2,1)S(1)} %collective-permute-done.3.rest_3_), channel_id=1, source_target_pairs={{0,8},{8,0},{1,9},{9,1},{2,10},{10,2},{3,11},{11,3},{4,12},{12,4},... | collective-permute-start | bytes 1966088 | tf_op jit(solution)/shard_map/ppermute | solution.py:53
  70.7 2.2 %collective-permute-start.11 = (bf16[4,8,80,128]{3,2,1,0:T(8,128)(2,1)S(1)}, bf16[4,8,80,128]{3,2,1,0:T(8,128)(2,1)S(1)}, u32[]{:S(2)}, u32[]{:S(2)}) collective-permute-start(bf16[4,8,80,128]{3,2,1,0:T(8,128)(2,1)S(1)} %get-tuple-element.46), channel_id=1, source_target_pairs={{0,8},{8,0},{1,9},{9,1},{2,10},{10,2},{3,11},{11,3},{4,12},{12,4},... | collective-permute-start | bytes 1966088 | tf_op jit(solution)/shard_map/ppermute | solution.py:53
  71.0 3.1 %collective-permute-start.13 = (bf16[4,8,80,128]{3,2,1,0:T(8,128)(2,1)S(1)}, bf16[4,8,80,128]{3,2,1,0:T(8,128)(2,1)S(1)}, u32[]{:S(2)}, u32[]{:S(2)}) collective-permute-start(bf16[4,8,80,128]{3,2,1,0:T(8,128)(2,1)S(1)} %get-tuple-element.48), channel_id=1, source_target_pairs={{0,8},{8,0},{1,9},{9,1},{2,10},{10,2},{3,11},{11,3},{4,12},{12,4},... | collective-permute-start | bytes 1966088 | tf_op jit(solution)/shard_map/ppermute | solution.py:53
  71.3 5.2 %collective-permute-start.15 = (bf16[4,8,80,128]{3,2,1,0:T(8,128)(2,1)S(1)}, bf16[4,8,80,128]{3,2,1,0:T(8,128)(2,1)S(1)}, u32[]{:S(2)}, u32[]{:S(2)}) collective-permute-start(bf16[4,8,80,128]{3,2,1,0:T(8,128)(2,1)S(1)} %get-tuple-element.50), channel_id=1, source_target_pairs={{0,8},{8,0},{1,9},{9,1},{2,10},{10,2},{3,11},{11,3},{4,12},{12,4},... | collective-permute-start | bytes 1966088 | tf_op jit(solution)/shard_map/ppermute | solution.py:53
  71.5 16.6 %collective-permute-start.10 = (bf16[4,8,80,128]{3,2,1,0:T(8,128)(2,1)S(1)}, bf16[4,8,80,128]{3,2,1,0:T(8,128)(2,1)S(1)}, u32[]{:S(2)}, u32[]{:S(2)}) collective-permute-start(bf16[4,8,80,128]{3,2,1,0:T(8,128)(2,1)S(1)} %get-tuple-element.44), channel_id=1, source_target_pairs={{0,8},{8,0},{1,9},{9,1},{2,10},{10,2},{3,11},{11,3},{4,12},{12,4},... | collective-permute-start | bytes 1966088 | tf_op jit(solution)/shard_map/ppermute | solution.py:53
  73.1 18.9 %collective-permute-start.12 = (bf16[4,8,80,128]{3,2,1,0:T(8,128)(2,1)S(1)}, bf16[4,8,80,128]{3,2,1,0:T(8,128)(2,1)S(1)}, u32[]{:S(2)}, u32[]{:S(2)}) collective-permute-start(bf16[4,8,80,128]{3,2,1,0:T(8,128)(2,1)S(1)} %add_convert_fusion.3), channel_id=1, source_target_pairs={{3,0},{0,1},{1,2},{2,3},{140,8},{141,9},{142,10},{143,11},{19,16},... | collective-permute-start | bytes 1966088 | tf_op jit(solution)/shard_map/ppermute | solution.py:49
  74.3 4.4 %copy-start.2 = (bf16[512,1024]{1,0:T(8,128)(2,1)S(1)}, bf16[512,1024]{1,0:T(8,128)(2,1)}, u32[]{:S(2)}) copy-start(bf16[512,1024]{1,0:T(8,128)(2,1)} %cot.5) | copy-start | bytes 3145732
  74.3 17.6 %collective-permute-start.14 = (bf16[4,8,80,128]{3,2,1,0:T(8,128)(2,1)S(1)}, bf16[4,8,80,128]{3,2,1,0:T(8,128)(2,1)S(1)}, u32[]{:S(2)}, u32[]{:S(2)}) collective-permute-start(bf16[4,8,80,128]{3,2,1,0:T(8,128)(2,1)S(1)} %add_convert_fusion.2), channel_id=1, source_target_pairs={{2,0},{3,1},{0,2},{1,3},{136,8},{137,9},{138,10},{139,11},{18,16},... | collective-permute-start | bytes 1966088 | tf_op jit(solution)/shard_map/ppermute | solution.py:49
  76.7 16.4 %collective-permute-start.16 = (bf16[4,8,80,128]{3,2,1,0:T(8,128)(2,1)S(1)}, bf16[4,8,80,128]{3,2,1,0:T(8,128)(2,1)S(1)}, u32[]{:S(2)}, u32[]{:S(2)}) collective-permute-start(bf16[4,8,80,128]{3,2,1,0:T(8,128)(2,1)S(1)} %add_convert_fusion.1), channel_id=1, source_target_pairs={{1,0},{2,1},{3,2},{0,3},{12,8},{13,9},{14,10},{15,11},{17,16},{18,... | collective-permute-start | bytes 1966088 | tf_op jit(solution)/shard_map/ppermute | solution.py:49
  93.6 6.6 %collective-permute-start.17 = (bf16[8,80,128]{2,1,0:T(8,128)(2,1)S(1)}, bf16[8,80,128]{2,1,0:T(8,128)(2,1)S(1)}, u32[]{:S(2)}, u32[]{:S(2)}) collective-permute-start(bf16[8,80,128]{2,1,0:T(8,128)(2,1)S(1)} %get-tuple-element.62), channel_id=1, source_target_pairs={{132,0},{133,1},{134,2},{135,3},{11,8},{8,9},{9,10},{10,11},{148,1... | collective-permute-start | bytes 491528 | tf_op jit(solution)/shard_map/ppermute | solution.py:49
  95.3 5.3 %collective-permute-start.19 = (bf16[8,80,128]{2,1,0:T(8,128)(2,1)S(1)}, bf16[8,80,128]{2,1,0:T(8,128)(2,1)S(1)}, u32[]{:S(2)}, u32[]{:S(2)}) collective-permute-start(bf16[8,80,128]{2,1,0:T(8,128)(2,1)S(1)} %get-tuple-element.63), channel_id=1, source_target_pairs={{4,0},{5,1},{6,2},{7,3},{9,8},{10,9},{11,10},{8,11},{20,16},{21,17... | collective-permute-start | bytes 491528 | tf_op jit(solution)/shard_map/ppermute | solution.py:49
  96.9 6.8 %collective-permute-start.18 = (bf16[8,80,128]{2,1,0:T(8,128)(2,1)S(1)}, bf16[8,80,128]{2,1,0:T(8,128)(2,1)S(1)}, u32[]{:S(2)}, u32[]{:S(2)}) collective-permute-start(bf16[8,80,128]{2,1,0:T(8,128)(2,1)S(1)} %get-tuple-element.64), channel_id=1, source_target_pairs={{128,0},{129,1},{130,2},{131,3},{10,8},{11,9},{8,10},{9,11},{144,1... | collective-permute-start | bytes 491528 | tf_op jit(solution)/shard_map/ppermute | solution.py:49
  (5 other events, 5.1 us)

commit v6 on v5

--- a/solution.py
+++ b/solution.py
@@ -57,7 +57,8 @@
     mine = lax.all_to_all(jnp.broadcast_to(block[None], (8, ROWS, 128)), "z", 0, 0, tiled=True)
     first = jnp.stack([mine] + [shift(mine, 0, step) for step in (1, 2, 3)])
     pieces = [first] + [shift(first, 1, step) for step in (1, 2, 3)]
-    pieces[3], ready = lax.optimization_barrier((pieces[3], ready))
+    pieces[3], mask = lax.optimization_barrier((pieces[3], ready[3]))
+    ready = (*ready[:3], mask)
     return pieces + [swap(piece) for piece in pieces], ready
 
 

time: 119 us -> 119 us (level)
  no operation moved by 1% of the time
where the time goes in v6:
time: 119 us; the launch traced here: 117 us
  Pallas kernels  29 us (24%)
  blocking collectives  28.5 us (24%)
  waiting for transfers between devices  27 us (23%)
  starting transfers between devices  23.2 us (19%)
  local copies, waits for them, and re-layouts  6.33 us (5%)
  other arithmetic  2.09 us (2%)
    ppermute x12, waiting for transfers between devices, shift(): return lax.ppermute(block, AXES, pairs)  22.4 us
    ppermute x12, starting transfers between devices, shift(): return lax.ppermute(block, AXES, pairs)  21.6 us
    pallas_call x1, Pallas kernels, local(): pl.pallas_call(attend, name='attend', out_shape=[PIECE] * 8 + shapes, in_...  17.7 us
    all_to_all x1, blocking collectives, gather_blocks(): lax.all_to_all(jnp.broadcast_to(block[None], (8, ROWS, 128)), 'z', 0, 0,...  16.7 us
    all_to_all x1, blocking collectives, scatter_blocks(): parts = lax.all_to_all(summed, 'z', 0, 0, tiled=True)  11.8 us
    pallas_call x1, Pallas kernels, local(): pl.pallas_call(close, name='close', out_shape=[jax.ShapeDtypeStruct((TOKE...  9.3 us
    unnamed x18, local copies, waits for them, and re-layouts  5.05 us
    ppermute x8, waiting for transfers between devices, swap(): return lax.ppermute(block, 'c', [(0, 1), (1, 0)])  4.59 us
  transfers between devices with their start and end apart: 20, of which 13 were waited for; matrix products, arithmetic and copies ran while one was open for 1% of the time, Pallas kernels for 10%

profile of v6, /device:TPU:32, one launch (start us, length us, event | category | flops | bytes accessed | tf_op | source)
XLA Modules:
  0.0 116.9 jit_solution(18112988619086252438)
XLA Ops:
  1.5 16.7 %all_to_all.10 = bf16[8,80,128]{2,1,0:T(8,128)(2,1)S(1)} all-to-all(bf16[8,80,128]{2,1,0:T(8,128)(2,1)S(1)} %broadcast_in_dim.2), channel_id=1, replica_groups=mesh['xh'=2,'z'=8,'c'=2,'xl'=2,'y'=4] {'z'}, dimensions={0} | all-to-all | bytes 327680 | tf_op jit(solution)/shard_map/all_to_all | solution.py:57
  18.2 1.5 %collective-permute-start.2 = (bf16[8,80,128]{2,1,0:T(8,128)(2,1)S(1)}, bf16[8,80,128]{2,1,0:T(8,128)(2,1)S(1)}, u32[]{:S(2)}, u32[]{:S(2)}) collective-permute-start(bf16[8,80,128]{2,1,0:T(8,128)(2,1)S(1)} %all_to_all.10), channel_id=1, source_target_pairs={{132,0},{133,1},{134,2},{135,3},{11,8},{8,9},{9,10},{10,11},{148,1... | collective-permute-start | bytes 491528 | tf_op jit(solution)/shard_map/ppermute | solution.py:49
  19.7 2.7 %collective-permute-start.1 = (bf16[8,80,128]{2,1,0:T(8,128)(2,1)S(1)}, bf16[8,80,128]{2,1,0:T(8,128)(2,1)S(1)}, u32[]{:S(2)}, u32[]{:S(2)}) collective-permute-start(bf16[8,80,128]{2,1,0:T(8,128)(2,1)S(1)} %all_to_all.10), channel_id=1, source_target_pairs={{128,0},{129,1},{130,2},{131,3},{10,8},{11,9},{8,10},{9,11},{144,1... | collective-permute-start | bytes 491528 | tf_op jit(solution)/shard_map/ppermute | solution.py:49
  22.4 1.4 %collective-permute-start = (bf16[8,80,128]{2,1,0:T(8,128)(2,1)S(1)}, bf16[8,80,128]{2,1,0:T(8,128)(2,1)S(1)}, u32[]{:S(2)}, u32[]{:S(2)}) collective-permute-start(bf16[8,80,128]{2,1,0:T(8,128)(2,1)S(1)} %all_to_all.10), channel_id=1, source_target_pairs={{4,0},{5,1},{6,2},{7,3},{9,8},{10,9},{11,10},{8,11},{20,16},{21,17... | collective-permute-start | bytes 491528 | tf_op jit(solution)/shard_map/ppermute | solution.py:49
  24.7 2.7 %collective-permute-done.1 = bf16[8,80,128]{2,1,0:T(8,128)(2,1)S(1)} collective-permute-done((bf16[8,80,128]{2,1,0:T(8,128)(2,1)S(1)}, bf16[8,80,128]{2,1,0:T(8,128)(2,1)S(1)}, u32[]{:S(2)}, u32[]{:S(2)}) %collective-permute-start.1) | collective-permute-done | bytes 163872 | tf_op jit(solution)/shard_map/ppermute | solution.py:49
  27.8 1.7 %collective-permute-start.3 = (bf16[4,8,80,128]{3,2,1,0:T(8,128)(2,1)S(1)}, bf16[4,8,80,128]{3,2,1,0:T(8,128)(2,1)S(1)}, u32[]{:S(2)}, u32[]{:S(2)}) collective-permute-start(bf16[4,8,80,128]{3,2,1,0:T(8,128)(2,1)S(1)} %pad_maximum_fusion.rest_0_), channel_id=1, source_target_pairs={{3,0},{0,1},{1,2},{2,3},{140,8},{141,9},{142,10},{143,11},{19,16},... | collective-permute-start | bytes 1966088 | tf_op jit(solution)/shard_map/ppermute | solution.py:49
  29.5 2.9 %collective-permute-start.5 = (bf16[4,8,80,128]{3,2,1,0:T(8,128)(2,1)S(1)}, bf16[4,8,80,128]{3,2,1,0:T(8,128)(2,1)S(1)}, u32[]{:S(2)}, u32[]{:S(2)}) collective-permute-start(bf16[4,8,80,128]{3,2,1,0:T(8,128)(2,1)S(1)} %pad_maximum_fusion.rest_0_), channel_id=1, source_target_pairs={{2,0},{3,1},{0,2},{1,3},{136,8},{137,9},{138,10},{139,11},{18,16},... | collective-permute-start | bytes 1966088 | tf_op jit(solution)/shard_map/ppermute | solution.py:49
  32.4 1.3 %collective-permute-start.4 = (bf16[4,8,80,128]{3,2,1,0:T(8,128)(2,1)S(1)}, bf16[4,8,80,128]{3,2,1,0:T(8,128)(2,1)}, u32[]{:S(2)}, u32[]{:S(2)}) collective-permute-start(bf16[4,8,80,128]{3,2,1,0:T(8,128)(2,1)S(1)} %pad_maximum_fusion.rest_0_), channel_id=1, source_target_pairs={{1,0},{2,1},{3,2},{0,3},{12,8},{13,9},{14,10},{15,11},{17,16},{18,... | collective-permute-start | bytes 1966088 | tf_op jit(solution)/shard_map/ppermute | solution.py:49
  33.8 1.2 %copy-done.1 = bf16[512,1024]{1,0:T(8,128)(2,1)S(1)} copy-done((bf16[512,1024]{1,0:T(8,128)(2,1)S(1)}, bf16[512,1024]{1,0:T(8,128)(2,1)}, u32[]{:S(2)}) %copy-start.1) | copy-done | bytes 1048600
  35.0 1.9 %prepare.1 = (bf16[512,1024]{1,0:T(8,128)(2,1)S(1)}, bf16[1024,512]{1,0:T(8,128)(2,1)S(1)}, bf16[1024,512]{1,0:T(8,128)(2,1)S(1)}, f32[2,256,256]{2,1,0:T(8,128)S(1)}) custom-call(s32[2,4]{1,0:T(2,128)S(1)} %copy-done.4, f32[1,1024]{1,0:T(1,128)S(1)} %bitcast.29, bf16[512,1024]{1,0:T(8,128)(2,1)S(1)} %copy-done, bf16[512,1024]{1,0:T(8,128)(2,1)S(1)} %copy-done.1), custom_call_target="tpu_custom_call" | custom-call | tf_op jit(solution)/shard_map/prepare/pallas_call | solution.py:326
  39.9 8.1 %collective-permute-done.5.rest_2_ = bf16[4,8,80,128]{3,2,1,0:T(8,128)(2,1)S(1)} collective-permute-done((bf16[4,8,80,128]{3,2,1,0:T(8,128)(2,1)S(1)}, bf16[4,8,80,128]{3,2,1,0:T(8,128)(2,1)S(1)}, u32[]{:S(2)}, u32[]{:S(2)}) %collective-permute-start.5) | collective-permute-done | bytes 655392 | tf_op jit(solution)/shard_map/ppermute | solution.py:49
  48.6 2.5 %collective-permute-done.8.rest_6_ = bf16[4,8,80,128]{3,2,1,0:T(8,128)(2,1)} collective-permute-done((bf16[4,8,80,128]{3,2,1,0:T(8,128)(2,1)S(1)}, bf16[4,8,80,128]{3,2,1,0:T(8,128)(2,1)}, u32[]{:S(2)}, u32[]{:S(2)}) %collective-permute-start.8) | collective-permute-done | bytes 655392 | tf_op jit(solution)/shard_map/ppermute | solution.py:53
  53.0 17.7 %attend.1 = (bf16[4,8,80,128]{3,2,1,0:T(8,128)(2,1)S(1)}, bf16[4,8,80,128]{3,2,1,0:T(8,128)(2,1)S(1)}, bf16[4,8,80,128]{3,2,1,0:T(8,128)(2,1)S(1)}, bf16[4,8,80,...) custom-call(s32[3]{0:T(128)S(1)} %pad_add_fusion.where, ...), custom_call_target="tpu_custom_call" | custom-call | flops 7000000000 | bytes 20000000 | tf_op jit(solution)/shard_map/attend/pallas_call | solution.py:340
  74.3 2.2 %collective-permute-start.14 = (bf16[4,8,80,128]{3,2,1,0:T(8,128)(2,1)S(1)}, bf16[4,8,80,128]{3,2,1,0:T(8,128)(2,1)S(1)}, u32[]{:S(2)}, u32[]{:S(2)}) collective-permute-start(bf16[4,8,80,128]{3,2,1,0:T(8,128)(2,1)S(1)} %add_convert_fusion.2), channel_id=1, source_target_pairs={{2,0},{3,1},{0,2},{1,3},{136,8},{137,9},{138,10},{139,11},{18,16},... | collective-permute-start | bytes 1966088 | tf_op jit(solution)/shard_map/ppermute | solution.py:49
  76.7 2.0 %collective-permute-start.16 = (bf16[4,8,80,128]{3,2,1,0:T(8,128)(2,1)S(1)}, bf16[4,8,80,128]{3,2,1,0:T(8,128)(2,1)S(1)}, u32[]{:S(2)}, u32[]{:S(2)}) collective-permute-start(bf16[4,8,80,128]{3,2,1,0:T(8,128)(2,1)S(1)} %add_convert_fusion.1), channel_id=1, source_target_pairs={{1,0},{2,1},{3,2},{0,3},{12,8},{13,9},{14,10},{15,11},{17,16},{18,... | collective-permute-start | bytes 1966088 | tf_op jit(solution)/shard_map/ppermute | solution.py:49
  78.8 9.3 %close.1 = (bf16[512,1024]{1,0:T(8,128)(2,1)}, bf16[512,1024]{1,0:T(8,128)(2,1)}) custom-call(s32[3]{0:T(128)S(1)} %pad_add_fusion.where, f32[1,1024]{1,0:T(1,128)S(1)} %bitcast.30, bf16[512,1024]{1,0:T(8,128)(2,1)S(1)} %copy-done, bf16[512,1024]{1,0:T(8,128)(2,1)S(1)} %copy-done.2, bf16[512,1024]{1,0:T(8,128)(2,1)S(1)} %get-tuple-element.45.mix, ...), custom_call_target="tpu_custom_call" | custom-call | flops 3000000000 | bytes 15000000 | tf_op jit(solution)/shard_map/close/pallas_call | solution.py:365
  88.1 3.9 %collective-permute-done.12 = bf16[4,8,80,128]{3,2,1,0:T(8,128)(2,1)S(1)} collective-permute-done((bf16[4,8,80,128]{3,2,1,0:T(8,128)(2,1)S(1)}, bf16[4,8,80,128]{3,2,1,0:T(8,128)(2,1)S(1)}, u32[]{:S(2)}, u32[]{:S(2)}) %collective-permute-start.12) | collective-permute-done | bytes 655392 | tf_op jit(solution)/shard_map/ppermute | solution.py:49
  92.0 1.2 %collective-permute-done.16 = bf16[4,8,80,128]{3,2,1,0:T(8,128)(2,1)S(1)} collective-permute-done((bf16[4,8,80,128]{3,2,1,0:T(8,128)(2,1)S(1)}, bf16[4,8,80,128]{3,2,1,0:T(8,128)(2,1)S(1)}, u32[]{:S(2)}, u32[]{:S(2)}) %collective-permute-start.16) | collective-permute-done | bytes 655392 | tf_op jit(solution)/shard_map/ppermute | solution.py:49
  93.6 1.7 %collective-permute-start.17 = (bf16[8,80,128]{2,1,0:T(8,128)(2,1)S(1)}, bf16[8,80,128]{2,1,0:T(8,128)(2,1)S(1)}, u32[]{:S(2)}, u32[]{:S(2)}) collective-permute-start(bf16[8,80,128]{2,1,0:T(8,128)(2,1)S(1)} %get-tuple-element.56), channel_id=1, source_target_pairs={{132,0},{133,1},{134,2},{135,3},{11,8},{8,9},{9,10},{10,11},{148,1... | collective-permute-start | bytes 491528 | tf_op jit(solution)/shard_map/ppermute | solution.py:49
  95.3 1.6 %collective-permute-start.19 = (bf16[8,80,128]{2,1,0:T(8,128)(2,1)S(1)}, bf16[8,80,128]{2,1,0:T(8,128)(2,1)S(1)}, u32[]{:S(2)}, u32[]{:S(2)}) collective-permute-start(bf16[8,80,128]{2,1,0:T(8,128)(2,1)S(1)} %get-tuple-element.57), channel_id=1, source_target_pairs={{4,0},{5,1},{6,2},{7,3},{9,8},{10,9},{11,10},{8,11},{20,16},{21,17... | collective-permute-start | bytes 491528 | tf_op jit(solution)/shard_map/ppermute | solution.py:49
  96.9 1.5 %collective-permute-start.18 = (bf16[8,80,128]{2,1,0:T(8,128)(2,1)S(1)}, bf16[8,80,128]{2,1,0:T(8,128)(2,1)S(1)}, u32[]{:S(2)}, u32[]{:S(2)}) collective-permute-start(bf16[8,80,128]{2,1,0:T(8,128)(2,1)S(1)} %get-tuple-element.58), channel_id=1, source_target_pairs={{128,0},{129,1},{130,2},{131,3},{10,8},{11,9},{8,10},{9,11},{144,1... | collective-permute-start | bytes 491528 | tf_op jit(solution)/shard_map/ppermute | solution.py:49
  98.4 1.8 %collective-permute-done.17 = bf16[8,80,128]{2,1,0:T(8,128)(2,1)S(1)} collective-permute-done((bf16[8,80,128]{2,1,0:T(8,128)(2,1)S(1)}, bf16[8,80,128]{2,1,0:T(8,128)(2,1)S(1)}, u32[]{:S(2)}, u32[]{:S(2)}) %collective-permute-start.17) | collective-permute-done | bytes 163872 | tf_op jit(solution)/shard_map/ppermute | solution.py:49
  100.7 3.1 %collective-permute-done.18 = bf16[8,80,128]{2,1,0:T(8,128)(2,1)S(1)} collective-permute-done((bf16[8,80,128]{2,1,0:T(8,128)(2,1)S(1)}, bf16[8,80,128]{2,1,0:T(8,128)(2,1)S(1)}, u32[]{:S(2)}, u32[]{:S(2)}) %collective-permute-start.18) | collective-permute-done | bytes 163872 | tf_op jit(solution)/shard_map/ppermute | solution.py:49
  103.9 11.8 %all_to_all.11 = bf16[8,80,128]{2,1,0:T(8,128)(2,1)S(1)} all-to-all(bf16[8,80,128]{2,1,0:T(8,128)(2,1)S(1)} %fusion.2), channel_id=1, replica_groups=mesh['xh'=2,'z'=8,'c'=2,'xl'=2,'y'=4] {'z'}, dimensions={0} | all-to-all | bytes 327680 | tf_op jit(solution)/shard_map/all_to_all | solution.py:74
  (52 shorter events, 13.5 us)
Async XLA Ops:
  0.6 33.1 %copy-start = (bf16[512,1024]{1,0:T(8,128)(2,1)S(1)}, bf16[512,1024]{1,0:T(8,128)(2,1)}, u32[]{:S(2)}) copy-start(bf16[512,1024]{1,0:T(8,128)(2,1)} %hidden.3) | copy-start | bytes 3145732
  0.6 33.1 %copy-start.4 = (s32[2,4]{1,0:T(2,128)S(1)}, s32[2,4]{1,0:T(2,128)}, u32[]{:S(2)}) copy-start(s32[2,4]{1,0:T(2,128)} %docs.1) | copy-start | bytes 100
  0.7 33.1 %copy-start.3 = (f32[1024]{0:T(1024)S(1)}, f32[1024]{0:T(1024)}, u32[]{:S(2)}) copy-start(f32[1024]{0:T(1024)} %param.10) | copy-start | bytes 12292
  18.2 6.5 %collective-permute-start.2 = (bf16[8,80,128]{2,1,0:T(8,128)(2,1)S(1)}, bf16[8,80,128]{2,1,0:T(8,128)(2,1)S(1)}, u32[]{:S(2)}, u32[]{:S(2)}) collective-permute-start(bf16[8,80,128]{2,1,0:T(8,128)(2,1)S(1)} %all_to_all.10), channel_id=1, source_target_pairs={{132,0},{133,1},{134,2},{135,3},{11,8},{8,9},{9,10},{10,11},{148,1... | collective-permute-start | bytes 491528 | tf_op jit(solution)/shard_map/ppermute | solution.py:49
  19.7 7.8 %collective-permute-start.1 = (bf16[8,80,128]{2,1,0:T(8,128)(2,1)S(1)}, bf16[8,80,128]{2,1,0:T(8,128)(2,1)S(1)}, u32[]{:S(2)}, u32[]{:S(2)}) collective-permute-start(bf16[8,80,128]{2,1,0:T(8,128)(2,1)S(1)} %all_to_all.10), channel_id=1, source_target_pairs={{128,0},{129,1},{130,2},{131,3},{10,8},{11,9},{8,10},{9,11},{144,1... | collective-permute-start | bytes 491528 | tf_op jit(solution)/shard_map/ppermute | solution.py:49
  22.4 5.3 %collective-permute-start = (bf16[8,80,128]{2,1,0:T(8,128)(2,1)S(1)}, bf16[8,80,128]{2,1,0:T(8,128)(2,1)S(1)}, u32[]{:S(2)}, u32[]{:S(2)}) collective-permute-start(bf16[8,80,128]{2,1,0:T(8,128)(2,1)S(1)} %all_to_all.10), channel_id=1, source_target_pairs={{4,0},{5,1},{6,2},{7,3},{9,8},{10,9},{11,10},{8,11},{20,16},{21,17... | collective-permute-start | bytes 491528 | tf_op jit(solution)/shard_map/ppermute | solution.py:49
  27.8 12.0 %collective-permute-start.3 = (bf16[4,8,80,128]{3,2,1,0:T(8,128)(2,1)S(1)}, bf16[4,8,80,128]{3,2,1,0:T(8,128)(2,1)S(1)}, u32[]{:S(2)}, u32[]{:S(2)}) collective-permute-start(bf16[4,8,80,128]{3,2,1,0:T(8,128)(2,1)S(1)} %pad_maximum_fusion.rest_0_), channel_id=1, source_target_pairs={{3,0},{0,1},{1,2},{2,3},{140,8},{141,9},{142,10},{143,11},{19,16},... | collective-permute-start | bytes 1966088 | tf_op jit(solution)/shard_map/ppermute | solution.py:49
  29.5 18.5 %collective-permute-start.5 = (bf16[4,8,80,128]{3,2,1,0:T(8,128)(2,1)S(1)}, bf16[4,8,80,128]{3,2,1,0:T(8,128)(2,1)S(1)}, u32[]{:S(2)}, u32[]{:S(2)}) collective-permute-start(bf16[4,8,80,128]{3,2,1,0:T(8,128)(2,1)S(1)} %pad_maximum_fusion.rest_0_), channel_id=1, source_target_pairs={{2,0},{3,1},{0,2},{1,3},{136,8},{137,9},{138,10},{139,11},{18,16},... | collective-permute-start | bytes 1966088 | tf_op jit(solution)/shard_map/ppermute | solution.py:49
  32.4 15.6 %collective-permute-start.4 = (bf16[4,8,80,128]{3,2,1,0:T(8,128)(2,1)S(1)}, bf16[4,8,80,128]{3,2,1,0:T(8,128)(2,1)}, u32[]{:S(2)}, u32[]{:S(2)}) collective-permute-start(bf16[4,8,80,128]{3,2,1,0:T(8,128)(2,1)S(1)} %pad_maximum_fusion.rest_0_), channel_id=1, source_target_pairs={{1,0},{2,1},{3,2},{0,3},{12,8},{13,9},{14,10},{15,11},{17,16},{18,... | collective-permute-start | bytes 1966088 | tf_op jit(solution)/shard_map/ppermute | solution.py:49
  39.9 8.7 %collective-permute-start.6 = (bf16[4,8,80,128]{3,2,1,0:T(8,128)(2,1)S(1)}, bf16[4,8,80,128]{3,2,1,0:T(8,128)(2,1)}, u32[]{:S(2)}, u32[]{:S(2)}) collective-permute-start(bf16[4,8,80,128]{3,2,1,0:T(8,128)(2,1)S(1)} %pad_maximum_fusion.rest_0_), channel_id=1, source_target_pairs={{0,8},{8,0},{1,9},{9,1},{2,10},{10,2},{3,11},{11,3},{4,12},{12,4},... | collective-permute-start | bytes 1966088 | tf_op jit(solution)/shard_map/ppermute | solution.py:53
  48.0 3.1 %collective-permute-start.8 = (bf16[4,8,80,128]{3,2,1,0:T(8,128)(2,1)S(1)}, bf16[4,8,80,128]{3,2,1,0:T(8,128)(2,1)}, u32[]{:S(2)}, u32[]{:S(2)}) collective-permute-start(bf16[4,8,80,128]{3,2,1,0:T(8,128)(2,1)S(1)} %collective-permute-done.5.rest_2_), channel_id=1, source_target_pairs={{0,8},{8,0},{1,9},{9,1},{2,10},{10,2},{3,11},{11,3},{4,12},{12,4},... | collective-permute-start | bytes 1966088 | tf_op jit(solution)/shard_map/ppermute | solution.py:53
  48.0 3.9 %collective-permute-start.7 = (bf16[4,8,80,128]{3,2,1,0:T(8,128)(2,1)}, bf16[4,8,80,128]{3,2,1,0:T(8,128)(2,1)}, u32[]{:S(2)}, u32[]{:S(2)}) collective-permute-start(bf16[4,8,80,128]{3,2,1,0:T(8,128)(2,1)} %collective-permute-done.4.rest_1_), channel_id=1, source_target_pairs={{0,8},{8,0},{1,9},{9,1},{2,10},{10,2},{3,11},{11,3},{4,12},{12,4},... | collective-permute-start | bytes 1966088 | tf_op jit(solution)/shard_map/ppermute | solution.py:53
  48.5 3.6 %collective-permute-start.9 = (bf16[4,8,80,128]{3,2,1,0:T(8,128)(2,1)S(1)}, bf16[4,8,80,128]{3,2,1,0:T(8,128)(2,1)}, u32[]{:S(2)}, u32[]{:S(2)}) collective-permute-start(bf16[4,8,80,128]{3,2,1,0:T(8,128)(2,1)S(1)} %collective-permute-done.3.rest_3_), channel_id=1, source_target_pairs={{0,8},{8,0},{1,9},{9,1},{2,10},{10,2},{3,11},{11,3},{4,12},{12,4},... | collective-permute-start | bytes 1966088 | tf_op jit(solution)/shard_map/ppermute | solution.py:53
  70.7 2.2 %collective-permute-start.11 = (bf16[4,8,80,128]{3,2,1,0:T(8,128)(2,1)S(1)}, bf16[4,8,80,128]{3,2,1,0:T(8,128)(2,1)S(1)}, u32[]{:S(2)}, u32[]{:S(2)}) collective-permute-start(bf16[4,8,80,128]{3,2,1,0:T(8,128)(2,1)S(1)} %get-tuple-element.40), channel_id=1, source_target_pairs={{0,8},{8,0},{1,9},{9,1},{2,10},{10,2},{3,11},{11,3},{4,12},{12,4},... | collective-permute-start | bytes 1966088 | tf_op jit(solution)/shard_map/ppermute | solution.py:53
  71.0 3.1 %collective-permute-start.13 = (bf16[4,8,80,128]{3,2,1,0:T(8,128)(2,1)S(1)}, bf16[4,8,80,128]{3,2,1,0:T(8,128)(2,1)S(1)}, u32[]{:S(2)}, u32[]{:S(2)}) collective-permute-start(bf16[4,8,80,128]{3,2,1,0:T(8,128)(2,1)S(1)} %get-tuple-element.42), channel_id=1, source_target_pairs={{0,8},{8,0},{1,9},{9,1},{2,10},{10,2},{3,11},{11,3},{4,12},{12,4},... | collective-permute-start | bytes 1966088 | tf_op jit(solution)/shard_map/ppermute | solution.py:53
  71.3 5.2 %collective-permute-start.15 = (bf16[4,8,80,128]{3,2,1,0:T(8,128)(2,1)S(1)}, bf16[4,8,80,128]{3,2,1,0:T(8,128)(2,1)S(1)}, u32[]{:S(2)}, u32[]{:S(2)}) collective-permute-start(bf16[4,8,80,128]{3,2,1,0:T(8,128)(2,1)S(1)} %get-tuple-element.44), channel_id=1, source_target_pairs={{0,8},{8,0},{1,9},{9,1},{2,10},{10,2},{3,11},{11,3},{4,12},{12,4},... | collective-permute-start | bytes 1966088 | tf_op jit(solution)/shard_map/ppermute | solution.py:53
  71.5 16.6 %collective-permute-start.10 = (bf16[4,8,80,128]{3,2,1,0:T(8,128)(2,1)S(1)}, bf16[4,8,80,128]{3,2,1,0:T(8,128)(2,1)S(1)}, u32[]{:S(2)}, u32[]{:S(2)}) collective-permute-start(bf16[4,8,80,128]{3,2,1,0:T(8,128)(2,1)S(1)} %get-tuple-element.38), channel_id=1, source_target_pairs={{0,8},{8,0},{1,9},{9,1},{2,10},{10,2},{3,11},{11,3},{4,12},{12,4},... | collective-permute-start | bytes 1966088 | tf_op jit(solution)/shard_map/ppermute | solution.py:53
  73.1 18.9 %collective-permute-start.12 = (bf16[4,8,80,128]{3,2,1,0:T(8,128)(2,1)S(1)}, bf16[4,8,80,128]{3,2,1,0:T(8,128)(2,1)S(1)}, u32[]{:S(2)}, u32[]{:S(2)}) collective-permute-start(bf16[4,8,80,128]{3,2,1,0:T(8,128)(2,1)S(1)} %add_convert_fusion.3), channel_id=1, source_target_pairs={{3,0},{0,1},{1,2},{2,3},{140,8},{141,9},{142,10},{143,11},{19,16},... | collective-permute-start | bytes 1966088 | tf_op jit(solution)/shard_map/ppermute | solution.py:49
  74.3 4.4 %copy-start.2 = (bf16[512,1024]{1,0:T(8,128)(2,1)S(1)}, bf16[512,1024]{1,0:T(8,128)(2,1)}, u32[]{:S(2)}) copy-start(bf16[512,1024]{1,0:T(8,128)(2,1)} %cot.5) | copy-start | bytes 3145732
  74.3 17.6 %collective-permute-start.14 = (bf16[4,8,80,128]{3,2,1,0:T(8,128)(2,1)S(1)}, bf16[4,8,80,128]{3,2,1,0:T(8,128)(2,1)S(1)}, u32[]{:S(2)}, u32[]{:S(2)}) collective-permute-start(bf16[4,8,80,128]{3,2,1,0:T(8,128)(2,1)S(1)} %add_convert_fusion.2), channel_id=1, source_target_pairs={{2,0},{3,1},{0,2},{1,3},{136,8},{137,9},{138,10},{139,11},{18,16},... | collective-permute-start | bytes 1966088 | tf_op jit(solution)/shard_map/ppermute | solution.py:49
  76.7 16.4 %collective-permute-start.16 = (bf16[4,8,80,128]{3,2,1,0:T(8,128)(2,1)S(1)}, bf16[4,8,80,128]{3,2,1,0:T(8,128)(2,1)S(1)}, u32[]{:S(2)}, u32[]{:S(2)}) collective-permute-start(bf16[4,8,80,128]{3,2,1,0:T(8,128)(2,1)S(1)} %add_convert_fusion.1), channel_id=1, source_target_pairs={{1,0},{2,1},{3,2},{0,3},{12,8},{13,9},{14,10},{15,11},{17,16},{18,... | collective-permute-start | bytes 1966088 | tf_op jit(solution)/shard_map/ppermute | solution.py:49
  93.6 6.6 %collective-permute-start.17 = (bf16[8,80,128]{2,1,0:T(8,128)(2,1)S(1)}, bf16[8,80,128]{2,1,0:T(8,128)(2,1)S(1)}, u32[]{:S(2)}, u32[]{:S(2)}) collective-permute-start(bf16[8,80,128]{2,1,0:T(8,128)(2,1)S(1)} %get-tuple-element.56), channel_id=1, source_target_pairs={{132,0},{133,1},{134,2},{135,3},{11,8},{8,9},{9,10},{10,11},{148,1... | collective-permute-start | bytes 491528 | tf_op jit(solution)/shard_map/ppermute | solution.py:49
  95.3 5.3 %collective-permute-start.19 = (bf16[8,80,128]{2,1,0:T(8,128)(2,1)S(1)}, bf16[8,80,128]{2,1,0:T(8,128)(2,1)S(1)}, u32[]{:S(2)}, u32[]{:S(2)}) collective-permute-start(bf16[8,80,128]{2,1,0:T(8,128)(2,1)S(1)} %get-tuple-element.57), channel_id=1, source_target_pairs={{4,0},{5,1},{6,2},{7,3},{9,8},{10,9},{11,10},{8,11},{20,16},{21,17... | collective-permute-start | bytes 491528 | tf_op jit(solution)/shard_map/ppermute | solution.py:49
  96.9 6.8 %collective-permute-start.18 = (bf16[8,80,128]{2,1,0:T(8,128)(2,1)S(1)}, bf16[8,80,128]{2,1,0:T(8,128)(2,1)S(1)}, u32[]{:S(2)}, u32[]{:S(2)}) collective-permute-start(bf16[8,80,128]{2,1,0:T(8,128)(2,1)S(1)} %get-tuple-element.58), channel_id=1, source_target_pairs={{128,0},{129,1},{130,2},{131,3},{10,8},{11,9},{8,10},{9,11},{144,1... | collective-permute-start | bytes 491528 | tf_op jit(solution)/shard_map/ppermute | solution.py:49
  (5 other events, 5.1 us)
